TPU v7x, 32 devices: a whole 2x2x4 slice. The times are simulated.
32 devices in a mesh: grp: 2 (over x), lon: 16 (over z, y, core).
Axes of the slice: x: 2, y: 2, z: 4, core: 2. Of those that a mesh axis runs over, the one named last changes fastest.
Arguments:
- control: float32 [32, 512, 512], P('grp', 'lon'), parts along dimension 0, may hold values from -6 to 6
- std_field: float32 [16, 512, 512], P(None, 'lon'), may hold values from 0.5 to 2
- kappa_lon: float32 [512, 512], P('lon'), may hold values from 0.18 to 0.245
- kappa_lat: float32 [512, 512], P('lon'), may hold values from 0.18 to 0.245
- sea_mask: int32 [512, 512], P('lon'), may hold values 0 or 1
- vertical: float32 [16, 16], replicated, may hold values from -1.5 to 1.5
- block_index: int32 [32, 16, 8], P(('grp', 'lon')), parts along dimension 0, may hold values from 0 to 2047, as said below
- weights: float32 [32, 16, 8, 128], P(('grp', 'lon')), parts along dimension 0, may hold values from -1 to 1
- obs_value: float32 [32, 16, 8], P(('grp', 'lon')), parts along dimension 0, may hold values from -6 to 6
- obs_rinv: float32 [32, 16, 8], P(('grp', 'lon')), parts along dimension 0, may hold values from 0.5 to 4
- obs_count: int32 [32, 16], P(('grp', 'lon')), parts along dimension 0, may hold values from 0 to 8, as said below
Outputs:
- gradient: float32 [32, 512, 512], P('grp', 'lon'), parts along dimension 0
- departure: float32 [32, 16, 8], P(('grp', 'lon')), parts along dimension 0
There are 2 independent parts, one for each index of `grp`. A program takes and returns all parts, laid end to end along the dimension named above; an argument that names none is the same for every part. Nothing has to cross between parts.
Inputs may be any that keep to these rules, and one draw needn't show every extreme that they name: Slot c of owner p for tile t holds an observation exactly when c < obs_count[p, t]; in every draw one tile has 8 observations from every owner. `block_index`: each slot names one stencil block of its tile.
All inputs are finite; a program needn't handle non-finite values. No bound on the sum of `sea_mask` on one device may be relied on, other than what follows from the above.
Results may differ from a plain program's by a relative error of at most 0.000067.
Values sent between devices are 32-bit elements; how exact they have to be, the bound alone decides.
No kernel may reach another device: no remote copies, remote signals or barrier semaphores. Data moves between devices by JAX's collectives and lax.ppermute only.
A program may use at most 64 MiB of HBM per device.

v0:
```python
import jax
import jax.numpy as jnp
from jax import lax
from jax.sharding import PartitionSpec as P

STEN = 128
PASSES = 10


def with_halo(cells, sides, width):
    for axis, dim in sides:
        count = lax.axis_size(axis)
        head = lax.slice_in_dim(cells, 0, width, axis=dim)
        tail = lax.slice_in_dim(cells, cells.shape[dim] - width, cells.shape[dim], axis=dim)
        cells = jnp.concatenate(
            [
                lax.ppermute(tail, axis, [(i, (i + 1) % count) for i in range(count)]),
                cells,
                lax.ppermute(head, axis, [((i + 1) % count, i) for i in range(count)]),
            ],
            axis=dim,
        )
    return cells


def mix_levels(matrix, field):
    return jnp.einsum("ab,bxy->axy", matrix, field, precision=lax.Precision.HIGHEST)


def smooth_step(field, face_lon, face_lat):
    flux_lon = face_lon[None] * (field[:, 1:] - field[:, :-1])
    centre = field[:, 1:-1]
    flux_lat = face_lat[None] * (centre[:, :, 1:] - centre[:, :, :-1])
    padded = jnp.pad(flux_lat, ((0, 0), (0, 0), (1, 1)))
    return centre + (flux_lon[:, 1:] - flux_lon[:, :-1]) + (padded[:, :, 1:] - padded[:, :, :-1])


def local(
    control,
    std_field,
    kappa_lon,
    kappa_lat,
    sea_mask,
    vertical,
    block_index,
    weights,
    obs_value,
    obs_rinv,
    obs_count,
):
    depth = 1
    wet = sea_mask.astype(jnp.float32)
    stacked = jnp.stack([kappa_lon, kappa_lat, wet])
    widened = with_halo(stacked, (("lon", 1),), depth)
    lon_rate, lat_rate, wet_wide = (widened[0], widened[1], widened[2])
    face_lon = lon_rate[:-1] * wet_wide[:-1] * wet_wide[1:]
    face_lat = lat_rate[:, :-1] * wet_wide[:, :-1] * wet_wide[:, 1:]
    extent = face_lon.shape[0] + 1

    def diffuse(field):

        def one_group(turn, current):
            extended = with_halo(current, (("lon", 1),), depth)
            extended = smooth_step(extended, face_lon, face_lat[1 : extent - 1])
            return extended

        return lax.fori_loop(0, PASSES // depth, one_group, field)

    mixed = mix_levels(vertical, control)
    state = wet[None] * std_field * diffuse(mixed)
    blocks = state.reshape(-1, STEN)
    index_here = block_index[0]
    slots = index_here.shape[1]
    asked = lax.all_to_all(index_here, "lon", split_axis=0, concat_axis=0, tiled=True)
    picked = blocks[asked]
    values = lax.all_to_all(picked, "lon", split_axis=0, concat_axis=0, tiled=True)
    evolved = jnp.sum(values * weights[0], axis=-1)
    valid = jnp.arange(slots, dtype=jnp.int32)[None, :] < obs_count[0][:, None]
    departure = jnp.where(valid, evolved - obs_value[0], jnp.float32(0.0))
    scaled = obs_rinv[0] * departure
    spread = lax.all_to_all(
        scaled[..., None] * weights[0], "lon", split_axis=0, concat_axis=0, tiled=True
    )
    adjoint_blocks = jnp.zeros_like(blocks).at[asked.reshape(-1)].add(spread.reshape(-1, STEN))
    adjoint_state = adjoint_blocks.reshape(state.shape)
    weighted = wet[None] * std_field * adjoint_state
    gradient = control + mix_levels(vertical.T, diffuse(weighted))
    return (gradient, departure[None])


def solution(mesh):
    in_specs = (
        P("grp", "lon", None),
        P(None, "lon", None),
        P("lon", None),
        P("lon", None),
        P("lon", None),
        P(),
        P(("grp", "lon"), None, None),
        P(("grp", "lon"), None, None, None),
        P(("grp", "lon"), None, None),
        P(("grp", "lon"), None, None),
        P(("grp", "lon"), None),
    )
    out_specs = (P("grp", "lon", None), P(("grp", "lon"), None, None))
    return jax.shard_map(local, mesh=mesh, in_specs=in_specs, out_specs=out_specs, check_vma=False)
```

profile of v0, /device:TPU:0, one launch (start us, length us, event | category | flops | bytes accessed | tf_op | source)
XLA Modules:
  0.0 193.3 jit_solution(7009337845439063173)
XLA Ops:
  2.8 5.1 %collective-permute-start.5 = (f32[3,1,512]{2,1,0:T(1,128)S(1)}, f32[3,1,512]{2,1,0:T(1,128)S(1)}, u32[]{:S(2)}, u32[]{:S(2)}) collective-permute-start(f32[3,1,512]{2,1,0:T(1,128)S(1)} %get-tuple-element.151), channel_id=1, source_target_pairs={{1,0},{2,1},{3,2},{4,3},{5,4},{6,5},{7,6},{8,7},{9,8},{10,9},{11,1... | collective-permute-start | bytes 18440 | tf_op jit(solution)/shard_map/ppermute | solution.py:19
  9.2 3.6 %all-to-all-start = ((s32[16,1,8]{2,1,0:T(1,128)}), s32[16,1,8]{2,1,0:T(1,128)S(1)}, u32[]{:S(2)}, u32[]{:S(2)}) async-start(s32[16,1,8]{2,1,0:T(1,128)} %copy.31), calls=%async_computation | async-start | bytes 16384 | tf_op jit(solution)/shard_map/all_to_all | solution.py:74
  12.8 2.7 %fusion.10 = f32[16,32,512]{2,0,1:T(8,128)S(1)} fusion(f32[16,32,512]{2,1,0:T(8,128)} %param.15, f32[16,16]{1,0:T(8,128)S(1)} %copy-done), kind=kOutput, calls=%fused_computation.23 | convolution fusion | flops 50331648 | bytes 2098176 | tf_op jit(solution)/shard_map/ab,bxy->axy/dot_general | solution.py:27
  16.4 2.8 %all-to-all-done = s32[16,1,8]{2,1,0:T(1,128)S(1)} async-done(((s32[16,1,8]{2,1,0:T(1,128)}), s32[16,1,8]{2,1,0:T(1,128)S(1)}, u32[]{:S(2)}, u32[]{:S(2)}) %all-to-all-start) | async-done | bytes 544 | tf_op jit(solution)/shard_map/all_to_all | solution.py:74
  20.9 72.4 %while.24 = (s32[]{:T(128)}, f32[16,32,512]{2,1,0:T(8,128)S(1)}, f32[33,512]{1,0:T(8,128)S(1)}, f32[34,511]{1,0:T(8,128)S(1)}, s32[]{:T(128)}) while((s32[]{:T(128)}, f32[16,32,512]{2,1,0:T(8,128)S(1)}, f32[33,512]{1,0:T(8,128)S(1)}, f32[34,511]{1,0:T(8,128)S(1)}, s32[]{:T(128)}) %tuple.66), condition=%wide.region_1.2_spmd, body=%wide.region_0.1_spmd.sunk | while | flops 2653186 | bytes 11233037 | solution.py:67
  21.0 1.6 collective-permute-start
  24.2 4.4 %collective-permute-done.1 = f32[16,1,512]{2,1,0:T(1,128)S(1)} collective-permute-done((f32[16,1,512]{2,1,0:T(1,128)S(1)}, f32[16,1,512]{2,1,0:T(1,128)S(1)}, u32[]{:S(2)}, u32[]{:S(2)}) %collective-permute-start.1) | collective-permute-done | bytes 32800 | tf_op jit(solution)/shard_map/while/body/eval_jaxpr/ppermute | solution.py:17
  31.3 4.5 %collective-permute-done.1 = f32[16,1,512]{2,1,0:T(1,128)S(1)} collective-permute-done((f32[16,1,512]{2,1,0:T(1,128)S(1)}, f32[16,1,512]{2,1,0:T(1,128)S(1)}, u32[]{:S(2)}, u32[]{:S(2)}) %collective-permute-start.1) | collective-permute-done | bytes 32800 | tf_op jit(solution)/shard_map/while/body/eval_jaxpr/ppermute | solution.py:17
  38.3 4.5 %collective-permute-done.1 = f32[16,1,512]{2,1,0:T(1,128)S(1)} collective-permute-done((f32[16,1,512]{2,1,0:T(1,128)S(1)}, f32[16,1,512]{2,1,0:T(1,128)S(1)}, u32[]{:S(2)}, u32[]{:S(2)}) %collective-permute-start.1) | collective-permute-done | bytes 32800 | tf_op jit(solution)/shard_map/while/body/eval_jaxpr/ppermute | solution.py:17
  45.4 4.5 %collective-permute-done.1 = f32[16,1,512]{2,1,0:T(1,128)S(1)} collective-permute-done((f32[16,1,512]{2,1,0:T(1,128)S(1)}, f32[16,1,512]{2,1,0:T(1,128)S(1)}, u32[]{:S(2)}, u32[]{:S(2)}) %collective-permute-start.1) | collective-permute-done | bytes 32800 | tf_op jit(solution)/shard_map/while/body/eval_jaxpr/ppermute | solution.py:17
  52.5 4.5 %collective-permute-done.1 = f32[16,1,512]{2,1,0:T(1,128)S(1)} collective-permute-done((f32[16,1,512]{2,1,0:T(1,128)S(1)}, f32[16,1,512]{2,1,0:T(1,128)S(1)}, u32[]{:S(2)}, u32[]{:S(2)}) %collective-permute-start.1) | collective-permute-done | bytes 32800 | tf_op jit(solution)/shard_map/while/body/eval_jaxpr/ppermute | solution.py:17
  59.6 4.5 %collective-permute-done.1 = f32[16,1,512]{2,1,0:T(1,128)S(1)} collective-permute-done((f32[16,1,512]{2,1,0:T(1,128)S(1)}, f32[16,1,512]{2,1,0:T(1,128)S(1)}, u32[]{:S(2)}, u32[]{:S(2)}) %collective-permute-start.1) | collective-permute-done | bytes 32800 | tf_op jit(solution)/shard_map/while/body/eval_jaxpr/ppermute | solution.py:17
  66.7 4.5 %collective-permute-done.1 = f32[16,1,512]{2,1,0:T(1,128)S(1)} collective-permute-done((f32[16,1,512]{2,1,0:T(1,128)S(1)}, f32[16,1,512]{2,1,0:T(1,128)S(1)}, u32[]{:S(2)}, u32[]{:S(2)}) %collective-permute-start.1) | collective-permute-done | bytes 32800 | tf_op jit(solution)/shard_map/while/body/eval_jaxpr/ppermute | solution.py:17
  73.8 4.5 %collective-permute-done.1 = f32[16,1,512]{2,1,0:T(1,128)S(1)} collective-permute-done((f32[16,1,512]{2,1,0:T(1,128)S(1)}, f32[16,1,512]{2,1,0:T(1,128)S(1)}, u32[]{:S(2)}, u32[]{:S(2)}) %collective-permute-start.1) | collective-permute-done | bytes 32800 | tf_op jit(solution)/shard_map/while/body/eval_jaxpr/ppermute | solution.py:17
  80.9 4.5 %collective-permute-done.1 = f32[16,1,512]{2,1,0:T(1,128)S(1)} collective-permute-done((f32[16,1,512]{2,1,0:T(1,128)S(1)}, f32[16,1,512]{2,1,0:T(1,128)S(1)}, u32[]{:S(2)}, u32[]{:S(2)}) %collective-permute-start.1) | collective-permute-done | bytes 32800 | tf_op jit(solution)/shard_map/while/body/eval_jaxpr/ppermute | solution.py:17
  88.0 4.5 %collective-permute-done.1 = f32[16,1,512]{2,1,0:T(1,128)S(1)} collective-permute-done((f32[16,1,512]{2,1,0:T(1,128)S(1)}, f32[16,1,512]{2,1,0:T(1,128)S(1)}, u32[]{:S(2)}, u32[]{:S(2)}) %collective-permute-start.1) | collective-permute-done | bytes 32800 | tf_op jit(solution)/shard_map/while/body/eval_jaxpr/ppermute | solution.py:17
  95.0 3.5 %all-to-all-start.1 = ((f32[16,8,128]{2,1,0:T(8,128)}), f32[16,8,128]{2,1,0:T(8,128)S(1)}, u32[]{:S(2)}, u32[]{:S(2)}) async-start(f32[16,8,128]{2,1,0:T(8,128)} %bitcast.12), calls=%async_computation.1 | async-start | bytes 131072 | tf_op jit(solution)/shard_map/all_to_all | solution.py:76
  98.5 6.8 %all-to-all-done.1 = f32[16,8,128]{2,1,0:T(8,128)S(1)} async-done(((f32[16,8,128]{2,1,0:T(8,128)}), f32[16,8,128]{2,1,0:T(8,128)S(1)}, u32[]{:S(2)}, u32[]{:S(2)}) %all-to-all-start.1) | async-done | bytes 65568 | tf_op jit(solution)/shard_map/all_to_all | solution.py:76
  106.3 3.5 %all-to-all-start.2 = ((f32[16,8,128]{2,1,0:T(8,128)}), f32[16,8,128]{2,1,0:T(8,128)S(1)}, u32[]{:S(2)}, u32[]{:S(2)}) async-start(f32[16,8,128]{2,1,0:T(8,128)} %bitcast_multiply_fusion), calls=%async_computation.2 | async-start | bytes 131072 | tf_op jit(solution)/shard_map/all_to_all | solution.py:81
  110.4 6.3 %all-to-all-done.2 = f32[16,8,128]{2,1,0:T(8,128)S(1)} async-done(((f32[16,8,128]{2,1,0:T(8,128)}), f32[16,8,128]{2,1,0:T(8,128)S(1)}, u32[]{:S(2)}, u32[]{:S(2)}) %all-to-all-start.2) | async-done | bytes 65568 | tf_op jit(solution)/shard_map/all_to_all | solution.py:81
  118.4 71.1 %while.25 = (s32[]{:T(128)}, f32[16,32,512]{2,1,0:T(8,128)S(1)}, f32[33,512]{1,0:T(8,128)S(1)}, f32[34,511]{1,0:T(8,128)S(1)}, s32[]{:T(128)}) while((s32[]{:T(128)}, f32[16,32,512]{2,1,0:T(8,128)S(1)}, f32[33,512]{1,0:T(8,128)S(1)}, f32[34,511]{1,0:T(8,128)S(1)}, s32[]{:T(128)}) %tuple.73), condition=%wide.region_5.6_spmd, body=%wide.region_4.5_spmd.sunk | while | flops 2653186 | bytes 11233037 | solution.py:67
  120.4 4.4 %collective-permute-done.3 = f32[16,1,512]{2,1,0:T(1,128)S(1)} collective-permute-done((f32[16,1,512]{2,1,0:T(1,128)S(1)}, f32[16,1,512]{2,1,0:T(1,128)S(1)}, u32[]{:S(2)}, u32[]{:S(2)}) %collective-permute-start.3) | collective-permute-done | bytes 32800 | tf_op jit(solution)/shard_map/while/body/eval_jaxpr/ppermute | solution.py:17
  127.4 4.5 %collective-permute-done.3 = f32[16,1,512]{2,1,0:T(1,128)S(1)} collective-permute-done((f32[16,1,512]{2,1,0:T(1,128)S(1)}, f32[16,1,512]{2,1,0:T(1,128)S(1)}, u32[]{:S(2)}, u32[]{:S(2)}) %collective-permute-start.3) | collective-permute-done | bytes 32800 | tf_op jit(solution)/shard_map/while/body/eval_jaxpr/ppermute | solution.py:17
  134.5 4.5 %collective-permute-done.3 = f32[16,1,512]{2,1,0:T(1,128)S(1)} collective-permute-done((f32[16,1,512]{2,1,0:T(1,128)S(1)}, f32[16,1,512]{2,1,0:T(1,128)S(1)}, u32[]{:S(2)}, u32[]{:S(2)}) %collective-permute-start.3) | collective-permute-done | bytes 32800 | tf_op jit(solution)/shard_map/while/body/eval_jaxpr/ppermute | solution.py:17
  141.6 4.5 %collective-permute-done.3 = f32[16,1,512]{2,1,0:T(1,128)S(1)} collective-permute-done((f32[16,1,512]{2,1,0:T(1,128)S(1)}, f32[16,1,512]{2,1,0:T(1,128)S(1)}, u32[]{:S(2)}, u32[]{:S(2)}) %collective-permute-start.3) | collective-permute-done | bytes 32800 | tf_op jit(solution)/shard_map/while/body/eval_jaxpr/ppermute | solution.py:17
  148.7 4.5 %collective-permute-done.3 = f32[16,1,512]{2,1,0:T(1,128)S(1)} collective-permute-done((f32[16,1,512]{2,1,0:T(1,128)S(1)}, f32[16,1,512]{2,1,0:T(1,128)S(1)}, u32[]{:S(2)}, u32[]{:S(2)}) %collective-permute-start.3) | collective-permute-done | bytes 32800 | tf_op jit(solution)/shard_map/while/body/eval_jaxpr/ppermute | solution.py:17
  155.8 4.5 %collective-permute-done.3 = f32[16,1,512]{2,1,0:T(1,128)S(1)} collective-permute-done((f32[16,1,512]{2,1,0:T(1,128)S(1)}, f32[16,1,512]{2,1,0:T(1,128)S(1)}, u32[]{:S(2)}, u32[]{:S(2)}) %collective-permute-start.3) | collective-permute-done | bytes 32800 | tf_op jit(solution)/shard_map/while/body/eval_jaxpr/ppermute | solution.py:17
  162.9 4.5 %collective-permute-done.3 = f32[16,1,512]{2,1,0:T(1,128)S(1)} collective-permute-done((f32[16,1,512]{2,1,0:T(1,128)S(1)}, f32[16,1,512]{2,1,0:T(1,128)S(1)}, u32[]{:S(2)}, u32[]{:S(2)}) %collective-permute-start.3) | collective-permute-done | bytes 32800 | tf_op jit(solution)/shard_map/while/body/eval_jaxpr/ppermute | solution.py:17
  170.0 4.5 %collective-permute-done.3 = f32[16,1,512]{2,1,0:T(1,128)S(1)} collective-permute-done((f32[16,1,512]{2,1,0:T(1,128)S(1)}, f32[16,1,512]{2,1,0:T(1,128)S(1)}, u32[]{:S(2)}, u32[]{:S(2)}) %collective-permute-start.3) | collective-permute-done | bytes 32800 | tf_op jit(solution)/shard_map/while/body/eval_jaxpr/ppermute | solution.py:17
  177.1 4.5 %collective-permute-done.3 = f32[16,1,512]{2,1,0:T(1,128)S(1)} collective-permute-done((f32[16,1,512]{2,1,0:T(1,128)S(1)}, f32[16,1,512]{2,1,0:T(1,128)S(1)}, u32[]{:S(2)}, u32[]{:S(2)}) %collective-permute-start.3) | collective-permute-done | bytes 32800 | tf_op jit(solution)/shard_map/while/body/eval_jaxpr/ppermute | solution.py:17
  184.2 4.5 %collective-permute-done.3 = f32[16,1,512]{2,1,0:T(1,128)S(1)} collective-permute-done((f32[16,1,512]{2,1,0:T(1,128)S(1)}, f32[16,1,512]{2,1,0:T(1,128)S(1)}, u32[]{:S(2)}, u32[]{:S(2)}) %collective-permute-start.3) | collective-permute-done | bytes 32800 | tf_op jit(solution)/shard_map/while/body/eval_jaxpr/ppermute | solution.py:17
  189.5 2.2 %fusion.8 = f32[16,32,512]{2,0,1:T(8,128)S(1)} fusion(f32[16,32,512]{2,1,0:T(8,128)S(1)} %get-tuple-element.109, f32[16,32,512]{2,1,0:T(8,128)S(1)} %copy-done.2, f32[16,16]{1,0:T(8,128)S(1)} %copy-done), kind=kOutput, calls=%fused_computation.21 | convolution fusion | flops 50593792 | bytes 3146752 | tf_op jit(solution)/shard_map/ab,bxy->axy/dot_general | solution.py:27
  (210 shorter events, 63.4 us)
Async XLA Ops:
  2.3 18.4 %collective-permute-start.4 = (f32[3,1,512]{2,1,0:T(1,128)S(1)}, f32[3,1,512]{2,1,0:T(1,128)S(1)}, u32[]{:S(2)}, u32[]{:S(2)}) collective-permute-start(f32[3,1,512]{2,1,0:T(1,128)S(1)} %get-tuple-element.150), channel_id=1, source_target_pairs={{0,1},{1,2},{2,3},{3,4},{4,5},{5,6},{6,7},{7,8},{8,9},{9,10},{10,1... | collective-permute-start | bytes 18440 | tf_op jit(solution)/shard_map/ppermute | solution.py:17
  2.8 17.9 %collective-permute-start.5 = (f32[3,1,512]{2,1,0:T(1,128)S(1)}, f32[3,1,512]{2,1,0:T(1,128)S(1)}, u32[]{:S(2)}, u32[]{:S(2)}) collective-permute-start(f32[3,1,512]{2,1,0:T(1,128)S(1)} %get-tuple-element.151), channel_id=1, source_target_pairs={{1,0},{2,1},{3,2},{4,3},{5,4},{6,5},{7,6},{8,7},{9,8},{10,9},{11,1... | collective-permute-start | bytes 18440 | tf_op jit(solution)/shard_map/ppermute | solution.py:19
  9.2 10.0 %all-to-all-start = ((s32[16,1,8]{2,1,0:T(1,128)}), s32[16,1,8]{2,1,0:T(1,128)S(1)}, u32[]{:S(2)}, u32[]{:S(2)}) async-start(s32[16,1,8]{2,1,0:T(1,128)} %copy.31), calls=%async_computation | async-start | bytes 16384 | tf_op jit(solution)/shard_map/all_to_all | solution.py:74
  21.0 3.2 %collective-permute-start = (f32[16,1,512]{2,1,0:T(1,128)S(1)}, f32[16,1,512]{2,1,0:T(1,128)S(1)}, u32[]{:S(2)}, u32[]{:S(2)}) collective-permute-start(f32[16,1,512]{2,1,0:T(1,128)S(1)} %get-tuple-element.204), channel_id=1, source_target_pairs={{1,0},{2,1},{3,2},{4,3},{5,4},{6,5},{7,6},{8,7},{9,8},{10,9},{11,1... | collective-permute-start | bytes 98312 | tf_op jit(solution)/shard_map/while/body/eval_jaxpr/ppermute | solution.py:19
  22.6 6.0 %collective-permute-start.1 = (f32[16,1,512]{2,1,0:T(1,128)S(1)}, f32[16,1,512]{2,1,0:T(1,128)S(1)}, u32[]{:S(2)}, u32[]{:S(2)}) collective-permute-start(f32[16,1,512]{2,1,0:T(1,128)S(1)} %get-tuple-element.205), channel_id=1, source_target_pairs={{0,1},{1,2},{2,3},{3,4},{4,5},{5,6},{6,7},{7,8},{8,9},{9,10},{10,1... | collective-permute-start | bytes 98312 | tf_op jit(solution)/shard_map/while/body/eval_jaxpr/ppermute | solution.py:17
  29.7 6.1 %collective-permute-start.1 = (f32[16,1,512]{2,1,0:T(1,128)S(1)}, f32[16,1,512]{2,1,0:T(1,128)S(1)}, u32[]{:S(2)}, u32[]{:S(2)}) collective-permute-start(f32[16,1,512]{2,1,0:T(1,128)S(1)} %get-tuple-element.205), channel_id=1, source_target_pairs={{0,1},{1,2},{2,3},{3,4},{4,5},{5,6},{6,7},{7,8},{8,9},{9,10},{10,1... | collective-permute-start | bytes 98312 | tf_op jit(solution)/shard_map/while/body/eval_jaxpr/ppermute | solution.py:17
  36.7 1.7 collective-permute-start
  36.8 6.1 %collective-permute-start.1 = (f32[16,1,512]{2,1,0:T(1,128)S(1)}, f32[16,1,512]{2,1,0:T(1,128)S(1)}, u32[]{:S(2)}, u32[]{:S(2)}) collective-permute-start(f32[16,1,512]{2,1,0:T(1,128)S(1)} %get-tuple-element.205), channel_id=1, source_target_pairs={{0,1},{1,2},{2,3},{3,4},{4,5},{5,6},{6,7},{7,8},{8,9},{9,10},{10,1... | collective-permute-start | bytes 98312 | tf_op jit(solution)/shard_map/while/body/eval_jaxpr/ppermute | solution.py:17
  43.8 1.7 collective-permute-start
  43.8 6.1 %collective-permute-start.1 = (f32[16,1,512]{2,1,0:T(1,128)S(1)}, f32[16,1,512]{2,1,0:T(1,128)S(1)}, u32[]{:S(2)}, u32[]{:S(2)}) collective-permute-start(f32[16,1,512]{2,1,0:T(1,128)S(1)} %get-tuple-element.205), channel_id=1, source_target_pairs={{0,1},{1,2},{2,3},{3,4},{4,5},{5,6},{6,7},{7,8},{8,9},{9,10},{10,1... | collective-permute-start | bytes 98312 | tf_op jit(solution)/shard_map/while/body/eval_jaxpr/ppermute | solution.py:17
  50.9 1.7 collective-permute-start
  50.9 6.1 %collective-permute-start.1 = (f32[16,1,512]{2,1,0:T(1,128)S(1)}, f32[16,1,512]{2,1,0:T(1,128)S(1)}, u32[]{:S(2)}, u32[]{:S(2)}) collective-permute-start(f32[16,1,512]{2,1,0:T(1,128)S(1)} %get-tuple-element.205), channel_id=1, source_target_pairs={{0,1},{1,2},{2,3},{3,4},{4,5},{5,6},{6,7},{7,8},{8,9},{9,10},{10,1... | collective-permute-start | bytes 98312 | tf_op jit(solution)/shard_map/while/body/eval_jaxpr/ppermute | solution.py:17
  58.0 1.7 collective-permute-start
  58.0 6.1 %collective-permute-start.1 = (f32[16,1,512]{2,1,0:T(1,128)S(1)}, f32[16,1,512]{2,1,0:T(1,128)S(1)}, u32[]{:S(2)}, u32[]{:S(2)}) collective-permute-start(f32[16,1,512]{2,1,0:T(1,128)S(1)} %get-tuple-element.205), channel_id=1, source_target_pairs={{0,1},{1,2},{2,3},{3,4},{4,5},{5,6},{6,7},{7,8},{8,9},{9,10},{10,1... | collective-permute-start | bytes 98312 | tf_op jit(solution)/shard_map/while/body/eval_jaxpr/ppermute | solution.py:17
  65.0 1.7 collective-permute-start
  65.1 6.1 %collective-permute-start.1 = (f32[16,1,512]{2,1,0:T(1,128)S(1)}, f32[16,1,512]{2,1,0:T(1,128)S(1)}, u32[]{:S(2)}, u32[]{:S(2)}) collective-permute-start(f32[16,1,512]{2,1,0:T(1,128)S(1)} %get-tuple-element.205), channel_id=1, source_target_pairs={{0,1},{1,2},{2,3},{3,4},{4,5},{5,6},{6,7},{7,8},{8,9},{9,10},{10,1... | collective-permute-start | bytes 98312 | tf_op jit(solution)/shard_map/while/body/eval_jaxpr/ppermute | solution.py:17
  72.2 6.1 %collective-permute-start.1 = (f32[16,1,512]{2,1,0:T(1,128)S(1)}, f32[16,1,512]{2,1,0:T(1,128)S(1)}, u32[]{:S(2)}, u32[]{:S(2)}) collective-permute-start(f32[16,1,512]{2,1,0:T(1,128)S(1)} %get-tuple-element.205), channel_id=1, source_target_pairs={{0,1},{1,2},{2,3},{3,4},{4,5},{5,6},{6,7},{7,8},{8,9},{9,10},{10,1... | collective-permute-start | bytes 98312 | tf_op jit(solution)/shard_map/while/body/eval_jaxpr/ppermute | solution.py:17
  79.3 6.1 %collective-permute-start.1 = (f32[16,1,512]{2,1,0:T(1,128)S(1)}, f32[16,1,512]{2,1,0:T(1,128)S(1)}, u32[]{:S(2)}, u32[]{:S(2)}) collective-permute-start(f32[16,1,512]{2,1,0:T(1,128)S(1)} %get-tuple-element.205), channel_id=1, source_target_pairs={{0,1},{1,2},{2,3},{3,4},{4,5},{5,6},{6,7},{7,8},{8,9},{9,10},{10,1... | collective-permute-start | bytes 98312 | tf_op jit(solution)/shard_map/while/body/eval_jaxpr/ppermute | solution.py:17
  86.4 6.1 %collective-permute-start.1 = (f32[16,1,512]{2,1,0:T(1,128)S(1)}, f32[16,1,512]{2,1,0:T(1,128)S(1)}, u32[]{:S(2)}, u32[]{:S(2)}) collective-permute-start(f32[16,1,512]{2,1,0:T(1,128)S(1)} %get-tuple-element.205), channel_id=1, source_target_pairs={{0,1},{1,2},{2,3},{3,4},{4,5},{5,6},{6,7},{7,8},{8,9},{9,10},{10,1... | collective-permute-start | bytes 98312 | tf_op jit(solution)/shard_map/while/body/eval_jaxpr/ppermute | solution.py:17
  95.0 10.4 %all-to-all-start.1 = ((f32[16,8,128]{2,1,0:T(8,128)}), f32[16,8,128]{2,1,0:T(8,128)S(1)}, u32[]{:S(2)}, u32[]{:S(2)}) async-start(f32[16,8,128]{2,1,0:T(8,128)} %bitcast.12), calls=%async_computation.1 | async-start | bytes 131072 | tf_op jit(solution)/shard_map/all_to_all | solution.py:76
  106.3 10.4 %all-to-all-start.2 = ((f32[16,8,128]{2,1,0:T(8,128)}), f32[16,8,128]{2,1,0:T(8,128)S(1)}, u32[]{:S(2)}, u32[]{:S(2)}) async-start(f32[16,8,128]{2,1,0:T(8,128)} %bitcast_multiply_fusion), calls=%async_computation.2 | async-start | bytes 131072 | tf_op jit(solution)/shard_map/all_to_all | solution.py:81
  118.4 2.0 %collective-permute-start.2 = (f32[16,1,512]{2,1,0:T(1,128)S(1)}, f32[16,1,512]{2,1,0:T(1,128)S(1)}, u32[]{:S(2)}, u32[]{:S(2)}) collective-permute-start(f32[16,1,512]{2,1,0:T(1,128)S(1)} %get-tuple-element.210), channel_id=1, source_target_pairs={{1,0},{2,1},{3,2},{4,3},{5,4},{6,5},{7,6},{8,7},{9,8},{10,9},{11,1... | collective-permute-start | bytes 98312 | tf_op jit(solution)/shard_map/while/body/eval_jaxpr/ppermute | solution.py:19
  118.8 6.0 %collective-permute-start.3 = (f32[16,1,512]{2,1,0:T(1,128)S(1)}, f32[16,1,512]{2,1,0:T(1,128)S(1)}, u32[]{:S(2)}, u32[]{:S(2)}) collective-permute-start(f32[16,1,512]{2,1,0:T(1,128)S(1)} %get-tuple-element.211), channel_id=1, source_target_pairs={{0,1},{1,2},{2,3},{3,4},{4,5},{5,6},{6,7},{7,8},{8,9},{9,10},{10,1... | collective-permute-start | bytes 98312 | tf_op jit(solution)/shard_map/while/body/eval_jaxpr/ppermute | solution.py:17
  125.8 6.1 %collective-permute-start.3 = (f32[16,1,512]{2,1,0:T(1,128)S(1)}, f32[16,1,512]{2,1,0:T(1,128)S(1)}, u32[]{:S(2)}, u32[]{:S(2)}) collective-permute-start(f32[16,1,512]{2,1,0:T(1,128)S(1)} %get-tuple-element.211), channel_id=1, source_target_pairs={{0,1},{1,2},{2,3},{3,4},{4,5},{5,6},{6,7},{7,8},{8,9},{9,10},{10,1... | collective-permute-start | bytes 98312 | tf_op jit(solution)/shard_map/while/body/eval_jaxpr/ppermute | solution.py:17
  132.9 6.1 %collective-permute-start.3 = (f32[16,1,512]{2,1,0:T(1,128)S(1)}, f32[16,1,512]{2,1,0:T(1,128)S(1)}, u32[]{:S(2)}, u32[]{:S(2)}) collective-permute-start(f32[16,1,512]{2,1,0:T(1,128)S(1)} %get-tuple-element.211), channel_id=1, source_target_pairs={{0,1},{1,2},{2,3},{3,4},{4,5},{5,6},{6,7},{7,8},{8,9},{9,10},{10,1... | collective-permute-start | bytes 98312 | tf_op jit(solution)/shard_map/while/body/eval_jaxpr/ppermute | solution.py:17
  140.0 6.1 %collective-permute-start.3 = (f32[16,1,512]{2,1,0:T(1,128)S(1)}, f32[16,1,512]{2,1,0:T(1,128)S(1)}, u32[]{:S(2)}, u32[]{:S(2)}) collective-permute-start(f32[16,1,512]{2,1,0:T(1,128)S(1)} %get-tuple-element.211), channel_id=1, source_target_pairs={{0,1},{1,2},{2,3},{3,4},{4,5},{5,6},{6,7},{7,8},{8,9},{9,10},{10,1... | collective-permute-start | bytes 98312 | tf_op jit(solution)/shard_map/while/body/eval_jaxpr/ppermute | solution.py:17
  147.1 6.1 %collective-permute-start.3 = (f32[16,1,512]{2,1,0:T(1,128)S(1)}, f32[16,1,512]{2,1,0:T(1,128)S(1)}, u32[]{:S(2)}, u32[]{:S(2)}) collective-permute-start(f32[16,1,512]{2,1,0:T(1,128)S(1)} %get-tuple-element.211), channel_id=1, source_target_pairs={{0,1},{1,2},{2,3},{3,4},{4,5},{5,6},{6,7},{7,8},{8,9},{9,10},{10,1... | collective-permute-start | bytes 98312 | tf_op jit(solution)/shard_map/while/body/eval_jaxpr/ppermute | solution.py:17
  154.2 6.1 %collective-permute-start.3 = (f32[16,1,512]{2,1,0:T(1,128)S(1)}, f32[16,1,512]{2,1,0:T(1,128)S(1)}, u32[]{:S(2)}, u32[]{:S(2)}) collective-permute-start(f32[16,1,512]{2,1,0:T(1,128)S(1)} %get-tuple-element.211), channel_id=1, source_target_pairs={{0,1},{1,2},{2,3},{3,4},{4,5},{5,6},{6,7},{7,8},{8,9},{9,10},{10,1... | collective-permute-start | bytes 98312 | tf_op jit(solution)/shard_map/while/body/eval_jaxpr/ppermute | solution.py:17
  161.3 6.1 %collective-permute-start.3 = (f32[16,1,512]{2,1,0:T(1,128)S(1)}, f32[16,1,512]{2,1,0:T(1,128)S(1)}, u32[]{:S(2)}, u32[]{:S(2)}) collective-permute-start(f32[16,1,512]{2,1,0:T(1,128)S(1)} %get-tuple-element.211), channel_id=1, source_target_pairs={{0,1},{1,2},{2,3},{3,4},{4,5},{5,6},{6,7},{7,8},{8,9},{9,10},{10,1... | collective-permute-start | bytes 98312 | tf_op jit(solution)/shard_map/while/body/eval_jaxpr/ppermute | solution.py:17
  168.4 6.1 %collective-permute-start.3 = (f32[16,1,512]{2,1,0:T(1,128)S(1)}, f32[16,1,512]{2,1,0:T(1,128)S(1)}, u32[]{:S(2)}, u32[]{:S(2)}) collective-permute-start(f32[16,1,512]{2,1,0:T(1,128)S(1)} %get-tuple-element.211), channel_id=1, source_target_pairs={{0,1},{1,2},{2,3},{3,4},{4,5},{5,6},{6,7},{7,8},{8,9},{9,10},{10,1... | collective-permute-start | bytes 98312 | tf_op jit(solution)/shard_map/while/body/eval_jaxpr/ppermute | solution.py:17
  175.5 6.1 %collective-permute-start.3 = (f32[16,1,512]{2,1,0:T(1,128)S(1)}, f32[16,1,512]{2,1,0:T(1,128)S(1)}, u32[]{:S(2)}, u32[]{:S(2)}) collective-permute-start(f32[16,1,512]{2,1,0:T(1,128)S(1)} %get-tuple-element.211), channel_id=1, source_target_pairs={{0,1},{1,2},{2,3},{3,4},{4,5},{5,6},{6,7},{7,8},{8,9},{9,10},{10,1... | collective-permute-start | bytes 98312 | tf_op jit(solution)/shard_map/while/body/eval_jaxpr/ppermute | solution.py:17
  182.6 6.1 %collective-permute-start.3 = (f32[16,1,512]{2,1,0:T(1,128)S(1)}, f32[16,1,512]{2,1,0:T(1,128)S(1)}, u32[]{:S(2)}, u32[]{:S(2)}) collective-permute-start(f32[16,1,512]{2,1,0:T(1,128)S(1)} %get-tuple-element.211), channel_id=1, source_target_pairs={{0,1},{1,2},{2,3},{3,4},{4,5},{5,6},{6,7},{7,8},{8,9},{9,10},{10,1... | collective-permute-start | bytes 98312 | tf_op jit(solution)/shard_map/while/body/eval_jaxpr/ppermute | solution.py:17
  (22 other events, 212.7 us)
where the time goes:
time: 194 us; the launch traced here: 193 us
  waiting for transfers between devices  121 us (62%)
  other arithmetic  29.4 us (15%)
  starting transfers between devices  28.4 us (15%)
  local copies, waits for them, and re-layouts  7.33 us (4%)
  matrix products  4.85 us (2%)
    ppermute x21, waiting for transfers between devices, with_halo(): lax.ppermute(tail, axis, [(i, (i + 1) % count) for i in range(count)])  89.8 us
    ppermute x21, waiting for transfers between devices, with_halo(): lax.ppermute(head, axis, [((i + 1) % count, i) for i in range(count)])  15.5 us
    add x20, other arithmetic, smooth_step(): centre + (flux_lon[:, 1:] - flux_lon[:, :-1])  12.8 us
    ppermute x21, starting transfers between devices, with_halo(): lax.ppermute(tail, axis, [(i, (i + 1) % count) for i in range(count)])  9.65 us
    ppermute x21, starting transfers between devices, with_halo(): lax.ppermute(head, axis, [((i + 1) % count, i) for i in range(count)])  8.11 us
    all_to_all x1, waiting for transfers between devices, local(): lax.all_to_all(picked, 'lon', split_axis=0, concat_axis=0, tiled=True)  6.85 us
    mul x20, other arithmetic, smooth_step(): flux_lat = face_lat[None] * (centre[:, :, 1:] - centre[:, :, :-1])  6.82 us
    all_to_all x1, waiting for transfers between devices, local(): lax.all_to_all(scaled[..., None] * weights[0], 'lon', split_axis=0, conca...  6.26 us
  transfers between devices with their start and end apart: 45, of which 43 were waited for; matrix products, arithmetic and copies ran while one was open for 7% of the time, Pallas kernels for 0%

commit v1 on v0

v1 whole, which is shorter than its diff:
```python
import jax
import jax.numpy as jnp
from jax import lax
from jax.experimental import pallas as pl
from jax.experimental.pallas import tpu as pltpu
from jax.sharding import PartitionSpec as P

STEN = 128
PASSES = 10
WIDE = 256
F32 = jnp.float32
BF16 = jnp.bfloat16
VMEM_LIMIT = 40 * 1024 * 1024

VMEM_SPEC = pl.BlockSpec(memory_space=pltpu.VMEM)
SMEM_SPEC = pl.BlockSpec(memory_space=pltpu.SMEM)


def split(x):
    high = x.astype(BF16)
    return high, (x - high.astype(F32)).astype(BF16)


def dot(a, b):
    return jnp.dot(a, b, preferred_element_type=F32)


def iota(shape, dim):
    return lax.broadcasted_iota(jnp.int32, shape, dim)


def onehot(condition):
    return jnp.where(condition, F32(1.0), F32(0.0)).astype(BF16)


def product(left, right):
    (lh, ll), (rh, rl) = left, right
    return dot(lh, rh) + (dot(lh, rl) + dot(ll, rh))


def mixing_matrix(vertical):
    levels = vertical.shape[0]
    group = WIDE // levels
    expand = onehot(iota((levels, WIDE), 1) // group == iota((levels, WIDE), 0))
    keep = iota((WIDE, WIDE), 0) // levels == iota((WIDE, WIDE), 1) % group
    out = []
    for part in split(vertical):
        rows = dot(part, expand)
        tiled = jnp.concatenate([rows] * group, axis=0)
        out.append(jnp.where(keep, tiled, F32(0.0)).astype(BF16))
    return tuple(out)


def mixing_matrix_back(vertical_t):
    levels = vertical_t.shape[0]
    group = WIDE // levels
    spread = onehot(iota((levels, WIDE), 1) % levels == iota((levels, WIDE), 0))
    repeat = onehot(iota((WIDE, levels), 0) // group == iota((WIDE, levels), 1))
    keep = iota((WIDE, WIDE), 0) % group == iota((WIDE, WIDE), 1) // levels
    out = []
    for part in split(vertical_t):
        rows = dot(part, spread).astype(BF16)
        out.append(jnp.where(keep, dot(repeat, rows), F32(0.0)).astype(BF16))
    return tuple(out)


def head_kernel(v_ref, control_ref, klon_ref, klat_ref, mask_ref, mixed_ref, faces_ref, left_ref, right_ref):
    levels, cols, lat = control_ref.shape
    group = WIDE // levels
    wet = mask_ref[...].astype(F32)
    east = jnp.where(iota((cols, lat), 0) == cols - 1, F32(1.0), pltpu.roll(wet, cols - 1, 0))
    north = jnp.where(iota((cols, lat), 1) == lat - 1, F32(0.0), pltpu.roll(wet, lat - 1, 1))
    faces_ref[0] = klon_ref[...] * wet * east
    faces_ref[1] = klat_ref[...] * wet * north
    matrix = mixing_matrix(v_ref[...])
    for g in range(cols // group):
        x = control_ref[:, g * group : (g + 1) * group, :].reshape(WIDE, lat)
        y = product(matrix, split(x))
        mixed_ref[g * group : (g + 1) * group] = y.reshape(group, levels, lat)
    halo = PASSES
    for out, start in ((left_ref, 0), (right_ref, cols - halo)):
        out[0:halo] = mixed_ref[start : start + halo]
        for k in range(2):
            out[halo + k, 0:halo, :] = faces_ref[k, start : start + halo, :]
            out[halo + k, halo:levels, :] = jnp.zeros((levels - halo, lat), F32)
        out[halo, halo : halo + 1, :] = wet[0:1]


def build_faces(faces_ref, mask_ref, from_left, from_right, lon_ref, lat_ref):
    halo = PASSES
    cols = faces_ref.shape[1]
    shape = lon_ref.shape[1:]
    for c in range(cols + 2 * halo):
        if c < halo:
            lon_row = from_left[halo, c : c + 1, :]
            lat_row = from_left[halo + 1, c : c + 1, :]
            if c == halo - 1:
                lon_row = lon_row * mask_ref[0:1, :].astype(F32)
        elif c < halo + cols:
            own = c - halo
            lon_row = faces_ref[0, own : own + 1, :]
            lat_row = faces_ref[1, own : own + 1, :]
            if own == cols - 1:
                lon_row = lon_row * from_right[halo, halo : halo + 1, :]
        else:
            far = c - halo - cols
            lon_row = from_right[halo, far : far + 1, :]
            lat_row = from_right[halo + 1, far : far + 1, :]
        lon_ref[c] = jnp.broadcast_to(lon_row, shape)
        lat_ref[c] = jnp.broadcast_to(lat_row, shape)


def one_pass(src, dst, lon_ref, lat_ref, low, high):
    levels, lat = src.shape[1:]
    half = lon_ref.shape[1]
    for h in range(levels // half):
        rows = slice(h * half, (h + 1) * half)
        here = src[low, rows, :]
        flux_west = lon_ref[low - 1] * (here - src[low - 1, rows, :])
        for c in range(low, high):
            east = src[c + 1, rows, :]
            flux_east = lon_ref[c] * (east - here)
            flux_north = lat_ref[c] * (pltpu.roll(here, lat - 1, 1) - here)
            flux_south = pltpu.roll(flux_north, 1, 1)
            dst[c, rows, :] = here + (flux_east - flux_west) + (flux_north - flux_south)
            here, flux_west = east, flux_east


def diffuse(a_ref, b_ref, lon_ref, lat_ref):
    width = a_ref.shape[0]

    def pair(turn, carry):
        one_pass(a_ref, b_ref, lon_ref, lat_ref, 1, width - 1)
        one_pass(b_ref, a_ref, lon_ref, lat_ref, 2, width - 2)
        return carry

    lax.fori_loop(0, PASSES // 2, pair, 0)


def block_place(index, cols, segs):
    return index // (cols * segs), (index // segs) % cols, index % segs


def weights_kernel(index_ref, recv_ref, std_ref, mask_ref, out_ref, pick_ref, std_rows, wet_rows):
    owners, rows, _ = recv_ref.shape
    slots = rows // 2
    levels, cols, lat = std_ref.shape
    segs = lat // STEN
    for s in range(segs):
        part = slice(s * STEN, (s + 1) * STEN)
        wet_rows[s * cols : (s + 1) * cols, :] = mask_ref[:, part].astype(F32)
        for a in range(levels):
            first = (a * segs + s) * cols
            std_rows[first : first + cols, :] = std_ref[a, :, part]

    def pick(o, carry):
        for k in range(slots):
            slot = o * slots + k
            level, column, seg = block_place(index_ref[slot], cols, segs)
            value = std_rows[pl.ds((level * segs + seg) * cols + column, 1), :]
            wet = wet_rows[pl.ds(seg * cols + column, 1), :]
            pick_ref[pl.ds(slot, 1), :] = value * wet
        return carry

    lax.fori_loop(0, owners, pick, 0)
    out_ref[...] = recv_ref[:, 0:slots, :].reshape(owners * slots, STEN) * pick_ref[...]


def to_row(column):
    eye = iota((STEN, STEN), 0) == iota((STEN, STEN), 1)
    return jnp.sum(jnp.where(eye, column, F32(0.0)), axis=0, keepdims=True)


def first_kernel(
    index_ref, mixed_ref, from_left, from_right, faces_ref, mask_ref, recv_ref, ws_ref,
    spread_ref, departure_ref, a_ref, b_ref, lon_ref, lat_ref, rows_ref, pick_ref,
):
    halo = PASSES
    cols, levels, lat = mixed_ref.shape
    segs = lat // STEN
    owners, rows, _ = recv_ref.shape
    slots = rows // 2
    total = owners * slots
    build_faces(faces_ref, mask_ref, from_left, from_right, lon_ref, lat_ref)
    a_ref[0:halo] = from_left[0:halo]
    a_ref[halo : halo + cols] = mixed_ref[...]
    a_ref[halo + cols : 2 * halo + cols] = from_right[0:halo]
    diffuse(a_ref, b_ref, lon_ref, lat_ref)
    for c in range(cols):
        for s in range(segs):
            first = (c * segs + s) * levels
            rows_ref[first : first + levels, :] = a_ref[halo + c, :, s * STEN : (s + 1) * STEN]

    def pick(o, carry):
        for k in range(slots):
            slot = o * slots + k
            level, column, seg = block_place(index_ref[slot], cols, segs)
            pick_ref[pl.ds(slot, 1), :] = rows_ref[pl.ds((column * segs + seg) * levels + level, 1), :]
        return carry

    lax.fori_loop(0, owners, pick, 0)
    ws = ws_ref[...]
    meta = recv_ref[:, slots:, :].reshape(total, STEN)
    evolved = jnp.sum(pick_ref[...] * ws, axis=1, keepdims=True)
    departure = jnp.where(meta[:, 3:4] > 0.5, evolved - meta[:, 0:1], F32(0.0))
    scaled = meta[:, 1:2] * departure
    spread_ref[0:total, :] = scaled * ws
    spread_ref[total:, :] = jnp.zeros((spread_ref.shape[0] - total, STEN), F32)
    for j in range(total // STEN):
        part = slice(j * STEN, (j + 1) * STEN)
        departure_ref[j : j + 1, :] = to_row(departure[part])
        spread_ref[total + j : total + j + 1, :] = to_row(meta[part, 2:3])


def second_kernel(
    vt_ref, control_ref, own_ref, left_ref, right_ref, faces_ref, mask_ref, from_left, from_right,
    out_ref, a_ref, b_ref, lon_ref, lat_ref,
):
    halo = PASSES
    levels, cols, lat = control_ref.shape
    segs = lat // STEN
    rows = segs * levels
    total = own_ref.shape[0] // STEN * STEN
    build_faces(faces_ref, mask_ref, from_left, from_right, lon_ref, lat_ref)

    def scatter(source, first, count, place):
        keys = source[total : total + total // STEN, :].astype(jnp.int32)
        keys = (keys % (cols * segs)) * levels + keys // (cols * segs) - first * rows
        pieces = [jnp.concatenate(split(source[j * STEN : (j + 1) * STEN, :]), axis=1) for j in range(total // STEN)]
        for c in range(count):
            sums = jnp.zeros((rows, 2 * STEN), F32)
            for j, piece in enumerate(pieces):
                hit = iota((rows, STEN), 0) + c * rows == keys[j : j + 1, :]
                sums = sums + dot(onehot(hit), piece)
            sums = sums[:, :STEN] + sums[:, STEN:]
            for s in range(segs):
                a_ref[place + c, :, s * STEN : (s + 1) * STEN] = sums[s * levels : (s + 1) * levels]

    scatter(own_ref, 0, cols, halo)
    scatter(left_ref, cols - halo, halo, 0)
    scatter(right_ref, 0, halo, halo + cols)
    diffuse(a_ref, b_ref, lon_ref, lat_ref)
    matrix = mixing_matrix_back(vt_ref[...])
    group = WIDE // levels
    for g in range(cols // group):
        part = slice(g * group, (g + 1) * group)
        x = a_ref[halo + g * group : halo + (g + 1) * group].reshape(WIDE, lat)
        y = product(matrix, split(x)).reshape(levels, group, lat)
        out_ref[:, part, :] = control_ref[:, part, :] + y


def call(kernel, out_shape, specs, scratch=()):
    return pl.pallas_call(
        kernel,
        out_shape=out_shape,
        in_specs=specs,
        out_specs=jax.tree.map(lambda _: VMEM_SPEC, out_shape),
        scratch_shapes=list(scratch),
        compiler_params=pltpu.CompilerParams(vmem_limit_bytes=VMEM_LIMIT),
    )


def shape(*dims):
    return jax.ShapeDtypeStruct(dims, F32)


def local(
    control, std_field, kappa_lon, kappa_lat, sea_mask, vertical,
    block_index, weights, obs_value, obs_rinv, obs_count,
):
    levels, cols, lat = control.shape
    owners, slots = block_index.shape[1:]
    total = owners * slots
    halo = PASSES
    width = cols + 2 * halo
    count = lax.axis_size("lon")
    to_right = [(i, (i + 1) % count) for i in range(count)]
    to_left = [((i + 1) % count, i) for i in range(count)]

    valid = jnp.arange(slots, dtype=jnp.int32)[None, :] < obs_count[0][:, None]
    meta = jnp.stack(
        [obs_value[0], obs_rinv[0], block_index[0].astype(F32), valid.astype(F32)], axis=-1
    )
    meta = jnp.pad(meta, ((0, 0), (0, 0), (0, STEN - 4)))
    sent = jnp.concatenate([weights[0], meta], axis=1)

    mixed, faces, edge_left, edge_right = call(
        head_kernel,
        (shape(cols, levels, lat), shape(2, cols, lat), shape(halo + 2, levels, lat), shape(halo + 2, levels, lat)),
        [VMEM_SPEC] * 5,
    )(vertical, control, kappa_lon, kappa_lat, sea_mask)
    from_left = lax.ppermute(edge_right, "lon", to_right)
    from_right = lax.ppermute(edge_left, "lon", to_left)

    recv = lax.all_to_all(sent, "lon", split_axis=0, concat_axis=0, tiled=True)
    index = recv[:, slots:, 2].reshape(total).astype(jnp.int32)
    picked = pltpu.VMEM((total, STEN), F32)
    blocks = pltpu.VMEM((levels * cols * lat // STEN, STEN), F32)
    ws = call(
        weights_kernel, shape(total, STEN), [SMEM_SPEC] + [VMEM_SPEC] * 3, [picked, blocks, pltpu.VMEM((cols * lat // STEN, STEN), F32)]
    )(index, recv, std_field, sea_mask)

    field = pltpu.VMEM((width, levels, lat), F32)
    face = pltpu.VMEM((width, 8, lat), F32)
    extra = -(-total // (8 * STEN)) * 8
    spread, departure = call(
        first_kernel,
        (shape(total + extra, STEN), shape(total // STEN, STEN)),
        [SMEM_SPEC] + [VMEM_SPEC] * 7,
        [field, field, face, face, blocks, picked],
    )(index, mixed, from_left, from_right, faces, sea_mask, recv, ws)

    spread_left = lax.ppermute(spread, "lon", to_right)
    spread_right = lax.ppermute(spread, "lon", to_left)
    everyone = lax.all_gather(departure, "lon").reshape(count, owners, slots)
    mine = lax.dynamic_index_in_dim(everyone, lax.axis_index("lon"), axis=1, keepdims=False)

    gradient = call(
        second_kernel, shape(levels, cols, lat), [VMEM_SPEC] * 9, [field, field, face, face]
    )(vertical.T, control, spread, spread_left, spread_right, faces, sea_mask, from_left, from_right)
    return gradient, mine[None]


def solution(mesh):
    in_specs = (
        P("grp", "lon", None),
        P(None, "lon", None),
        P("lon", None),
        P("lon", None),
        P("lon", None),
        P(),
        P(("grp", "lon"), None, None),
        P(("grp", "lon"), None, None, None),
        P(("grp", "lon"), None, None),
        P(("grp", "lon"), None, None),
        P(("grp", "lon"), None),
    )
    out_specs = (P("grp", "lon", None), P(("grp", "lon"), None, None))
    return jax.shard_map(local, mesh=mesh, in_specs=in_specs, out_specs=out_specs, check_vma=False)
```

time: 194 us -> 193 us (level)
  Pallas kernels: 0 us -> 146 us
  waiting for transfers between devices: 121 us -> 7.85 us
  other arithmetic: 29.4 us -> 1.08 us
  blocking collectives: 0 us -> 17.1 us
  starting transfers between devices: 28.4 us -> 13.7 us
  matrix products: 4.85 us -> 0 us
    pallas_call x0 -> x4, Pallas kernels: none -> 146 us  [the longest x1 71.2 us: local(): call(first_kernel, (shape(total + extra, STEN), shape(total // STEN, STEN...]
    ppermute x42 -> x4, waiting for transfers between devices: 105 us -> 0.01 us  [the longest x1 0.01 us: local(): from_left = lax.ppermute(edge_right, 'lon', to_right)]
    all_gather x0 -> x1, blocking collectives: none -> 17.1 us  [local(): everyone = lax.all_gather(departure, 'lon').reshape(count, owners, slots)]
    add x20 -> x0, other arithmetic: 12.8 us -> none  [smooth_step(): centre + (flux_lon[:, 1:] - flux_lon[:, :-1])]
    mul x46 -> x0, other arithmetic: 12.4 us -> none  [the longest x20 6.82 us: smooth_step(): flux_lat = face_lat[None] * (centre[:, :, 1:] - centre[:, :, :-1])]
    all_to_all x3 -> x1, waiting for transfers between devices: 15.9 us -> 7.84 us  [local(): recv = lax.all_to_all(sent, 'lon', split_axis=0, concat_axis=0, tiled=True)]
    ppermute x42 -> x4, starting transfers between devices: 17.8 us -> 9.93 us  [the longest x1 4.99 us: local(): from_right = lax.ppermute(edge_left, 'lon', to_left)]
    all_to_all x3 -> x1, starting transfers between devices: 10.6 us -> 3.82 us  [local(): recv = lax.all_to_all(sent, 'lon', split_axis=0, concat_axis=0, tiled=True)]
  transfers between devices with their start and end apart: 45 -> 5, of which waited for: 43 -> 1; matrix products, arithmetic and copies ran while one was open for 7% -> 1% of each run, Pallas kernels for 0% -> 1%
where the time goes in v1:
time: 193 us
  Pallas kernels  146 us (76%)
  blocking collectives  17.1 us (9%)
  starting transfers between devices  13.7 us (7%)
  waiting for transfers between devices  7.85 us (4%)
  local copies, waits for them, and re-layouts  6.14 us (3%)
    pallas_call x1, Pallas kernels, local(): call(first_kernel, (shape(total + extra, STEN), shape(total // STEN, STEN...  71.2 us
    pallas_call x1, Pallas kernels, local(): call(second_kernel, shape(levels, cols, lat), [VMEM_SPEC] * 9, [field, fi...  70.9 us
    all_gather x1, blocking collectives, local(): everyone = lax.all_gather(departure, 'lon').reshape(count, owners, slots)  17.1 us
    all_to_all x1, waiting for transfers between devices, local(): recv = lax.all_to_all(sent, 'lon', split_axis=0, concat_axis=0, tiled=True)  7.84 us
    unnamed x29, local copies, waits for them, and re-layouts  5.22 us
    ppermute x1, starting transfers between devices, local(): from_right = lax.ppermute(edge_left, 'lon', to_left)  4.99 us
    ppermute x1, starting transfers between devices, local(): spread_right = lax.ppermute(spread, 'lon', to_left)  4.43 us
  transfers between devices with their start and end apart: 5, of which 1 were waited for; matrix products, arithmetic and copies ran while one was open for 1% of the time, Pallas kernels for 1%

profile of v1, /device:TPU:0, one launch (start us, length us, event | category | flops | bytes accessed | tf_op | source)
XLA Modules:
  0.0 192.6 jit_solution(3267863850196536249)
XLA Ops:
  0.6 0.0 copy-start
  0.6 1.2 copy-done
  1.9 0.8 copy-done.2
  2.7 0.8 copy-done.5
  3.5 0.8 copy-done.6
  4.4 0.7 copy-done.7
  5.1 1.5 shard_map.122
  6.5 0.5 collective-permute-start
  7.0 5.0 %collective-permute-start.1 = (f32[12,16,512]{2,1,0:T(8,128)}, f32[12,16,512]{2,1,0:T(8,128)S(1)}, u32[]{:S(2)}, u32[]{:S(2)}) collective-permute-start(f32[12,16,512]{2,1,0:T(8,128)} %get-tuple-element.10), channel_id=1, source_target_pairs={{1,0},{2,1},{3,2},{4,3},{5,4},{6,5},{7,6},{8,7},{9,8},{10,9},{11,1... | collective-permute-start | bytes 1179656 | tf_op jit(solution)/shard_map/ppermute | solution.py:293
  12.0 0.6 copy-done.11
  12.7 0.0 copy-done.12
  12.7 0.1 copy.24
  12.8 0.0 copy-done.9
  12.9 0.7 select_maximum_fusion
  13.5 3.8 %all-to-all-start = ((f32[16,16,128]{2,1,0:T(8,128)}), f32[16,16,128]{2,1,0:T(8,128)S(1)}, u32[]{:S(2)}, u32[]{:S(2)}) async-start(f32[16,16,128]{2,1,0:T(8,128)} %select_maximum_fusion), calls=%async_computation | async-start | bytes 262144 | tf_op jit(solution)/shard_map/all_to_all | solution.py:295
  17.3 0.0 copy-start.3
  17.4 0.1 copy.23
  17.4 7.8 %all-to-all-done.recv_ref = f32[16,16,128]{2,1,0:T(8,128)S(1)} async-done(((f32[16,16,128]{2,1,0:T(8,128)}), f32[16,16,128]{2,1,0:T(8,128)S(1)}, u32[]{:S(2)}, u32[]{:S(2)}) %all-to-all-start) | async-done | bytes 131104 | tf_op jit(solution)/shard_map/all_to_all | solution.py:295
  25.3 0.4 fusion
  25.7 0.1 convert_element_type.34.index_ref
  25.8 2.4 %shard_map.123.ws_ref = f32[128,128]{1,0:T(8,128)S(1)} custom-call(s32[128]{0:T(128)S(1)} %convert_element_type.34.index_ref, f32[16,16,128]{2,1,0:T(8,128)S(1)} %all-to-all-done.recv_ref, f32[16,32,512]{2,1,0:T(8,128)S(1)} %copy-done.4, s32[32,512]{1,0:T(8,128)S(1)} %copy-done.3), custom_call_target="tpu_custom_call" | custom-call | tf_op jit(solution)/shard_map/pallas_call | solution.py:299
  28.2 0.0 collective-permute-done.from_left
  28.2 0.0 collective-permute-done.1.from_right
  28.2 0.0 copy-start.1
  28.2 71.2 %shard_map.124 = (f32[136,128]{1,0:T(8,128)S(1)}, f32[1,128]{1,0:T(1,128)S(1)}) custom-call(s32[128]{0:T(128)S(1)} %convert_element_type.34.index_ref, f32[32,16,512]{2,1,0:T(8,128)S(1)} %get-tuple-element.8.mixed_ref, f32[12,16,512]{2,1,0:T(8,128)S(1)} %collective-permute-done.from_left, f32[12,16,512]{2,1,0:T(8,128)S(1)} %collective-permute-done.1.from_right, ...), custom_call_target="tpu_custom_call" | custom-call | tf_op jit(solution)/shard_map/pallas_call | solution.py:306
  99.4 0.1 collective-permute-start.2
  99.4 4.4 %collective-permute-start.3 = (f32[136,128]{1,0:T(8,128)S(1)}, f32[136,128]{1,0:T(8,128)S(1)}, u32[]{:S(2)}, u32[]{:S(2)}) collective-permute-start(f32[136,128]{1,0:T(8,128)S(1)} %get-tuple-element.12.own_ref), channel_id=1, source_target_pairs={{1,0},{2,1},{3,2},{4,3},{5,4},{6,5},{7,6},{8,7},{9,8},{10,9},{11,1... | collective-permute-start | bytes 208904 | tf_op jit(solution)/shard_map/ppermute | solution.py:314
  103.9 17.1 %all-gather.1 = f32[16,1,128]{2,1,0:T(1,128)S(1)} all-gather(f32[1,1,128]{2,1,0:T(1,128)S(1)} %bitcast.12), channel_id=2, replica_groups=mesh['grp'=2,'lon'=16] {'lon'}, dimensions={0}, use_global_device_ids=true | all-gather | bytes 8704 | tf_op jit(solution)/shard_map/all_gather | solution.py:315
  120.9 0.1 copy.25
  121.0 0.6 dynamic-slice_bitcast_fusion
  121.6 0.0 collective-permute-done.2.left_ref
  121.6 70.9 %shard_map.125 = f32[16,32,512]{2,1,0:T(8,128)} custom-call(f32[16,16]{1,0:T(8,128)S(1)} %bitcast.11, f32[16,32,512]{2,1,0:T(8,128)S(1)} %copy-done.1, f32[136,128]{1,0:T(8,128)S(1)} %get-tuple-element.12.own_ref, f32[136,128]{1,0:T(8,128)S(1)} %collective-permute-done.2.left_ref, f32[136,128]{1,0:T(8,128)S(1)} %collective-permute-done.3.right_ref, ...), custom_call_target="tpu_custom_call" | custom-call | tf_op jit(solution)/shard_map/pallas_call | solution.py:318
  (21 shorter events, 0.0 us)
Async XLA Ops:
  0.6 1.2 copy-start
  1.9 0.8 copy-start.2
  2.7 0.8 copy-start.5
  3.5 0.8 copy-start.6
  4.4 0.7 copy-start.7
  5.1 6.9 %copy-start.13 = (s32[1,16]{1,0:T(1,128)S(1)}, s32[1,16]{1,0:T(1,128)}, u32[]{:S(2)}) copy-start(s32[1,16]{1,0:T(1,128)} %param.21) | copy-start | bytes 196
  5.1 20.7 %copy-start.4 = (f32[16,32,512]{2,1,0:T(8,128)S(1)}, f32[16,32,512]{2,1,0:T(8,128)}, u32[]{:S(2)}) copy-start(f32[16,32,512]{2,1,0:T(8,128)} %std_ref.1) | copy-start | bytes 3145732
  6.5 5.5 %copy-start.10 = (s32[1,16,8]{1,2,0:T(8,128)S(1)}, s32[1,16,8]{1,2,0:T(8,128)}, u32[]{:S(2)}) copy-start(s32[1,16,8]{1,2,0:T(8,128)} %param.17) | copy-start | bytes 1540
  6.5 21.6 %collective-permute-start = (f32[12,16,512]{2,1,0:T(8,128)}, f32[12,16,512]{2,1,0:T(8,128)S(1)}, u32[]{:S(2)}, u32[]{:S(2)}) collective-permute-start(f32[12,16,512]{2,1,0:T(8,128)} %get-tuple-element.9), channel_id=1, source_target_pairs={{0,1},{1,2},{2,3},{3,4},{4,5},{5,6},{6,7},{7,8},{8,9},{9,10},{10,1... | collective-permute-start | bytes 1179656 | tf_op jit(solution)/shard_map/ppermute | solution.py:292
  7.0 21.2 %collective-permute-start.1 = (f32[12,16,512]{2,1,0:T(8,128)}, f32[12,16,512]{2,1,0:T(8,128)S(1)}, u32[]{:S(2)}, u32[]{:S(2)}) collective-permute-start(f32[12,16,512]{2,1,0:T(8,128)} %get-tuple-element.10), channel_id=1, source_target_pairs={{1,0},{2,1},{3,2},{4,3},{5,4},{6,5},{7,6},{8,7},{9,8},{10,9},{11,1... | collective-permute-start | bytes 1179656 | tf_op jit(solution)/shard_map/ppermute | solution.py:293
  12.0 0.7 copy-start.11
  12.0 0.7 copy-start.12
  12.0 0.9 copy-start.9
  13.5 3.8 %copy-start.8 = (f32[16,16]{1,0:T(8,128)S(1)}, f32[16,16]{1,0:T(8,128)}, u32[]{:S(2)}) copy-start(f32[16,16]{1,0:T(8,128)} %v_ref.1) | copy-start | bytes 3076
  13.5 11.8 %all-to-all-start = ((f32[16,16,128]{2,1,0:T(8,128)}), f32[16,16,128]{2,1,0:T(8,128)S(1)}, u32[]{:S(2)}, u32[]{:S(2)}) async-start(f32[16,16,128]{2,1,0:T(8,128)} %select_maximum_fusion), calls=%async_computation | async-start | bytes 262144 | tf_op jit(solution)/shard_map/all_to_all | solution.py:295
  17.3 8.5 %copy-start.3 = (s32[32,512]{1,0:T(8,128)S(1)}, s32[32,512]{1,0:T(8,128)}, u32[]{:S(2)}) copy-start(s32[32,512]{1,0:T(8,128)} %mask_ref.7) | copy-start | bytes 196612
  28.2 93.5 %copy-start.1 = (f32[16,32,512]{2,1,0:T(8,128)S(1)}, f32[16,32,512]{2,1,0:T(8,128)}, u32[]{:S(2)}) copy-start(f32[16,32,512]{2,1,0:T(8,128)} %control_ref.3) | copy-start | bytes 3145732
  99.4 22.3 %collective-permute-start.2 = (f32[136,128]{1,0:T(8,128)S(1)}, f32[136,128]{1,0:T(8,128)S(1)}, u32[]{:S(2)}, u32[]{:S(2)}) collective-permute-start(f32[136,128]{1,0:T(8,128)S(1)} %get-tuple-element.12.own_ref), channel_id=1, source_target_pairs={{0,1},{1,2},{2,3},{3,4},{4,5},{5,6},{6,7},{7,8},{8,9},{9,10},{10,1... | collective-permute-start | bytes 208904 | tf_op jit(solution)/shard_map/ppermute | solution.py:313
  99.4 22.2 %collective-permute-start.3 = (f32[136,128]{1,0:T(8,128)S(1)}, f32[136,128]{1,0:T(8,128)S(1)}, u32[]{:S(2)}, u32[]{:S(2)}) collective-permute-start(f32[136,128]{1,0:T(8,128)S(1)} %get-tuple-element.12.own_ref), channel_id=1, source_target_pairs={{1,0},{2,1},{3,2},{4,3},{5,4},{6,5},{7,6},{8,7},{9,8},{10,9},{11,1... | collective-permute-start | bytes 208904 | tf_op jit(solution)/shard_map/ppermute | solution.py:314

commit v2 on v1

v2 whole, which is shorter than its diff:
```python
import jax
import jax.numpy as jnp
from jax import lax
from jax.experimental import pallas as pl
from jax.experimental.pallas import tpu as pltpu
from jax.sharding import PartitionSpec as P

STEN = 128
PASSES = 10
WIDE = 256
F32 = jnp.float32
BF16 = jnp.bfloat16
VMEM_LIMIT = 40 * 1024 * 1024

VMEM_SPEC = pl.BlockSpec(memory_space=pltpu.VMEM)
SMEM_SPEC = pl.BlockSpec(memory_space=pltpu.SMEM)


def split(x):
    high = x.astype(BF16)
    return high, (x - high.astype(F32)).astype(BF16)


def split3(x):
    high = x.astype(BF16)
    rest = x - high.astype(F32)
    middle = rest.astype(BF16)
    return high, middle, (rest - middle.astype(F32)).astype(BF16)


def dot(a, b):
    return jnp.dot(a, b, preferred_element_type=F32)


def log2(n):
    assert n & (n - 1) == 0
    return n.bit_length() - 1


def iota(shape, dim):
    return lax.broadcasted_iota(jnp.int32, shape, dim)


def onehot(condition):
    return jnp.where(condition, F32(1.0), F32(0.0)).astype(BF16)


def product(left, right):
    (lh, ll), (rh, rl) = left, right
    return dot(lh, rh) + (dot(lh, rl) + dot(ll, rh))


def mixing_matrix(vertical):
    levels = vertical.shape[0]
    group = WIDE // levels
    expand = onehot(iota((levels, WIDE), 1) // group == iota((levels, WIDE), 0))
    keep = iota((WIDE, WIDE), 0) // levels == iota((WIDE, WIDE), 1) % group
    out = []
    for part in split(vertical):
        rows = dot(part, expand)
        tiled = jnp.concatenate([rows] * group, axis=0)
        out.append(jnp.where(keep, tiled, F32(0.0)).astype(BF16))
    return tuple(out)


def mixing_matrix_back(vertical_t):
    levels = vertical_t.shape[0]
    group = WIDE // levels
    spread = onehot(iota((levels, WIDE), 1) % levels == iota((levels, WIDE), 0))
    repeat = onehot(iota((WIDE, levels), 0) // group == iota((WIDE, levels), 1))
    keep = iota((WIDE, WIDE), 0) % group == iota((WIDE, WIDE), 1) // levels
    out = []
    for part in split(vertical_t):
        rows = dot(part, spread).astype(BF16)
        out.append(jnp.where(keep, dot(repeat, rows), F32(0.0)).astype(BF16))
    return tuple(out)


def deinterleave(lat):
    parts = lat // STEN
    target = iota((lat, lat), 1)
    return onehot(iota((lat, lat), 0) == (target % STEN) * parts + target // STEN)


def interleave(lat):
    parts = lat // STEN
    source = iota((lat, lat), 0)
    return onehot(iota((lat, lat), 1) == (source % STEN) * parts + source // STEN)


def spread_block(lat):
    parts = lat // STEN
    target = iota((STEN, lat), 1)
    return onehot(iota((STEN, lat), 0) == (target % (STEN // parts)) * parts + target // STEN)


def lane_segment(rows, lat):
    parts = lat // STEN
    return (iota((rows, lat), 1) % STEN) // (STEN // parts)


def move(x, matrix):
    return tuple(dot(part, matrix).astype(BF16) for part in x)


def head_kernel(
    v_ref, control_hbm, klon_hbm, klat_hbm, mask_hbm, mixed_ref, faces_ref, left_ref, right_ref,
    control_ref, klon_ref, klat_ref, mask_ref, sems,
):
    copies = [
        pltpu.make_async_copy(source, target, sems.at[k])
        for k, (source, target) in enumerate(
            ((mask_hbm, mask_ref), (klon_hbm, klon_ref), (klat_hbm, klat_ref), (control_hbm, control_ref))
        )
    ]
    for copy in copies:
        copy.start()
    levels, cols, lat = control_ref.shape
    parts = lat // STEN
    group = WIDE // levels
    halo = PASSES
    edge = halo * levels
    place = deinterleave(lat)
    matrix = mixing_matrix(v_ref[...])
    for copy in copies[:3]:
        copy.wait()
    wet = mask_ref[...].astype(F32)
    east = jnp.where(iota((cols, lat), 0) == cols - 1, F32(1.0), pltpu.roll(wet, cols - 1, 0))
    north = jnp.where(iota((cols, lat), 1) == lat - 1, F32(0.0), pltpu.roll(wet, lat - 1, 1))
    for k, face in enumerate((klon_ref[...] * wet * east, klat_ref[...] * wet * north, wet)):
        held = sum(dot(piece, place) for piece in (split3(face) if k < 2 else (face.astype(BF16),)))
        for q in range(parts):
            faces_ref[k * parts + q] = held[:, q * STEN : (q + 1) * STEN]
    copies[3].wait()
    for g in range(cols // group):
        x = control_ref[:, g * group : (g + 1) * group, :].reshape(WIDE, lat)
        y = product(matrix, move(split(x), place))
        for q in range(parts):
            mixed_ref[q, g * WIDE : (g + 1) * WIDE, :] = y[:, q * STEN : (q + 1) * STEN]
    for out, start in ((left_ref, 0), (right_ref, cols - halo)):
        for q in range(parts):
            out[q * edge : (q + 1) * edge, :] = mixed_ref[q, start * levels : start * levels + edge, :]
        for k in range(2 * parts):
            first = parts * edge + k * halo
            out[first : first + halo, :] = faces_ref[k, start : start + halo, :]
        first = parts * edge + 2 * parts * halo
        for q in range(parts):
            out[first + q : first + q + 1, :] = faces_ref[2 * parts + q, 0:1, :]
        out[first + parts :, :] = jnp.zeros((out.shape[0] - first - parts, STEN), F32)


def build_faces(faces_ref, from_left, from_right, lon_ref, lat_ref, levels):
    halo = PASSES
    cols = faces_ref.shape[1]
    parts = faces_ref.shape[0] // 3
    first = parts * halo * levels
    shape = (8, STEN)

    def far(source, k, c):
        at = first + k * halo + c
        return source[at : at + 1, :]

    for c in range(cols + 2 * halo):
        rows = slice(8 * c, 8 * c + 8)
        for q in range(parts):
            if c < halo:
                lon_row, lat_row = far(from_left, q, c), far(from_left, parts + q, c)
                if c == halo - 1:
                    lon_row = lon_row * faces_ref[2 * parts + q, 0:1, :]
            elif c < halo + cols:
                own = c - halo
                lon_row = faces_ref[q, own : own + 1, :]
                lat_row = faces_ref[parts + q, own : own + 1, :]
                if own == cols - 1:
                    at = first + 2 * parts * halo + q
                    lon_row = lon_row * from_right[at : at + 1, :]
            else:
                own = c - halo - cols
                lon_row, lat_row = far(from_right, q, own), far(from_right, parts + q, own)
            lon_ref[q, rows, :] = jnp.broadcast_to(lon_row, shape)
            lat_ref[q, rows, :] = jnp.broadcast_to(lat_row, shape)
            if q == parts - 1:
                lat_ref[parts, rows, :] = jnp.broadcast_to(pltpu.roll(lat_row, 1, 1), shape)


def add_ghosts(ref, first, values):
    count = values[0].shape[0]
    parts = len(values)
    ref[parts, first : first + count, :] = pltpu.roll(values[0], STEN - 1, 1)
    ref[parts + 1, first : first + count, :] = pltpu.roll(values[-1], 1, 1)


def fill(ref, first, values):
    for q, value in enumerate(values):
        ref[q, first : first + value.shape[0], :] = value
    add_ghosts(ref, first, values)


def one_pass(src, dst, lon_ref, lat_ref, levels, low, high):
    parts = lon_ref.shape[0]
    halves = range(levels // 8)

    def load(k, c, h):
        return src[k, c * levels + 8 * h : c * levels + 8 * h + 8, :]

    def face(ref, k, c):
        return ref[k, 8 * c : 8 * c + 8, :]

    here = [[load(q, low, h) for q in range(parts)] for h in halves]
    west = [[face(lon_ref, q, low - 1) * (here[h][q] - load(q, low - 1, h)) for q in range(parts)] for h in halves]
    for c in range(low, high):
        lon = [face(lon_ref, q, c) for q in range(parts)]
        lat = [face(lat_ref, q, c) for q in range(parts + 1)]
        for h in halves:
            line = here[h]
            east = [load(q, c + 1, h) for q in range(parts)]
            flux_east = [lon[q] * (east[q] - line[q]) for q in range(parts)]
            ahead = line[1:] + [load(parts, c, h)]
            flux_north = [lat[parts] * (line[0] - load(parts + 1, c, h))]
            flux_north += [lat[q] * (ahead[q] - line[q]) for q in range(parts)]
            out = [
                line[q] + (flux_east[q] - west[h][q]) + (flux_north[q + 1] - flux_north[q])
                for q in range(parts)
            ]
            first = c * levels + 8 * h
            for q in range(parts):
                dst[q, first : first + 8, :] = out[q]
            add_ghosts(dst, first, out)
            here[h], west[h] = east, flux_east


def diffuse(a_ref, b_ref, lon_ref, lat_ref, levels):
    width = a_ref.shape[1] // levels

    def pair(turn, carry):
        one_pass(a_ref, b_ref, lon_ref, lat_ref, levels, 1, width - 1)
        one_pass(b_ref, a_ref, lon_ref, lat_ref, levels, 2, width - 2)
        return carry

    lax.fori_loop(0, PASSES // 2, pair, 0)


def block_place(index, cols, parts):
    return (
        lax.shift_right_logical(index, log2(cols * parts)),
        lax.shift_right_logical(index, log2(parts)) & (cols - 1),
        index & (parts - 1),
    )


def weights_kernel(index_ref, recv_ref, std_ref, mask_ref, out_ref, held_ref, pick_ref, std_rows, wet_rows):
    owners, rows, _ = recv_ref.shape
    slots = rows // 2
    total = owners * slots
    levels, cols, lat = std_ref.shape
    parts = lat // STEN
    for s in range(parts):
        part = slice(s * STEN, (s + 1) * STEN)
        wet_rows[s * cols : (s + 1) * cols, :] = mask_ref[:, part].astype(F32)
        for a in range(levels):
            first = (a * parts + s) * cols
            std_rows[first : first + cols, :] = std_ref[a, :, part]

    def pick(o, carry):
        for k in range(slots):
            slot = o * slots + k
            level, column, seg = block_place(index_ref[slot], cols, parts)
            value = std_rows[pl.ds((level * parts + seg) * cols + column, 1), :]
            wet = wet_rows[pl.ds(seg * cols + column, 1), :]
            pick_ref[pl.ds(slot, 1), :] = value * wet
        return carry

    lax.fori_loop(0, owners, pick, 0)
    ws = recv_ref[:, 0:slots, :].reshape(total, STEN) * pick_ref[...]
    out_ref[...] = ws
    place = spread_block(lat)
    for j in range(total // STEN):
        part = slice(j * STEN, (j + 1) * STEN)
        index = recv_ref[j * (STEN // slots) : (j + 1) * (STEN // slots), slots:, :].reshape(STEN, STEN)
        seg = index[:, 2:3].astype(jnp.int32) & (parts - 1)
        held = sum(dot(piece, place) for piece in split3(ws[part]))
        held = jnp.where(lane_segment(STEN, lat) == seg, held, F32(0.0))
        for q in range(parts):
            held_ref[q, part, :] = held[:, q * STEN : (q + 1) * STEN]


def to_row(column):
    eye = iota((STEN, STEN), 0) == iota((STEN, STEN), 1)
    return jnp.sum(jnp.where(eye, column, F32(0.0)), axis=0, keepdims=True)


def to_column(row):
    eye = iota((STEN, STEN), 0) == iota((STEN, STEN), 1)
    return jnp.sum(jnp.where(eye, row, F32(0.0)), axis=1, keepdims=True)


def first_kernel(
    index_ref, mixed_ref, from_left, from_right, faces_ref, recv_ref, ws_ref, held_ref,
    spread_ref, departure_ref, a_ref, b_ref, lon_ref, lat_ref, pick_ref,
):
    halo = PASSES
    parts, own_rows, _ = mixed_ref.shape
    owners, rows, _ = recv_ref.shape
    cols = faces_ref.shape[1]
    levels = own_rows // cols
    slots = rows // 2
    total = owners * slots
    edge = halo * levels
    build_faces(faces_ref, from_left, from_right, lon_ref, lat_ref, levels)
    fill(a_ref, 0, [from_left[q * edge : (q + 1) * edge, :] for q in range(parts)])
    fill(a_ref, edge, [mixed_ref[q] for q in range(parts)])
    fill(a_ref, edge + own_rows, [from_right[q * edge : (q + 1) * edge, :] for q in range(parts)])
    diffuse(a_ref, b_ref, lon_ref, lat_ref, levels)

    def pick(o, carry):
        for k in range(slots):
            slot = o * slots + k
            level, column, _ = block_place(index_ref[slot], cols, parts)
            row = edge + column * levels + level
            for q in range(parts):
                pick_ref[q, pl.ds(slot, 1), :] = a_ref[q, pl.ds(row, 1), :]
        return carry

    lax.fori_loop(0, owners, pick, 0)
    meta = recv_ref[:, slots:, :].reshape(total, STEN)
    evolved = sum(pick_ref[q] * held_ref[q] for q in range(parts))
    evolved = jnp.sum(evolved, axis=1, keepdims=True)
    departure = jnp.where(meta[:, 3:4] > 0.5, evolved - meta[:, 0:1], F32(0.0))
    scaled = meta[:, 1:2] * departure
    spread_ref[0:total, :] = scaled * ws_ref[...]
    spread_ref[total:, :] = jnp.zeros((spread_ref.shape[0] - total, STEN), F32)
    for j in range(total // STEN):
        part = slice(j * STEN, (j + 1) * STEN)
        spread_ref[total + j : total + j + 1, :] = to_row(meta[part, 2:3])
    lanes = jnp.where(iota((total, STEN), 1) == (iota((total, STEN), 0) & (slots - 1)), departure, F32(0.0))
    departure_ref[...] = jnp.sum(lanes.reshape(owners, slots, STEN), axis=1)


def second_kernel(
    vt_ref, control_ref, own_ref, left_ref, right_ref, faces_ref, from_left, from_right,
    out_ref, a_ref, b_ref, lon_ref, lat_ref,
):
    halo = PASSES
    levels, cols, lat = control_ref.shape
    parts = lat // STEN
    edge = halo * levels
    total = own_ref.shape[0] // STEN * STEN
    build_faces(faces_ref, from_left, from_right, lon_ref, lat_ref, levels)
    place = spread_block(lat)

    def scatter(source, first, count, step, target):
        pieces = []
        keys = []
        for j in range(total // STEN):
            index = source[total + j : total + j + 1, :].astype(jnp.int32)
            level, column, seg = block_place(index, cols, parts)
            keys.append((column - first) * levels + level)
            keep = lane_segment(STEN, lat) == to_column(seg.astype(F32)).astype(jnp.int32)
            held = [dot(piece, place) for piece in split(source[j * STEN : (j + 1) * STEN, :])]
            held = [jnp.where(keep, piece, F32(0.0)).astype(BF16) for piece in held]
            pieces.append(jnp.concatenate(held, axis=1))
        for c in range(0, count, step):
            rows = step * levels
            sums = jnp.zeros((rows, 2 * lat), F32)
            for key, piece in zip(keys, pieces):
                sums = sums + dot(onehot(iota((rows, STEN), 0) + c * levels == key), piece)
            sums = sums[:, :lat] + sums[:, lat:]
            fill(a_ref, (target + c) * levels, [sums[:, q * STEN : (q + 1) * STEN] for q in range(parts)])

    scatter(own_ref, 0, cols, 8, halo)
    scatter(left_ref, cols - halo, halo, halo // 2, 0)
    scatter(right_ref, 0, halo, halo // 2, halo + cols)
    diffuse(a_ref, b_ref, lon_ref, lat_ref, levels)
    matrix = mixing_matrix_back(vt_ref[...])
    back = interleave(lat)
    group = WIDE // levels
    for g in range(cols // group):
        part = slice(g * group, (g + 1) * group)
        rows = slice(edge + g * WIDE, edge + (g + 1) * WIDE)
        x = jnp.concatenate([a_ref[q, rows, :] for q in range(parts)], axis=1)
        y = product(matrix, move(split(x), back)).reshape(levels, group, lat)
        out_ref[:, part, :] = control_ref[:, part, :] + y


def call(kernel, out_shape, specs, scratch=()):
    return pl.pallas_call(
        kernel,
        out_shape=out_shape,
        in_specs=specs,
        out_specs=jax.tree.map(lambda _: VMEM_SPEC, out_shape),
        scratch_shapes=list(scratch),
        compiler_params=pltpu.CompilerParams(vmem_limit_bytes=VMEM_LIMIT),
    )


def shape(*dims):
    return jax.ShapeDtypeStruct(dims, F32)


def local(
    control, std_field, kappa_lon, kappa_lat, sea_mask, vertical,
    block_index, weights, obs_value, obs_rinv, obs_count,
):
    levels, cols, lat = control.shape
    parts = lat // STEN
    owners, slots = block_index.shape[1:]
    total = owners * slots
    halo = PASSES
    width = cols + 2 * halo
    count = lax.axis_size("lon")
    to_right = [(i, (i + 1) % count) for i in range(count)]
    to_left = [((i + 1) % count, i) for i in range(count)]

    valid = jnp.arange(slots, dtype=jnp.int32)[None, :] < obs_count[0][:, None]
    meta = jnp.stack(
        [obs_value[0], obs_rinv[0], block_index[0].astype(F32), valid.astype(F32)], axis=-1
    )
    meta = jnp.pad(meta, ((0, 0), (0, 0), (0, STEN - 4)))
    sent = jnp.concatenate([weights[0], meta], axis=1)

    message = parts * halo * (levels + 2) + parts
    message = -(-message // 8) * 8
    mixed, faces, edge_left, edge_right = call(
        head_kernel,
        (
            shape(parts, cols * levels, STEN), shape(3 * parts, cols, STEN),
            shape(message, STEN), shape(message, STEN),
        ),
        [VMEM_SPEC] + [pl.BlockSpec(memory_space=pl.ANY)] * 4,
        [
            pltpu.VMEM((levels, cols, lat), F32), pltpu.VMEM((cols, lat), F32), pltpu.VMEM((cols, lat), F32),
            pltpu.VMEM((cols, lat), jnp.int32), pltpu.SemaphoreType.DMA((4,)),
        ],
    )(vertical, control, kappa_lon, kappa_lat, sea_mask)
    from_left = lax.ppermute(edge_right, "lon", to_right)
    from_right = lax.ppermute(edge_left, "lon", to_left)

    recv = lax.all_to_all(sent, "lon", split_axis=0, concat_axis=0, tiled=True)
    index = recv[:, slots:, 2].reshape(total).astype(jnp.int32)
    ws, held = call(
        weights_kernel,
        (shape(total, STEN), shape(parts, total, STEN)),
        [SMEM_SPEC] + [VMEM_SPEC] * 3,
        [
            pltpu.VMEM((total, STEN), F32), pltpu.VMEM((levels * cols * parts, STEN), F32),
            pltpu.VMEM((cols * parts, STEN), F32),
        ],
    )(index, recv, std_field, sea_mask)

    field = pltpu.VMEM((parts + 2, width * levels, STEN), F32)
    faces_held = [pltpu.VMEM((parts, width * 8, STEN), F32), pltpu.VMEM((parts + 1, width * 8, STEN), F32)]
    extra = -(-total // (8 * STEN)) * 8
    spread, departure = call(
        first_kernel,
        (shape(total + extra, STEN), shape(owners, STEN)),
        [SMEM_SPEC] + [VMEM_SPEC] * 7,
        [field, field, *faces_held, pltpu.VMEM((parts, total, STEN), F32)],
    )(index, mixed, from_left, from_right, faces, recv, ws, held)

    spread_left = lax.ppermute(spread, "lon", to_right)
    spread_right = lax.ppermute(spread, "lon", to_left)
    mine = lax.all_to_all(departure[:, None, :], "lon", split_axis=0, concat_axis=0, tiled=True)

    gradient = call(
        second_kernel, shape(levels, cols, lat), [VMEM_SPEC] * 8, [field, field, *faces_held]
    )(vertical.T, control, spread, spread_left, spread_right, faces, from_left, from_right)
    return gradient, mine[:, 0, :slots][None]


def solution(mesh):
    in_specs = (
        P("grp", "lon", None),
        P(None, "lon", None),
        P("lon", None),
        P("lon", None),
        P("lon", None),
        P(),
        P(("grp", "lon"), None, None),
        P(("grp", "lon"), None, None, None),
        P(("grp", "lon"), None, None),
        P(("grp", "lon"), None, None),
        P(("grp", "lon"), None),
    )
    out_specs = (P("grp", "lon", None), P(("grp", "lon"), None, None))
    return jax.shard_map(local, mesh=mesh, in_specs=in_specs, out_specs=out_specs, check_vma=False)
```

time: 193 us -> 61.1 us (0.32)
  Pallas kernels: 146 us -> 21.7 us
  blocking collectives: 17.1 us -> 11.4 us
    pallas_call x4, Pallas kernels: 146 us -> 21.7 us  [the longest x1 9.2 us: local(): call(second_kernel, shape(levels, cols, lat), [VMEM_SPEC] * 8, [field, fi...]
    all_gather x1 -> x0, blocking collectives: 17.1 us -> none  [local(): everyone = lax.all_gather(departure, 'lon').reshape(count, owners, slots)]
    all_to_all x0 -> x1, blocking collectives: none -> 11.4 us  [local(): recv = lax.all_to_all(sent, 'lon', split_axis=0, concat_axis=0, tiled=True)]
    unnamed x29 -> x30, local copies, waits for them, and re-layouts: 5.22 us -> 6.19 us
  transfers between devices with their start and end apart: 5 -> 5, of which waited for: 1 -> 1; matrix products, arithmetic and copies ran while one was open for 1% -> 2% of each run, Pallas kernels for 1% -> 2%
where the time goes in v2:
time: 61.1 us; the launch traced here: 60.6 us
  Pallas kernels  21.7 us (36%)
  starting transfers between devices  13.6 us (22%)
  blocking collectives  11.4 us (19%)
  local copies, waits for them, and re-layouts  6.42 us (11%)
  waiting for transfers between devices  6.22 us (10%)
  between operations  0.76 us (1%)
    all_to_all x1, blocking collectives, local(): recv = lax.all_to_all(sent, 'lon', split_axis=0, concat_axis=0, tiled=True)  11.4 us
    pallas_call x1, Pallas kernels, local(): call(second_kernel, shape(levels, cols, lat), [VMEM_SPEC] * 8, [field, fi...  9.2 us
    pallas_call x1, Pallas kernels, local(): call(first_kernel, (shape(total + extra, STEN), shape(owners, STEN)), [SM...  7.75 us
    all_to_all x1, waiting for transfers between devices, local(): lax.all_to_all(departure[:, None, :], 'lon', split_axis=0, concat_axis=0,...  6.21 us
    unnamed x30, local copies, waits for them, and re-layouts  6.19 us
    ppermute x1, starting transfers between devices, local(): from_right = lax.ppermute(edge_left, 'lon', to_left)  5.06 us
    ppermute x1, starting transfers between devices, local(): spread_right = lax.ppermute(spread, 'lon', to_left)  4.44 us
    all_to_all x1, starting transfers between devices, local(): lax.all_to_all(departure[:, None, :], 'lon', split_axis=0, concat_axis=0,...  3.6 us
  transfers between devices with their start and end apart: 5, of which 1 were waited for; matrix products, arithmetic and copies ran while one was open for 2% of the time, Pallas kernels for 2%

profile of v2, /device:TPU:0, one launch (start us, length us, event | category | flops | bytes accessed | tf_op | source)
XLA Modules:
  0.0 60.6 jit_solution(3455053819119444195)
XLA Ops:
  0.6 0.0 copy-start
  0.6 1.2 %copy-done = f32[16,32,512]{2,1,0:T(8,128)S(1)} copy-done((f32[16,32,512]{2,1,0:T(8,128)S(1)}, f32[16,32,512]{2,1,0:T(8,128)}, u32[]{:S(2)}) %copy-start) | copy-done | bytes 1048600
  1.9 0.8 %copy-done.3 = s32[32,512]{1,0:T(8,128)S(1)} copy-done((s32[32,512]{1,0:T(8,128)S(1)}, s32[32,512]{1,0:T(8,128)}, u32[]{:S(2)}) %copy-start.3) | copy-done | bytes 65560
  2.7 0.8 %copy-done.5 = f32[32,512]{1,0:T(8,128)S(1)} copy-done((f32[32,512]{1,0:T(8,128)S(1)}, f32[32,512]{1,0:T(8,128)}, u32[]{:S(2)}) %copy-start.5) | copy-done | bytes 65560
  3.5 0.8 %copy-done.6 = f32[32,512]{1,0:T(8,128)S(1)} copy-done((f32[32,512]{1,0:T(8,128)S(1)}, f32[32,512]{1,0:T(8,128)}, u32[]{:S(2)}) %copy-start.6) | copy-done | bytes 65560
  4.4 0.7 %copy-done.7 = f32[16,16]{1,0:T(8,128)S(1)} copy-done((f32[16,16]{1,0:T(8,128)S(1)}, f32[16,16]{1,0:T(8,128)}, u32[]{:S(2)}) %copy-start.7) | copy-done | bytes 1048
  5.1 3.4 %shard_map.122 = (f32[4,512,128]{2,1,0:T(8,128)S(1)}, f32[12,32,128]{2,1,0:T(8,128)S(1)}, f32[728,128]{1,0:T(8,128)}, f32[728,128]{1,0:T(8,128)}) custom-call(f32[16,16]{1,0:T(8,128)S(1)} %copy-done.7, f32[16,32,512]{2,1,0:T(8,128)S(1)} %copy-done, f32[32,512]{1,0:T(8,128)S(1)} %copy-done.5, f32[32,512]{1,0:T(8,128)S(1)} %copy-done.6, s32[32,512]{1,0:T(8,128)S(1)} %copy-done.3), custom_call_target="tpu_custom_call" | custom-call | tf_op jit(solution)/shard_map/pallas_call | solution.py:423
  8.4 0.0 copy-start.10
  8.5 0.5 collective-permute-start
  9.0 5.1 %collective-permute-start.1 = (f32[728,128]{1,0:T(8,128)}, f32[728,128]{1,0:T(8,128)S(1)}, u32[]{:S(2)}, u32[]{:S(2)}) collective-permute-start(f32[728,128]{1,0:T(8,128)} %get-tuple-element.12), channel_id=1, source_target_pairs={{1,0},{2,1},{3,2},{4,3},{5,4},{6,5},{7,6},{8,7},{9,8},{10,9},{11,1... | collective-permute-start | bytes 1118216 | tf_op jit(solution)/shard_map/ppermute | solution.py:436
  14.1 0.6 %copy-done.11 = f32[1,16,8]{1,2,0:T(8,128)S(1)} copy-done((f32[1,16,8]{1,2,0:T(8,128)S(1)}, f32[1,16,8]{1,2,0:T(8,128)}, u32[]{:S(2)}) %copy-start.11) | copy-done | bytes 536
  14.7 0.0 copy-done.12
  14.7 0.1 copy.24
  14.9 0.0 copy-done.9
  14.9 11.4 %all_to_all.10.recv_ref = f32[16,16,128]{2,1,0:T(8,128)S(1)} all-to-all(f32[16,16,128]{2,1,0:T(8,128)S(1)} %select_maximum_fusion), channel_id=1, replica_groups=mesh['grp'=2,'lon'=16] {'lon'}, dimensions={0} | all-to-all | bytes 262144 | tf_op jit(solution)/shard_map/all_to_all | solution.py:438
  26.3 0.4 fusion
  26.7 0.1 convert_element_type.34.index_ref
  26.8 0.3 copy-done.4
  27.1 1.4 %shard_map.123 = (f32[128,128]{1,0:T(8,128)S(1)}, f32[4,128,128]{2,1,0:T(8,128)S(1)}) custom-call(s32[128]{0:T(128)S(1)} %convert_element_type.34.index_ref, f32[16,16,128]{2,1,0:T(8,128)S(1)} %all_to_all.10.recv_ref, f32[16,32,512]{2,1,0:T(8,128)S(1)} %copy-done.2, s32[32,512]{1,0:T(8,128)S(1)} %copy-done.4), custom_call_target="tpu_custom_call" | custom-call | tf_op jit(solution)/shard_map/pallas_call | solution.py:440
  28.5 0.0 collective-permute-done.from_left
  28.6 0.0 collective-permute-done.1.from_right
  28.6 0.0 copy-start.1
  28.6 7.7 %shard_map.124 = (f32[136,128]{1,0:T(8,128)S(1)}, f32[16,128]{1,0:T(8,128)}) custom-call(s32[128]{0:T(128)S(1)} %convert_element_type.34.index_ref, f32[4,512,128]{2,1,0:T(8,128)S(1)} %get-tuple-element.10.mixed_ref, f32[728,128]{1,0:T(8,128)S(1)} %collective-permute-done.from_left, f32[728,128]{1,0:T(8,128)S(1)} %collective-permute-done.1.from_right, ...), custom_call_target="tpu_custom_call" | custom-call | tf_op jit(solution)/shard_map/pallas_call | solution.py:453
  36.3 0.0 collective-permute-start.2
  36.3 4.4 %collective-permute-start.3 = (f32[136,128]{1,0:T(8,128)S(1)}, f32[136,128]{1,0:T(8,128)S(1)}, u32[]{:S(2)}, u32[]{:S(2)}) collective-permute-start(f32[136,128]{1,0:T(8,128)S(1)} %get-tuple-element.16.own_ref), channel_id=1, source_target_pairs={{1,0},{2,1},{3,2},{4,3},{5,4},{6,5},{7,6},{8,7},{9,8},{10,9},{11,1... | collective-permute-start | bytes 208904 | tf_op jit(solution)/shard_map/ppermute | solution.py:461
  40.8 3.6 %all-to-all-start.1 = ((f32[16,1,128]{2,1,0:T(1,128)}), f32[16,1,128]{2,1,0:T(1,128)S(1)}, u32[]{:S(2)}, u32[]{:S(2)}) async-start(f32[16,1,128]{2,1,0:T(1,128)} %bitcast.7), calls=%async_computation.1 | async-start | bytes 16384 | tf_op jit(solution)/shard_map/all_to_all | solution.py:462
  44.4 0.1 copy.23
  44.5 6.2 %all-to-all-done.1 = f32[16,1,128]{2,1,0:T(1,128)S(1)} async-done(((f32[16,1,128]{2,1,0:T(1,128)}), f32[16,1,128]{2,1,0:T(1,128)S(1)}, u32[]{:S(2)}, u32[]{:S(2)}) %all-to-all-start.1) | async-done | bytes 8224 | tf_op jit(solution)/shard_map/all_to_all | solution.py:462
  50.7 0.7 %copy.27 = f32[16,1,8]{0,2,1:T(8,128)} copy(f32[16,1,8]{2,1,0:T(1,128)S(1)} %bitcast.14) | data formatting | bytes 1024
  51.3 0.0 collective-permute-done.2.left_ref
  51.3 0.0 collective-permute-done.3.right_ref
  51.3 9.2 %shard_map.125 = f32[16,32,512]{2,1,0:T(8,128)} custom-call(f32[16,16]{1,0:T(8,128)S(1)} %bitcast.12, f32[16,32,512]{2,1,0:T(8,128)S(1)} %copy-done.1, f32[136,128]{1,0:T(8,128)S(1)} %get-tuple-element.16.own_ref, f32[136,128]{1,0:T(8,128)S(1)} %collective-permute-done.2.left_ref, f32[136,128]{1,0:T(8,128)S(1)} %collective-permute-done.3.right_ref, ...), custom_call_target="tpu_custom_call" | custom-call | tf_op jit(solution)/shard_map/pallas_call | solution.py:464
  (20 shorter events, 0.1 us)
Async XLA Ops:
  0.6 1.2 %copy-start = (f32[16,32,512]{2,1,0:T(8,128)S(1)}, f32[16,32,512]{2,1,0:T(8,128)}, u32[]{:S(2)}) copy-start(f32[16,32,512]{2,1,0:T(8,128)} %control_ref.1) | copy-start | bytes 3145732
  1.9 0.8 %copy-start.3 = (s32[32,512]{1,0:T(8,128)S(1)}, s32[32,512]{1,0:T(8,128)}, u32[]{:S(2)}) copy-start(s32[32,512]{1,0:T(8,128)} %mask_ref.1) | copy-start | bytes 196612
  2.7 0.8 %copy-start.5 = (f32[32,512]{1,0:T(8,128)S(1)}, f32[32,512]{1,0:T(8,128)}, u32[]{:S(2)}) copy-start(f32[32,512]{1,0:T(8,128)} %klon_hbm.1) | copy-start | bytes 196612
  3.5 0.8 %copy-start.6 = (f32[32,512]{1,0:T(8,128)S(1)}, f32[32,512]{1,0:T(8,128)}, u32[]{:S(2)}) copy-start(f32[32,512]{1,0:T(8,128)} %klat_hbm.1) | copy-start | bytes 196612
  4.4 0.7 %copy-start.7 = (f32[16,16]{1,0:T(8,128)S(1)}, f32[16,16]{1,0:T(8,128)}, u32[]{:S(2)}) copy-start(f32[16,16]{1,0:T(8,128)} %v_ref.1) | copy-start | bytes 3076
  5.1 9.0 %copy-start.13 = (s32[1,16]{1,0:T(1,128)S(1)}, s32[1,16]{1,0:T(1,128)}, u32[]{:S(2)}) copy-start(s32[1,16]{1,0:T(1,128)} %param.21) | copy-start | bytes 196
  5.1 21.7 %copy-start.2 = (f32[16,32,512]{2,1,0:T(8,128)S(1)}, f32[16,32,512]{2,1,0:T(8,128)}, u32[]{:S(2)}) copy-start(f32[16,32,512]{2,1,0:T(8,128)} %std_ref.1) | copy-start | bytes 3145732
  8.4 5.6 %copy-start.10 = (s32[1,16,8]{1,2,0:T(8,128)S(1)}, s32[1,16,8]{1,2,0:T(8,128)}, u32[]{:S(2)}) copy-start(s32[1,16,8]{1,2,0:T(8,128)} %param.17) | copy-start | bytes 1540
  8.5 20.1 %collective-permute-start = (f32[728,128]{1,0:T(8,128)}, f32[728,128]{1,0:T(8,128)S(1)}, u32[]{:S(2)}, u32[]{:S(2)}) collective-permute-start(f32[728,128]{1,0:T(8,128)} %get-tuple-element.11), channel_id=1, source_target_pairs={{0,1},{1,2},{2,3},{3,4},{4,5},{5,6},{6,7},{7,8},{8,9},{9,10},{10,1... | collective-permute-start | bytes 1118216 | tf_op jit(solution)/shard_map/ppermute | solution.py:435
  9.0 19.6 %collective-permute-start.1 = (f32[728,128]{1,0:T(8,128)}, f32[728,128]{1,0:T(8,128)S(1)}, u32[]{:S(2)}, u32[]{:S(2)}) collective-permute-start(f32[728,128]{1,0:T(8,128)} %get-tuple-element.12), channel_id=1, source_target_pairs={{1,0},{2,1},{3,2},{4,3},{5,4},{6,5},{7,6},{8,7},{9,8},{10,9},{11,1... | collective-permute-start | bytes 1118216 | tf_op jit(solution)/shard_map/ppermute | solution.py:436
  14.0 0.7 %copy-start.11 = (f32[1,16,8]{1,2,0:T(8,128)S(1)}, f32[1,16,8]{1,2,0:T(8,128)}, u32[]{:S(2)}) copy-start(f32[1,16,8]{1,2,0:T(8,128)} %param.20) | copy-start | bytes 1540
  14.0 0.7 %copy-start.12 = (f32[1,16,8]{1,2,0:T(8,128)S(1)}, f32[1,16,8]{1,2,0:T(8,128)}, u32[]{:S(2)}) copy-start(f32[1,16,8]{1,2,0:T(8,128)} %param.19) | copy-start | bytes 1540
  14.0 0.9 %copy-start.9 = (f32[1,16,8,128]{3,2,1,0:T(8,128)S(1)}, f32[1,16,8,128]{3,2,1,0:T(8,128)}, u32[]{:S(2)}) copy-start(f32[1,16,8,128]{3,2,1,0:T(8,128)} %param.18) | copy-start | bytes 196612
  26.3 0.8 %copy-start.4 = (s32[32,512]{1,0:T(8,128)S(1)}, s32[32,512]{1,0:T(8,128)}, u32[]{:S(2)}) copy-start(s32[32,512]{1,0:T(8,128)} %mask_ref.1) | copy-start | bytes 196612
  28.6 22.8 %copy-start.1 = (f32[16,32,512]{2,1,0:T(8,128)S(1)}, f32[16,32,512]{2,1,0:T(8,128)}, u32[]{:S(2)}) copy-start(f32[16,32,512]{2,1,0:T(8,128)} %control_ref.1) | copy-start | bytes 3145732
  36.3 15.0 %collective-permute-start.2 = (f32[136,128]{1,0:T(8,128)S(1)}, f32[136,128]{1,0:T(8,128)S(1)}, u32[]{:S(2)}, u32[]{:S(2)}) collective-permute-start(f32[136,128]{1,0:T(8,128)S(1)} %get-tuple-element.16.own_ref), channel_id=1, source_target_pairs={{0,1},{1,2},{2,3},{3,4},{4,5},{5,6},{6,7},{7,8},{8,9},{9,10},{10,1... | collective-permute-start | bytes 208904 | tf_op jit(solution)/shard_map/ppermute | solution.py:460
  36.3 15.0 %collective-permute-start.3 = (f32[136,128]{1,0:T(8,128)S(1)}, f32[136,128]{1,0:T(8,128)S(1)}, u32[]{:S(2)}, u32[]{:S(2)}) collective-permute-start(f32[136,128]{1,0:T(8,128)S(1)} %get-tuple-element.16.own_ref), channel_id=1, source_target_pairs={{1,0},{2,1},{3,2},{4,3},{5,4},{6,5},{7,6},{8,7},{9,8},{10,9},{11,1... | collective-permute-start | bytes 208904 | tf_op jit(solution)/shard_map/ppermute | solution.py:461
  40.8 3.6 %copy-start.8 = (f32[16,16]{1,0:T(8,128)S(1)}, f32[16,16]{1,0:T(8,128)}, u32[]{:S(2)}) copy-start(f32[16,16]{1,0:T(8,128)} %v_ref.1) | copy-start | bytes 3076
  40.8 9.9 %all-to-all-start.1 = ((f32[16,1,128]{2,1,0:T(1,128)}), f32[16,1,128]{2,1,0:T(1,128)S(1)}, u32[]{:S(2)}, u32[]{:S(2)}) async-start(f32[16,1,128]{2,1,0:T(1,128)} %bitcast.7), calls=%async_computation.1 | async-start | bytes 16384 | tf_op jit(solution)/shard_map/all_to_all | solution.py:462

commit v3 on v2

--- a/solution.py
+++ b/solution.py
@@ -10,7 +10,8 @@
 WIDE = 256
 F32 = jnp.float32
 BF16 = jnp.bfloat16
-VMEM_LIMIT = 40 * 1024 * 1024
+TIERS = ((0, 4), (4, PASSES))
+VMEM_LIMIT = 24 * 1024 * 1024
 
 VMEM_SPEC = pl.BlockSpec(memory_space=pltpu.VMEM)
 SMEM_SPEC = pl.BlockSpec(memory_space=pltpu.SMEM)
@@ -63,15 +64,16 @@
     return tuple(out)
 
 
-def mixing_matrix_back(vertical_t):
-    levels = vertical_t.shape[0]
+def mixing_matrix_back(vertical):
+    levels = vertical.shape[0]
     group = WIDE // levels
     spread = onehot(iota((levels, WIDE), 1) % levels == iota((levels, WIDE), 0))
     repeat = onehot(iota((WIDE, levels), 0) // group == iota((WIDE, levels), 1))
     keep = iota((WIDE, WIDE), 0) % group == iota((WIDE, WIDE), 1) // levels
     out = []
-    for part in split(vertical_t):
-        rows = dot(part, spread).astype(BF16)
+    for part in split(vertical):
+        rows = lax.dot_general(part, spread, (((0,), (0,)), ((), ())), preferred_element_type=F32)
+        rows = rows.astype(BF16)
         out.append(jnp.where(keep, dot(repeat, rows), F32(0.0)).astype(BF16))
     return tuple(out)
 
@@ -103,18 +105,7 @@
     return tuple(dot(part, matrix).astype(BF16) for part in x)
 
 
-def head_kernel(
-    v_ref, control_hbm, klon_hbm, klat_hbm, mask_hbm, mixed_ref, faces_ref, left_ref, right_ref,
-    control_ref, klon_ref, klat_ref, mask_ref, sems,
-):
-    copies = [
-        pltpu.make_async_copy(source, target, sems.at[k])
-        for k, (source, target) in enumerate(
-            ((mask_hbm, mask_ref), (klon_hbm, klon_ref), (klat_hbm, klat_ref), (control_hbm, control_ref))
-        )
-    ]
-    for copy in copies:
-        copy.start()
+def head_kernel(v_ref, control_ref, klon_ref, klat_ref, mask_ref, mixed_ref, faces_ref, left_ref, right_ref):
     levels, cols, lat = control_ref.shape
     parts = lat // STEN
     group = WIDE // levels
@@ -122,8 +113,6 @@
     edge = halo * levels
     place = deinterleave(lat)
     matrix = mixing_matrix(v_ref[...])
-    for copy in copies[:3]:
-        copy.wait()
     wet = mask_ref[...].astype(F32)
     east = jnp.where(iota((cols, lat), 0) == cols - 1, F32(1.0), pltpu.roll(wet, cols - 1, 0))
     north = jnp.where(iota((cols, lat), 1) == lat - 1, F32(0.0), pltpu.roll(wet, lat - 1, 1))
@@ -131,7 +120,6 @@
         held = sum(dot(piece, place) for piece in (split3(face) if k < 2 else (face.astype(BF16),)))
         for q in range(parts):
             faces_ref[k * parts + q] = held[:, q * STEN : (q + 1) * STEN]
-    copies[3].wait()
     for g in range(cols // group):
         x = control_ref[:, g * group : (g + 1) * group, :].reshape(WIDE, lat)
         y = product(matrix, move(split(x), place))
@@ -232,12 +220,14 @@
 def diffuse(a_ref, b_ref, lon_ref, lat_ref, levels):
     width = a_ref.shape[1] // levels
 
-    def pair(turn, carry):
-        one_pass(a_ref, b_ref, lon_ref, lat_ref, levels, 1, width - 1)
-        one_pass(b_ref, a_ref, lon_ref, lat_ref, levels, 2, width - 2)
-        return carry
-
-    lax.fori_loop(0, PASSES // 2, pair, 0)
+    for first, last in TIERS:
+
+        def pair(turn, carry):
+            one_pass(a_ref, b_ref, lon_ref, lat_ref, levels, first + 1, width - first - 1)
+            one_pass(b_ref, a_ref, lon_ref, lat_ref, levels, first + 2, width - first - 2)
+            return carry
+
+        lax.fori_loop(first // 2, last // 2, pair, 0)
 
 
 def block_place(index, cols, parts):
@@ -248,7 +238,7 @@
     )
 
 
-def weights_kernel(index_ref, recv_ref, std_ref, mask_ref, out_ref, held_ref, pick_ref, std_rows, wet_rows):
+def weights_kernel(place_ref, recv_ref, std_ref, mask_ref, out_ref, held_ref, pick_ref, std_rows, wet_rows):
     owners, rows, _ = recv_ref.shape
     slots = rows // 2
     total = owners * slots
@@ -264,7 +254,7 @@
     def pick(o, carry):
         for k in range(slots):
             slot = o * slots + k
-            level, column, seg = block_place(index_ref[slot], cols, parts)
+            level, column, seg = block_place(place_ref[0, slot], cols, parts)
             value = std_rows[pl.ds((level * parts + seg) * cols + column, 1), :]
             wet = wet_rows[pl.ds(seg * cols + column, 1), :]
             pick_ref[pl.ds(slot, 1), :] = value * wet
@@ -295,7 +285,7 @@
 
 
 def first_kernel(
-    index_ref, mixed_ref, from_left, from_right, faces_ref, recv_ref, ws_ref, held_ref,
+    place_ref, mixed_ref, from_left, from_right, faces_ref, recv_ref, ws_ref, held_ref,
     spread_ref, departure_ref, a_ref, b_ref, lon_ref, lat_ref, pick_ref,
 ):
     halo = PASSES
@@ -315,8 +305,7 @@
     def pick(o, carry):
         for k in range(slots):
             slot = o * slots + k
-            level, column, _ = block_place(index_ref[slot], cols, parts)
-            row = edge + column * levels + level
+            row = place_ref[1, slot]
             for q in range(parts):
                 pick_ref[q, pl.ds(slot, 1), :] = a_ref[q, pl.ds(row, 1), :]
         return carry
@@ -337,7 +326,7 @@
 
 
 def second_kernel(
-    vt_ref, control_ref, own_ref, left_ref, right_ref, faces_ref, from_left, from_right,
+    v_ref, control_ref, own_ref, left_ref, right_ref, faces_ref, from_left, from_right,
     out_ref, a_ref, b_ref, lon_ref, lat_ref,
 ):
     halo = PASSES
@@ -371,7 +360,7 @@
     scatter(left_ref, cols - halo, halo, halo // 2, 0)
     scatter(right_ref, 0, halo, halo // 2, halo + cols)
     diffuse(a_ref, b_ref, lon_ref, lat_ref, levels)
-    matrix = mixing_matrix_back(vt_ref[...])
+    matrix = mixing_matrix_back(v_ref[...])
     back = interleave(lat)
     group = WIDE // levels
     for g in range(cols // group):
@@ -382,13 +371,14 @@
         out_ref[:, part, :] = control_ref[:, part, :] + y
 
 
-def call(kernel, out_shape, specs, scratch=()):
+def call(kernel, out_shape, specs, scratch, flops, moved):
     return pl.pallas_call(
         kernel,
         out_shape=out_shape,
         in_specs=specs,
         out_specs=jax.tree.map(lambda _: VMEM_SPEC, out_shape),
         scratch_shapes=list(scratch),
+        cost_estimate=pl.CostEstimate(flops=flops, bytes_accessed=moved, transcendentals=0),
         compiler_params=pltpu.CompilerParams(vmem_limit_bytes=VMEM_LIMIT),
     )
 
@@ -407,6 +397,7 @@
     total = owners * slots
     halo = PASSES
     width = cols + 2 * halo
+    cells = width * levels * lat
     count = lax.axis_size("lon")
     to_right = [(i, (i + 1) % count) for i in range(count)]
     to_left = [((i + 1) % count, i) for i in range(count)]
@@ -417,6 +408,7 @@
     )
     meta = jnp.pad(meta, ((0, 0), (0, 0), (0, STEN - 4)))
     sent = jnp.concatenate([weights[0], meta], axis=1)
+    sent, matrix = lax.optimization_barrier((sent, vertical))
 
     message = parts * halo * (levels + 2) + parts
     message = -(-message // 8) * 8
@@ -426,17 +418,16 @@
             shape(parts, cols * levels, STEN), shape(3 * parts, cols, STEN),
             shape(message, STEN), shape(message, STEN),
         ),
-        [VMEM_SPEC] + [pl.BlockSpec(memory_space=pl.ANY)] * 4,
-        [
-            pltpu.VMEM((levels, cols, lat), F32), pltpu.VMEM((cols, lat), F32), pltpu.VMEM((cols, lat), F32),
-            pltpu.VMEM((cols, lat), jnp.int32), pltpu.SemaphoreType.DMA((4,)),
-        ],
-    )(vertical, control, kappa_lon, kappa_lat, sea_mask)
+        [VMEM_SPEC] * 5, [],
+        12 * cells * lat, 8 * 4 * cells,
+    )(matrix, control, kappa_lon, kappa_lat, sea_mask)
     from_left = lax.ppermute(edge_right, "lon", to_right)
     from_right = lax.ppermute(edge_left, "lon", to_left)
 
     recv = lax.all_to_all(sent, "lon", split_axis=0, concat_axis=0, tiled=True)
     index = recv[:, slots:, 2].reshape(total).astype(jnp.int32)
+    level, column, _ = block_place(index, cols, parts)
+    places = jnp.stack([index, (halo + column) * levels + level])
     ws, held = call(
         weights_kernel,
         (shape(total, STEN), shape(parts, total, STEN)),
@@ -445,7 +436,8 @@
             pltpu.VMEM((total, STEN), F32), pltpu.VMEM((levels * cols * parts, STEN), F32),
             pltpu.VMEM((cols * parts, STEN), F32),
         ],
-    )(index, recv, std_field, sea_mask)
+        6 * total * STEN * lat, 4 * 4 * cells,
+    )(places, recv, std_field, sea_mask)
 
     field = pltpu.VMEM((parts + 2, width * levels, STEN), F32)
     faces_held = [pltpu.VMEM((parts, width * 8, STEN), F32), pltpu.VMEM((parts + 1, width * 8, STEN), F32)]
@@ -455,15 +447,18 @@
         (shape(total + extra, STEN), shape(owners, STEN)),
         [SMEM_SPEC] + [VMEM_SPEC] * 7,
         [field, field, *faces_held, pltpu.VMEM((parts, total, STEN), F32)],
-    )(index, mixed, from_left, from_right, faces, recv, ws, held)
+        10 * PASSES * cells, 2 * PASSES * 4 * cells,
+    )(places, mixed, from_left, from_right, faces, recv, ws, held)
 
     spread_left = lax.ppermute(spread, "lon", to_right)
     spread_right = lax.ppermute(spread, "lon", to_left)
     mine = lax.all_to_all(departure[:, None, :], "lon", split_axis=0, concat_axis=0, tiled=True)
 
     gradient = call(
-        second_kernel, shape(levels, cols, lat), [VMEM_SPEC] * 8, [field, field, *faces_held]
-    )(vertical.T, control, spread, spread_left, spread_right, faces, from_left, from_right)
+        second_kernel, shape(levels, cols, lat), [VMEM_SPEC] * 8, [field, field, *faces_held],
+        10 * PASSES * cells, 2 * PASSES * 4 * cells,
+    )(vertical, control, spread, spread_left, spread_right, faces, from_left, from_right)
+    gradient, mine = lax.optimization_barrier((gradient, mine))
     return gradient, mine[:, 0, :slots][None]
 
 

time: 61.1 us -> 49.5 us (0.81)
  blocking collectives: 11.4 us -> 0 us
  starting transfers between devices: 13.6 us -> 20.9 us
  local copies, waits for them, and re-layouts: 6.42 us -> 3.48 us
  waiting for transfers between devices: 6.22 us -> 3.57 us
  Pallas kernels: 21.7 us -> 19.3 us
  other arithmetic: 0.44 us -> 1.1 us
    all_to_all x1 -> x0, blocking collectives: 11.4 us -> none  [local(): recv = lax.all_to_all(sent, 'lon', split_axis=0, concat_axis=0, tiled=True)]
    all_to_all x0 -> x1, starting transfers between devices: none -> 7.53 us  [local(): recv = lax.all_to_all(sent, 'lon', split_axis=0, concat_axis=0, tiled=True)]
    all_to_all x1, waiting for transfers between devices: 6.21 us -> 0.01 us  [local(): lax.all_to_all(departure[:, None, :], 'lon', split_axis=0, concat_axis=0,...]
    unnamed x30 -> x24, local copies, waits for them, and re-layouts: 6.19 us -> 2.56 us
    ppermute x1, waiting for transfers between devices: 0.01 us -> 3.56 us  [local(): from_left = lax.ppermute(edge_right, 'lon', to_right)]
    ppermute x1, starting transfers between devices: 4.44 us -> 1.22 us  [local(): spread_right = lax.ppermute(spread, 'lon', to_left)]
    ppermute x1, starting transfers between devices: 0.01 us -> 3.22 us  [local(): spread_left = lax.ppermute(spread, 'lon', to_right)]
    ppermute x1, starting transfers between devices: 5.06 us -> 4.04 us  [local(): from_right = lax.ppermute(edge_left, 'lon', to_left)]
  transfers between devices with their start and end apart: 5 -> 6, of which waited for: 1 -> 1; matrix products, arithmetic and copies ran while one was open for 2% -> 1% of each run, Pallas kernels for 2% -> 25%
where the time goes in v3:
time: 49.5 us; the launch traced here: 49.1 us
  starting transfers between devices  20.9 us (42%)
  Pallas kernels  19.3 us (39%)
  waiting for transfers between devices  3.57 us (7%)
  local copies, waits for them, and re-layouts  3.48 us (7%)
  other arithmetic  1.1 us (2%)
  between operations  0.79 us (2%)
    pallas_call x1, Pallas kernels, local(): call(second_kernel, shape(levels, cols, lat), [VMEM_SPEC] * 8, [field, fi...  8.32 us
    all_to_all x1, starting transfers between devices, local(): recv = lax.all_to_all(sent, 'lon', split_axis=0, concat_axis=0, tiled=True)  7.53 us
    pallas_call x1, Pallas kernels, local(): call(first_kernel, (shape(total + extra, STEN), shape(owners, STEN)), [SM...  6.82 us
    all_to_all x1, starting transfers between devices, local(): lax.all_to_all(departure[:, None, :], 'lon', split_axis=0, concat_axis=0,...  4.49 us
    ppermute x1, starting transfers between devices, local(): from_right = lax.ppermute(edge_left, 'lon', to_left)  4.04 us
    ppermute x1, waiting for transfers between devices, local(): from_left = lax.ppermute(edge_right, 'lon', to_right)  3.56 us
    ppermute x1, starting transfers between devices, local(): spread_left = lax.ppermute(spread, 'lon', to_right)  3.22 us
    pallas_call x1, Pallas kernels, local(): call(head_kernel, (shape(parts, cols * levels, STEN), shape(3 * parts, co...  2.7 us
  transfers between devices with their start and end apart: 6, of which 1 were waited for; matrix products, arithmetic and copies ran while one was open for 1% of the time, Pallas kernels for 25%

profile of v3, /device:TPU:0, one launch (start us, length us, event | category | flops | bytes accessed | tf_op | source)
XLA Modules:
  0.0 49.1 jit_solution(4910973483690090403)
XLA Ops:
  0.7 0.6 %copy-done.11 = s32[1,16]{1,0:T(1,128)S(1)} copy-done((s32[1,16]{1,0:T(1,128)S(1)}, s32[1,16]{1,0:T(1,128)}, u32[]{:S(2)}) %copy-start.11) | copy-done | bytes 88
  1.3 0.0 copy-done.8
  1.3 0.0 copy-done.9
  1.4 0.0 copy-done.10
  1.4 0.1 copy.21
  1.5 0.6 %copy-done.7 = f32[1,16,8,128]{3,2,1,0:T(8,128)S(1)} copy-done((f32[1,16,8,128]{3,2,1,0:T(8,128)S(1)}, f32[1,16,8,128]{3,2,1,0:T(8,128)}, u32[]{:S(2)}) %copy-start.7) | copy-done | bytes 65560
  2.1 0.7 %select_maximum_fusion = f32[16,16,128]{2,1,0:T(8,128)} fusion(f32[16,8,4]{2,1,0:T(8,128)S(1)} %copy.21, f32[16,8,128]{2,1,0:T(8,128)S(1)} %bitcast.11), kind=kLoop, calls=%fused_computation | loop fusion | flops 98304 | bytes 198656 | tf_op jit(solution)/shard_map/concatenate | solution.py:410
  2.8 7.5 %all-to-all-start = ((f32[16,16,128]{2,1,0:T(8,128)}), f32[16,16,128]{2,1,0:T(8,128)S(1)}, u32[]{:S(2)}, u32[]{:S(2)}) async-start(f32[16,16,128]{2,1,0:T(8,128)} %select_maximum_fusion), calls=%async_computation | async-start | bytes 262144 | tf_op jit(solution)/shard_map/all_to_all | solution.py:427
  10.3 0.0 copy-done.3
  10.3 0.0 copy-done.4
  10.3 0.0 copy-done.5
  10.4 0.0 copy-start.1
  10.4 1.2 %copy-done.1 = f32[16,32,512]{2,1,0:T(8,128)S(1)} copy-done((f32[16,32,512]{2,1,0:T(8,128)S(1)}, f32[16,32,512]{2,1,0:T(8,128)}, u32[]{:S(2)}) %copy-start.1) | copy-done | bytes 1048600
  11.6 2.7 %shard_map.122 = (f32[4,512,128]{2,1,0:T(8,128)S(1)}, f32[12,32,128]{2,1,0:T(8,128)S(1)}, f32[728,128]{1,0:T(8,128)}, f32[728,128]{1,0:T(8,128)}) custom-call(f32[16,16]{1,0:T(8,128)S(1)} %copy-done.4, f32[16,32,512]{2,1,0:T(8,128)S(1)} %copy-done.1, f32[32,512]{1,0:T(8,128)S(1)} %copy-done.5, f32[32,512]{1,0:T(8,128)S(1)} %copy-done.6, s32[32,512]{1,0:T(8,128)S(1)} %copy-done.3), custom_call_target="tpu_custom_call" | custom-call | flops 2617245696 | bytes 13631488 | tf_op jit(solution)/shard_map/pallas_call | solution.py:415
  14.3 0.4 collective-permute-start
  14.7 4.0 %collective-permute-start.1 = (f32[728,128]{1,0:T(8,128)}, f32[728,128]{1,0:T(8,128)S(1)}, u32[]{:S(2)}, u32[]{:S(2)}) collective-permute-start(f32[728,128]{1,0:T(8,128)} %get-tuple-element.18), channel_id=1, source_target_pairs={{1,0},{2,1},{3,2},{4,3},{5,4},{6,5},{7,6},{8,7},{9,8},{10,9},{11,1... | collective-permute-start | bytes 1118216 | tf_op jit(solution)/shard_map/ppermute | solution.py:425
  18.7 0.0 all-to-all-done.recv_ref
  18.8 0.4 fusion
  19.2 0.1 convert_element_type.46
  19.3 1.4 %shard_map.123 = (f32[128,128]{1,0:T(8,128)S(1)}, f32[4,128,128]{2,1,0:T(8,128)S(1)}) custom-call(s32[2,128]{1,0:T(2,128)S(1)} %pad_add_fusion.place_ref, f32[16,16,128]{2,1,0:T(8,128)S(1)} %all-to-all-done.recv_ref, f32[16,32,512]{2,1,0:T(8,128)S(1)} %copy-done, s32[32,512]{1,0:T(8,128)S(1)} %copy-done.3), custom_call_target="tpu_custom_call" | custom-call | flops 50331648 | bytes 6815744 | tf_op jit(solution)/shard_map/pallas_call | solution.py:431
  20.7 3.6 %collective-permute-done.from_left = f32[728,128]{1,0:T(8,128)S(1)} collective-permute-done((f32[728,128]{1,0:T(8,128)}, f32[728,128]{1,0:T(8,128)S(1)}, u32[]{:S(2)}, u32[]{:S(2)}) %collective-permute-start) | collective-permute-done | bytes 372768 | tf_op jit(solution)/shard_map/ppermute | solution.py:424
  24.3 0.0 collective-permute-done.1.from_right
  24.3 6.8 %shard_map.124 = (f32[136,128]{1,0:T(8,128)S(1)}, f32[16,128]{1,0:T(8,128)}) custom-call(s32[2,128]{1,0:T(2,128)S(1)} %pad_add_fusion.place_ref, f32[4,512,128]{2,1,0:T(8,128)S(1)} %get-tuple-element.16.mixed_ref, f32[728,128]{1,0:T(8,128)S(1)} %collective-permute-done.from_left, f32[728,128]{1,0:T(8,128)S(1)} %collective-permute-done.1.from_right, ...), custom_call_target="tpu_custom_call" | custom-call | flops 42598400 | bytes 34078720 | tf_op jit(solution)/shard_map/pallas_call | solution.py:445
  31.1 3.2 %collective-permute-start.2 = (f32[136,128]{1,0:T(8,128)S(1)}, f32[136,128]{1,0:T(8,128)S(1)}, u32[]{:S(2)}, u32[]{:S(2)}) collective-permute-start(f32[136,128]{1,0:T(8,128)S(1)} %get-tuple-element.22.own_ref), channel_id=1, source_target_pairs={{0,1},{1,2},{2,3},{3,4},{4,5},{5,6},{6,7},{7,8},{8,9},{9,10},{10,1... | collective-permute-start | bytes 208904 | tf_op jit(solution)/shard_map/ppermute | solution.py:453
  34.3 1.2 %collective-permute-start.3 = (f32[136,128]{1,0:T(8,128)S(1)}, f32[136,128]{1,0:T(8,128)S(1)}, u32[]{:S(2)}, u32[]{:S(2)}) collective-permute-start(f32[136,128]{1,0:T(8,128)S(1)} %get-tuple-element.22.own_ref), channel_id=1, source_target_pairs={{1,0},{2,1},{3,2},{4,3},{5,4},{6,5},{7,6},{8,7},{9,8},{10,9},{11,1... | collective-permute-start | bytes 208904 | tf_op jit(solution)/shard_map/ppermute | solution.py:454
  35.6 4.5 %all-to-all-start.1 = ((f32[16,1,128]{2,1,0:T(1,128)}), f32[16,1,128]{2,1,0:T(1,128)S(1)}, u32[]{:S(2)}, u32[]{:S(2)}) async-start(f32[16,1,128]{2,1,0:T(1,128)} %bitcast.6), calls=%async_computation.1 | async-start | bytes 16384 | tf_op jit(solution)/shard_map/all_to_all | solution.py:455
  40.1 0.0 collective-permute-done.2.left_ref
  40.1 0.0 collective-permute-done.3.right_ref
  40.1 8.3 %shard_map.125 = f32[16,32,512]{2,1,0:T(8,128)} custom-call(f32[16,16]{1,0:T(8,128)S(1)} %copy-done.4, f32[16,32,512]{2,1,0:T(8,128)S(1)} %copy-done.2, f32[136,128]{1,0:T(8,128)S(1)} %get-tuple-element.22.own_ref, f32[136,128]{1,0:T(8,128)S(1)} %collective-permute-done.2.left_ref, f32[136,128]{1,0:T(8,128)S(1)} %collective-permute-done.3.right_ref, ...), custom_call_target="tpu_custom_call" | custom-call | flops 42598400 | bytes 34078720 | tf_op jit(solution)/shard_map/pallas_call | solution.py:457
  48.4 0.0 all-to-all-done.1
  48.4 0.1 copy.23
  48.5 0.6 %slice_bitcast_fusion = f32[1,16,8]{1,2,0:T(8,128)} fusion(f32[16,1,128]{0,2,1:T(8,128)S(1)} %copy.23), kind=kLoop, calls=%fused_computation.5 | loop fusion | bytes 1024 | tf_op jit(solution)/shard_map/broadcast_in_dim;squeeze | solution.py:462
  (19 shorter events, 0.1 us)
Async XLA Ops:
  0.6 0.7 %copy-start.11 = (s32[1,16]{1,0:T(1,128)S(1)}, s32[1,16]{1,0:T(1,128)}, u32[]{:S(2)}) copy-start(s32[1,16]{1,0:T(1,128)} %param.21) | copy-start | bytes 196
  0.6 0.7 %copy-start.8 = (s32[1,16,8]{1,2,0:T(8,128)S(1)}, s32[1,16,8]{1,2,0:T(8,128)}, u32[]{:S(2)}) copy-start(s32[1,16,8]{1,2,0:T(8,128)} %param.17) | copy-start | bytes 1540
  0.7 0.7 %copy-start.9 = (f32[1,16,8]{1,2,0:T(8,128)S(1)}, f32[1,16,8]{1,2,0:T(8,128)}, u32[]{:S(2)}) copy-start(f32[1,16,8]{1,2,0:T(8,128)} %param.20) | copy-start | bytes 1540
  0.7 0.7 %copy-start.10 = (f32[1,16,8]{1,2,0:T(8,128)S(1)}, f32[1,16,8]{1,2,0:T(8,128)}, u32[]{:S(2)}) copy-start(f32[1,16,8]{1,2,0:T(8,128)} %param.19) | copy-start | bytes 1540
  1.3 0.8 %copy-start.7 = (f32[1,16,8,128]{3,2,1,0:T(8,128)S(1)}, f32[1,16,8,128]{3,2,1,0:T(8,128)}, u32[]{:S(2)}) copy-start(f32[1,16,8,128]{3,2,1,0:T(8,128)} %param.18) | copy-start | bytes 196612
  2.8 7.5 %copy-start.3 = (s32[32,512]{1,0:T(8,128)S(1)}, s32[32,512]{1,0:T(8,128)}, u32[]{:S(2)}) copy-start(s32[32,512]{1,0:T(8,128)} %mask_ref.3) | copy-start | bytes 196612
  2.8 7.6 %copy-start.4 = (f32[16,16]{1,0:T(8,128)S(1)}, f32[16,16]{1,0:T(8,128)}, u32[]{:S(2)}) copy-start(f32[16,16]{1,0:T(8,128)} %v_ref.2) | copy-start | bytes 3076
  2.8 7.6 %copy-start.5 = (f32[32,512]{1,0:T(8,128)S(1)}, f32[32,512]{1,0:T(8,128)}, u32[]{:S(2)}) copy-start(f32[32,512]{1,0:T(8,128)} %klon_ref.1) | copy-start | bytes 196612
  2.8 7.6 %copy-start.6 = (f32[32,512]{1,0:T(8,128)S(1)}, f32[32,512]{1,0:T(8,128)}, u32[]{:S(2)}) copy-start(f32[32,512]{1,0:T(8,128)} %klat_ref.1) | copy-start | bytes 196612
  2.8 16.0 %all-to-all-start = ((f32[16,16,128]{2,1,0:T(8,128)}), f32[16,16,128]{2,1,0:T(8,128)S(1)}, u32[]{:S(2)}, u32[]{:S(2)}) async-start(f32[16,16,128]{2,1,0:T(8,128)} %select_maximum_fusion), calls=%async_computation | async-start | bytes 262144 | tf_op jit(solution)/shard_map/all_to_all | solution.py:427
  10.4 1.2 %copy-start.1 = (f32[16,32,512]{2,1,0:T(8,128)S(1)}, f32[16,32,512]{2,1,0:T(8,128)}, u32[]{:S(2)}) copy-start(f32[16,32,512]{2,1,0:T(8,128)} %control_ref.3) | copy-start | bytes 3145732
  11.6 7.7 %copy-start = (f32[16,32,512]{2,1,0:T(8,128)S(1)}, f32[16,32,512]{2,1,0:T(8,128)}, u32[]{:S(2)}) copy-start(f32[16,32,512]{2,1,0:T(8,128)} %std_ref.1) | copy-start | bytes 3145732
  14.3 10.0 %collective-permute-start = (f32[728,128]{1,0:T(8,128)}, f32[728,128]{1,0:T(8,128)S(1)}, u32[]{:S(2)}, u32[]{:S(2)}) collective-permute-start(f32[728,128]{1,0:T(8,128)} %get-tuple-element.17), channel_id=1, source_target_pairs={{0,1},{1,2},{2,3},{3,4},{4,5},{5,6},{6,7},{7,8},{8,9},{9,10},{10,1... | collective-permute-start | bytes 1118216 | tf_op jit(solution)/shard_map/ppermute | solution.py:424
  14.7 9.6 %collective-permute-start.1 = (f32[728,128]{1,0:T(8,128)}, f32[728,128]{1,0:T(8,128)S(1)}, u32[]{:S(2)}, u32[]{:S(2)}) collective-permute-start(f32[728,128]{1,0:T(8,128)} %get-tuple-element.18), channel_id=1, source_target_pairs={{1,0},{2,1},{3,2},{4,3},{5,4},{6,5},{7,6},{8,7},{9,8},{10,9},{11,1... | collective-permute-start | bytes 1118216 | tf_op jit(solution)/shard_map/ppermute | solution.py:425
  24.3 15.8 %copy-start.2 = (f32[16,32,512]{2,1,0:T(8,128)S(1)}, f32[16,32,512]{2,1,0:T(8,128)}, u32[]{:S(2)}) copy-start(f32[16,32,512]{2,1,0:T(8,128)} %control_ref.3) | copy-start | bytes 3145732
  31.1 8.9 %collective-permute-start.2 = (f32[136,128]{1,0:T(8,128)S(1)}, f32[136,128]{1,0:T(8,128)S(1)}, u32[]{:S(2)}, u32[]{:S(2)}) collective-permute-start(f32[136,128]{1,0:T(8,128)S(1)} %get-tuple-element.22.own_ref), channel_id=1, source_target_pairs={{0,1},{1,2},{2,3},{3,4},{4,5},{5,6},{6,7},{7,8},{8,9},{9,10},{10,1... | collective-permute-start | bytes 208904 | tf_op jit(solution)/shard_map/ppermute | solution.py:453
  34.3 5.7 %collective-permute-start.3 = (f32[136,128]{1,0:T(8,128)S(1)}, f32[136,128]{1,0:T(8,128)S(1)}, u32[]{:S(2)}, u32[]{:S(2)}) collective-permute-start(f32[136,128]{1,0:T(8,128)S(1)} %get-tuple-element.22.own_ref), channel_id=1, source_target_pairs={{1,0},{2,1},{3,2},{4,3},{5,4},{6,5},{7,6},{8,7},{9,8},{10,9},{11,1... | collective-permute-start | bytes 208904 | tf_op jit(solution)/shard_map/ppermute | solution.py:454
  35.6 12.8 %all-to-all-start.1 = ((f32[16,1,128]{2,1,0:T(1,128)}), f32[16,1,128]{2,1,0:T(1,128)S(1)}, u32[]{:S(2)}, u32[]{:S(2)}) async-start(f32[16,1,128]{2,1,0:T(1,128)} %bitcast.6), calls=%async_computation.1 | async-start | bytes 16384 | tf_op jit(solution)/shard_map/all_to_all | solution.py:455

commit v4 on v3

--- a/solution.py
+++ b/solution.py
@@ -10,6 +10,7 @@
 WIDE = 256
 F32 = jnp.float32
 BF16 = jnp.bfloat16
+HEAD_VMEM = 52 * 1024 * 1024
 TIERS = ((0, 4), (4, PASSES))
 VMEM_LIMIT = 24 * 1024 * 1024
 
@@ -105,21 +106,36 @@
     return tuple(dot(part, matrix).astype(BF16) for part in x)
 
 
-def head_kernel(v_ref, control_ref, klon_ref, klat_ref, mask_ref, mixed_ref, faces_ref, left_ref, right_ref):
+def unpack_meta(recv_ref, slots, field):
+    owners = recv_ref.shape[0]
+    total = owners * slots
+    rows = jnp.broadcast_to(recv_ref[:, slots : slots + 1, :], (owners, slots, STEN)).reshape(total, STEN)
+    wanted = (iota((total, STEN), 0) & (slots - 1)) + field * slots
+    return jnp.sum(jnp.where(iota((total, STEN), 1) == wanted, rows, F32(0.0)), axis=1, keepdims=True)
+
+
+def head_kernel(
+    stack_ref, control_hbm, mixed_ref, faces_ref, left_ref, right_ref, control_ref, sem,
+):
+    copy = pltpu.make_async_copy(control_hbm, control_ref, sem)
+    copy.start()
     levels, cols, lat = control_ref.shape
     parts = lat // STEN
     group = WIDE // levels
     halo = PASSES
     edge = halo * levels
     place = deinterleave(lat)
-    matrix = mixing_matrix(v_ref[...])
-    wet = mask_ref[...].astype(F32)
+    matrix = mixing_matrix(stack_ref[3 * cols : 3 * cols + levels, 0:levels])
+    wet = stack_ref[2 * cols : 3 * cols, :]
     east = jnp.where(iota((cols, lat), 0) == cols - 1, F32(1.0), pltpu.roll(wet, cols - 1, 0))
     north = jnp.where(iota((cols, lat), 1) == lat - 1, F32(0.0), pltpu.roll(wet, lat - 1, 1))
-    for k, face in enumerate((klon_ref[...] * wet * east, klat_ref[...] * wet * north, wet)):
+    for k, face in enumerate(
+        (stack_ref[0:cols, :] * wet * east, stack_ref[cols : 2 * cols, :] * wet * north, wet)
+    ):
         held = sum(dot(piece, place) for piece in (split3(face) if k < 2 else (face.astype(BF16),)))
         for q in range(parts):
             faces_ref[k * parts + q] = held[:, q * STEN : (q + 1) * STEN]
+    copy.wait()
     for g in range(cols // group):
         x = control_ref[:, g * group : (g + 1) * group, :].reshape(WIDE, lat)
         y = product(matrix, move(split(x), place))
@@ -184,21 +200,21 @@
     add_ghosts(ref, first, values)
 
 
-def one_pass(src, dst, lon_ref, lat_ref, levels, low, high):
+def column_steps(src, dst, lon_ref, lat_ref, levels, low, high, step=0, face=0):
     parts = lon_ref.shape[0]
     halves = range(levels // 8)
 
     def load(k, c, h):
         return src[k, c * levels + 8 * h : c * levels + 8 * h + 8, :]
 
-    def face(ref, k, c):
-        return ref[k, 8 * c : 8 * c + 8, :]
+    def rate(ref, k, c):
+        return ref[k, pl.ds(pl.multiple_of(8 * (c + face), 8), 8), :]
 
     here = [[load(q, low, h) for q in range(parts)] for h in halves]
-    west = [[face(lon_ref, q, low - 1) * (here[h][q] - load(q, low - 1, h)) for q in range(parts)] for h in halves]
+    west = [[rate(lon_ref, q, low - 1) * (here[h][q] - load(q, low - 1, h)) for q in range(parts)] for h in halves]
     for c in range(low, high):
-        lon = [face(lon_ref, q, c) for q in range(parts)]
-        lat = [face(lat_ref, q, c) for q in range(parts + 1)]
+        lon = [rate(lon_ref, q, c) for q in range(parts)]
+        lat = [rate(lat_ref, q, c) for q in range(parts + 1)]
         for h in halves:
             line = here[h]
             east = [load(q, c + 1, h) for q in range(parts)]
@@ -210,24 +226,54 @@
                 line[q] + (flux_east[q] - west[h][q]) + (flux_north[q + 1] - flux_north[q])
                 for q in range(parts)
             ]
-            first = c * levels + 8 * h
+            first = (c + step) * levels + 8 * h
             for q in range(parts):
                 dst[q, first : first + 8, :] = out[q]
             add_ghosts(dst, first, out)
             here[h], west[h] = east, flux_east
 
 
-def diffuse(a_ref, b_ref, lon_ref, lat_ref, levels):
+def diffuse(a_ref, b_ref, lon_ref, lat_ref, levels, before_pass=None):
     width = a_ref.shape[1] // levels
 
     for first, last in TIERS:
 
         def pair(turn, carry):
-            one_pass(a_ref, b_ref, lon_ref, lat_ref, levels, first + 1, width - first - 1)
-            one_pass(b_ref, a_ref, lon_ref, lat_ref, levels, first + 2, width - first - 2)
+            for k, (src, dst) in enumerate(((a_ref, b_ref), (b_ref, a_ref))):
+                if before_pass is not None:
+                    before_pass(2 * turn + k, src)
+                column_steps(src, dst, lon_ref, lat_ref, levels, first + 1 + k, width - first - 1 - k)
             return carry
 
         lax.fori_loop(first // 2, last // 2, pair, 0)
+
+
+def inner_kernel(mixed_ref, faces_ref, inner_ref, strips_ref, a_ref, b_ref, lon_ref, lat_ref):
+    parts, own_rows, _ = mixed_ref.shape
+    cols = faces_ref.shape[1]
+    levels = own_rows // cols
+    shape = (8, STEN)
+    for c in range(cols):
+        rows = slice(8 * c, 8 * c + 8)
+        for q in range(parts):
+            lat_row = faces_ref[parts + q, c : c + 1, :]
+            lon_ref[q, rows, :] = jnp.broadcast_to(faces_ref[q, c : c + 1, :], shape)
+            lat_ref[q, rows, :] = jnp.broadcast_to(lat_row, shape)
+            if q == parts - 1:
+                lat_ref[parts, rows, :] = jnp.broadcast_to(pltpu.roll(lat_row, 1, 1), shape)
+    fill(a_ref, 0, [mixed_ref[q] for q in range(parts)])
+
+    def save(turn, src):
+        for side, (line, other) in enumerate(((turn, turn + 1), (cols - 1 - turn, cols - 2 - turn))):
+            line = pl.ds(pl.multiple_of(line * levels, levels), levels)
+            other = pl.ds(pl.multiple_of(other * levels, levels), levels)
+            for q in range(parts):
+                strips_ref[turn, side, q] = src[q, line, :]
+                strips_ref[turn, side, parts + q] = src[q, other, :]
+
+    diffuse(a_ref, b_ref, lon_ref, lat_ref, levels, save)
+    for q in range(parts):
+        inner_ref[q] = a_ref[q, PASSES * levels : (cols - PASSES) * levels, :]
 
 
 def block_place(index, cols, parts):
@@ -264,10 +310,10 @@
     ws = recv_ref[:, 0:slots, :].reshape(total, STEN) * pick_ref[...]
     out_ref[...] = ws
     place = spread_block(lat)
+    segs = unpack_meta(recv_ref, slots, 2).astype(jnp.int32) & (parts - 1)
     for j in range(total // STEN):
         part = slice(j * STEN, (j + 1) * STEN)
-        index = recv_ref[j * (STEN // slots) : (j + 1) * (STEN // slots), slots:, :].reshape(STEN, STEN)
-        seg = index[:, 2:3].astype(jnp.int32) & (parts - 1)
+        seg = segs[part]
         held = sum(dot(piece, place) for piece in split3(ws[part]))
         held = jnp.where(lane_segment(STEN, lat) == seg, held, F32(0.0))
         for q in range(parts):
@@ -284,43 +330,60 @@
     return jnp.sum(jnp.where(eye, row, F32(0.0)), axis=1, keepdims=True)
 
 
-def first_kernel(
-    place_ref, mixed_ref, from_left, from_right, faces_ref, recv_ref, ws_ref, held_ref,
-    spread_ref, departure_ref, a_ref, b_ref, lon_ref, lat_ref, pick_ref,
+def edge_kernel(
+    place_ref, inner_ref, strips_ref, from_left, from_right, faces_ref, recv_ref, ws_ref, held_ref,
+    spread_ref, departure_ref, rows_ref, left_a, left_b, right_a, right_b, lon_ref, lat_ref, pick_ref,
 ):
     halo = PASSES
-    parts, own_rows, _ = mixed_ref.shape
+    levels = strips_ref.shape[3]
+    parts = inner_ref.shape[0]
     owners, rows, _ = recv_ref.shape
     cols = faces_ref.shape[1]
-    levels = own_rows // cols
     slots = rows // 2
     total = owners * slots
     edge = halo * levels
     build_faces(faces_ref, from_left, from_right, lon_ref, lat_ref, levels)
-    fill(a_ref, 0, [from_left[q * edge : (q + 1) * edge, :] for q in range(parts)])
-    fill(a_ref, edge, [mixed_ref[q] for q in range(parts)])
-    fill(a_ref, edge + own_rows, [from_right[q * edge : (q + 1) * edge, :] for q in range(parts)])
-    diffuse(a_ref, b_ref, lon_ref, lat_ref, levels)
+    fill(left_a, 0, [from_left[q * edge : (q + 1) * edge, :] for q in range(parts)])
+    fill(right_a, 2 * levels, [from_right[q * edge : (q + 1) * edge, :] for q in range(parts)])
+
+    def pair(turn, carry):
+        for k, (left, left_to, right, right_to) in enumerate(
+            ((left_a, left_b, right_a, right_b), (left_b, left_a, right_b, right_a))
+        ):
+            now = 2 * turn + k
+            for side, ref, line, other in ((0, left, halo, halo + 1), (1, right, 1, 0)):
+                fill(ref, line * levels, [strips_ref[now, side, q] for q in range(parts)])
+                for q in range(parts):
+                    ref[q, other * levels : (other + 1) * levels, :] = strips_ref[now, side, parts + q]
+            column_steps(left, left_to, lon_ref, lat_ref, levels, 1, halo + 1, -1, now)
+            column_steps(right, right_to, lon_ref, lat_ref, levels, 1, halo + 1, 1, halo + cols - 2 - now)
+        return carry
+
+    lax.fori_loop(0, PASSES // 2, pair, 0)
+    for q in range(parts):
+        rows_ref[q, 0:edge, :] = left_a[q, 0:edge, :]
+        rows_ref[q, edge : cols * levels - edge, :] = inner_ref[q]
+        rows_ref[q, cols * levels - edge :, :] = right_a[q, 2 * levels : 2 * levels + edge, :]
 
     def pick(o, carry):
         for k in range(slots):
             slot = o * slots + k
             row = place_ref[1, slot]
             for q in range(parts):
-                pick_ref[q, pl.ds(slot, 1), :] = a_ref[q, pl.ds(row, 1), :]
+                pick_ref[q, pl.ds(slot, 1), :] = rows_ref[q, pl.ds(row, 1), :]
         return carry
 
     lax.fori_loop(0, owners, pick, 0)
-    meta = recv_ref[:, slots:, :].reshape(total, STEN)
+    value, rinv, index, valid = (unpack_meta(recv_ref, slots, field) for field in range(4))
     evolved = sum(pick_ref[q] * held_ref[q] for q in range(parts))
     evolved = jnp.sum(evolved, axis=1, keepdims=True)
-    departure = jnp.where(meta[:, 3:4] > 0.5, evolved - meta[:, 0:1], F32(0.0))
-    scaled = meta[:, 1:2] * departure
+    departure = jnp.where(valid > 0.5, evolved - value, F32(0.0))
+    scaled = rinv * departure
     spread_ref[0:total, :] = scaled * ws_ref[...]
     spread_ref[total:, :] = jnp.zeros((spread_ref.shape[0] - total, STEN), F32)
     for j in range(total // STEN):
         part = slice(j * STEN, (j + 1) * STEN)
-        spread_ref[total + j : total + j + 1, :] = to_row(meta[part, 2:3])
+        spread_ref[total + j : total + j + 1, :] = to_row(index[part])
     lanes = jnp.where(iota((total, STEN), 1) == (iota((total, STEN), 0) & (slots - 1)), departure, F32(0.0))
     departure_ref[...] = jnp.sum(lanes.reshape(owners, slots, STEN), axis=1)
 
@@ -371,7 +434,7 @@
         out_ref[:, part, :] = control_ref[:, part, :] + y
 
 
-def call(kernel, out_shape, specs, scratch, flops, moved):
+def call(kernel, out_shape, specs, scratch, flops, moved, limit=VMEM_LIMIT):
     return pl.pallas_call(
         kernel,
         out_shape=out_shape,
@@ -379,7 +442,7 @@
         out_specs=jax.tree.map(lambda _: VMEM_SPEC, out_shape),
         scratch_shapes=list(scratch),
         cost_estimate=pl.CostEstimate(flops=flops, bytes_accessed=moved, transcendentals=0),
-        compiler_params=pltpu.CompilerParams(vmem_limit_bytes=VMEM_LIMIT),
+        compiler_params=pltpu.CompilerParams(vmem_limit_bytes=limit),
     )
 
 
@@ -402,32 +465,34 @@
     to_right = [(i, (i + 1) % count) for i in range(count)]
     to_left = [((i + 1) % count, i) for i in range(count)]
 
-    valid = jnp.arange(slots, dtype=jnp.int32)[None, :] < obs_count[0][:, None]
-    meta = jnp.stack(
-        [obs_value[0], obs_rinv[0], block_index[0].astype(F32), valid.astype(F32)], axis=-1
-    )
-    meta = jnp.pad(meta, ((0, 0), (0, 0), (0, STEN - 4)))
-    sent = jnp.concatenate([weights[0], meta], axis=1)
-    sent, matrix = lax.optimization_barrier((sent, vertical))
-
     message = parts * halo * (levels + 2) + parts
     message = -(-message // 8) * 8
+    valid = jnp.arange(slots, dtype=jnp.int32)[None, :] < obs_count[0][:, None]
+    meta = jnp.concatenate([obs_value[0], obs_rinv[0], block_index[0].astype(F32), valid.astype(F32)], axis=1)
+    meta = jnp.pad(meta, ((0, 0), (0, STEN - 4 * slots)))
+    meta = jnp.broadcast_to(meta[:, None, :], (owners, slots, STEN))
+    sent = jnp.concatenate([weights[0], meta], axis=1)
+    stack = jnp.concatenate(
+        [kappa_lon, kappa_lat, sea_mask.astype(F32), jnp.pad(vertical, ((0, 0), (0, lat - levels)))]
+    )
+    sent, stack = lax.optimization_barrier((sent, stack))
     mixed, faces, edge_left, edge_right = call(
         head_kernel,
         (
             shape(parts, cols * levels, STEN), shape(3 * parts, cols, STEN),
             shape(message, STEN), shape(message, STEN),
         ),
-        [VMEM_SPEC] * 5, [],
-        12 * cells * lat, 8 * 4 * cells,
-    )(matrix, control, kappa_lon, kappa_lat, sea_mask)
+        [VMEM_SPEC, pl.BlockSpec(memory_space=pltpu.HBM)],
+        [pltpu.VMEM((levels, cols, lat), F32), pltpu.SemaphoreType.DMA(())],
+        12 * cells * lat, 8 * 4 * cells, HEAD_VMEM,
+    )(stack, control)
     from_left = lax.ppermute(edge_right, "lon", to_right)
     from_right = lax.ppermute(edge_left, "lon", to_left)
 
     recv = lax.all_to_all(sent, "lon", split_axis=0, concat_axis=0, tiled=True)
-    index = recv[:, slots:, 2].reshape(total).astype(jnp.int32)
+    index = recv[:, slots, 2 * slots : 3 * slots].reshape(total).astype(jnp.int32)
     level, column, _ = block_place(index, cols, parts)
-    places = jnp.stack([index, (halo + column) * levels + level])
+    places = jnp.stack([index, column * levels + level])
     ws, held = call(
         weights_kernel,
         (shape(total, STEN), shape(parts, total, STEN)),
@@ -442,13 +507,28 @@
     field = pltpu.VMEM((parts + 2, width * levels, STEN), F32)
     faces_held = [pltpu.VMEM((parts, width * 8, STEN), F32), pltpu.VMEM((parts + 1, width * 8, STEN), F32)]
     extra = -(-total // (8 * STEN)) * 8
+    inside = pltpu.VMEM((parts + 2, cols * levels, STEN), F32)
+    wedge = pltpu.VMEM((parts + 2, (halo + 2) * levels, STEN), F32)
+    inner, strips = call(
+        inner_kernel,
+        (shape(parts, (cols - 2 * halo) * levels, STEN), shape(PASSES, 2, 2 * parts, levels, STEN)),
+        [VMEM_SPEC] * 2,
+        [
+            inside, inside,
+            pltpu.VMEM((parts, cols * 8, STEN), F32), pltpu.VMEM((parts + 1, cols * 8, STEN), F32),
+        ],
+        5 * PASSES * cells, PASSES * 4 * cells,
+    )(mixed, faces)
     spread, departure = call(
-        first_kernel,
+        edge_kernel,
         (shape(total + extra, STEN), shape(owners, STEN)),
-        [SMEM_SPEC] + [VMEM_SPEC] * 7,
-        [field, field, *faces_held, pltpu.VMEM((parts, total, STEN), F32)],
-        10 * PASSES * cells, 2 * PASSES * 4 * cells,
-    )(places, mixed, from_left, from_right, faces, recv, ws, held)
+        [SMEM_SPEC] + [VMEM_SPEC] * 8,
+        [
+            pltpu.VMEM((parts, cols * levels, STEN), F32), wedge, wedge, wedge, wedge, *faces_held,
+            pltpu.VMEM((parts, total, STEN), F32),
+        ],
+        5 * PASSES * cells, PASSES * 4 * cells,
+    )(places, inner, strips, from_left, from_right, faces, recv, ws, held)
 
     spread_left = lax.ppermute(spread, "lon", to_right)
     spread_right = lax.ppermute(spread, "lon", to_left)

time: 49.5 us -> 50.8 us (1.026)
  other arithmetic: 1.1 us -> 5.43 us
  waiting for transfers between devices: 3.57 us -> 0.02 us
  Pallas kernels: 19.3 us -> 21.3 us
  starting transfers between devices: 20.9 us -> 19.8 us
  local copies, waits for them, and re-layouts: 3.48 us -> 2.86 us
    ppermute x1, waiting for transfers between devices: 3.56 us -> 0.01 us  [local(): from_left = lax.ppermute(edge_right, 'lon', to_right)]
    concatenate x0 -> x2, other arithmetic: none -> 1.61 us  [the longest x1 0.9 us: local(): jnp.concatenate([kappa_lon, kappa_lat, sea_mask.astype(F32), jnp.pad(vert...]
    ppermute x1, starting transfers between devices: 1.22 us -> 2.35 us  [local(): spread_right = lax.ppermute(spread, 'lon', to_left)]
    ppermute x1, starting transfers between devices: 3.22 us -> 2.09 us  [local(): spread_left = lax.ppermute(spread, 'lon', to_right)]
    pallas_call x1, Pallas kernels: 2.7 us -> 3.81 us  [local(): call(head_kernel, (shape(parts, cols * levels, STEN), shape(3 * parts, co...]
    all_to_all x1, starting transfers between devices: 4.49 us -> 3.43 us  [local(): lax.all_to_all(departure[:, None, :], 'lon', split_axis=0, concat_axis=0,...]
    pallas_call x1 -> x2, Pallas kernels: 6.82 us -> 7.79 us  [the longest x1 4.84 us: local(): call(edge_kernel, (shape(total + extra, STEN), shape(owners, STEN)), [SME...]
    concatenate x1, other arithmetic: 0.65 us -> 1.5 us  [local(): sent = jnp.concatenate([weights[0], meta], axis=1)]
  transfers between devices with their start and end apart: 6 -> 6, of which waited for: 1 -> 0; matrix products, arithmetic and copies ran while one was open for 1% -> 0% of each run, Pallas kernels for 25% -> 33%
where the time goes in v4:
time: 50.8 us; the launch traced here: 50.3 us
  Pallas kernels  21.3 us (42%)
  starting transfers between devices  19.8 us (39%)
  other arithmetic  5.43 us (11%)
  local copies, waits for them, and re-layouts  2.86 us (6%)
  between operations  0.83 us (2%)
    pallas_call x1, Pallas kernels, local(): call(second_kernel, shape(levels, cols, lat), [VMEM_SPEC] * 8, [field, fi...  8.3 us
    all_to_all x1, starting transfers between devices, local(): recv = lax.all_to_all(sent, 'lon', split_axis=0, concat_axis=0, tiled=True)  7.4 us
    pallas_call x1, Pallas kernels, local(): call(edge_kernel, (shape(total + extra, STEN), shape(owners, STEN)), [SME...  4.84 us
    ppermute x1, starting transfers between devices, local(): from_right = lax.ppermute(edge_left, 'lon', to_left)  4.05 us
    pallas_call x1, Pallas kernels, local(): call(head_kernel, (shape(parts, cols * levels, STEN), shape(3 * parts, co...  3.81 us
    all_to_all x1, starting transfers between devices, local(): lax.all_to_all(departure[:, None, :], 'lon', split_axis=0, concat_axis=0,...  3.43 us
    pallas_call x1, Pallas kernels, local(): call(inner_kernel, (shape(parts, (cols - 2 * halo) * levels, STEN), shape...  2.96 us
    ppermute x1, starting transfers between devices, local(): spread_right = lax.ppermute(spread, 'lon', to_left)  2.35 us
  transfers between devices with their start and end apart: 6, of which 0 were waited for; matrix products, arithmetic and copies ran while one was open for 0% of the time, Pallas kernels for 33%

profile of v4, /device:TPU:0, one launch (start us, length us, event | category | flops | bytes accessed | tf_op | source)
XLA Modules:
  0.0 50.3 jit_solution(1152020614482144030)
XLA Ops:
  0.6 0.7 %fusion.1 = f32[16,8]{0,1:T(8,128)S(1)} fusion(s32[16]{0:T(128)} %bitcast.14), kind=kLoop, calls=%fused_computation.9 | loop fusion | flops 256 | bytes 576 | tf_op jit(solution)/shard_map/convert_element_type | solution.py:471
  1.3 0.7 %convert_bitcast_fusion = f32[16,8]{0,1:T(8,128)S(1)} fusion(s32[1,16,8]{1,2,0:T(8,128)} %param.17), kind=kLoop, calls=%fused_computation.8 | loop fusion | flops 128 | bytes 1024 | tf_op jit(solution)/shard_map/convert_element_type | solution.py:471
  2.0 0.7 %pad_maximum_fusion.1 = f32[16,32]{0,1:T(8,128)S(1)} fusion(f32[16,8]{0,1:T(8,128)S(1)} %fusion.1, f32[16,8]{0,1:T(8,128)S(1)} %convert_bitcast_fusion, f32[16,8]{0,1:T(8,128)} %bitcast.12, f32[16,8]{0,1:T(8,128)} %bitcast.13), kind=kLoop, calls=%fused_computation.3 | loop fusion | flops 1536 | bytes 4096 | tf_op jit(solution)/shard_map/concatenate | solution.py:471
  2.7 0.1 copy.20
  2.8 0.8 %convert_element_type.36 = f32[32,512]{1,0:T(8,128)S(1)} convert(s32[32,512]{1,0:T(8,128)} %mask_ref.1) | non-fusion elementwise | flops 16384 | bytes 131072 | tf_op jit(solution)/shard_map/convert_element_type | solution.py:476
  3.6 1.5 %pad_maximum_fusion = f32[16,16,128]{2,1,0:T(8,128)} fusion(f32[16,8,128]{2,1,0:T(8,128)S(1)} %broadcast_in_dim.4, f32[16,8,128]{2,1,0:T(8,128)} %bitcast.11), kind=kLoop, calls=%fused_computation.2 | loop fusion | flops 32768 | bytes 262144 | tf_op jit(solution)/shard_map/concatenate | solution.py:474
  5.1 0.9 %select_maximum_fusion.stack_ref = f32[112,512]{1,0:T(8,128)S(1)} fusion(f32[16,16]{1,0:T(8,128)} %v_ref.1, f32[32,512]{1,0:T(8,128)S(1)} %convert_element_type.36, f32[32,512]{1,0:T(8,128)} %param.14, f32[32,512]{1,0:T(8,128)} %param.13), kind=kLoop, calls=%fused_computation | loop fusion | flops 286720 | bytes 427008 | tf_op jit(solution)/shard_map/concatenate | solution.py:475
  6.0 7.4 %all-to-all-start = ((f32[16,16,128]{2,1,0:T(8,128)}), f32[16,16,128]{2,1,0:T(8,128)S(1)}, u32[]{:S(2)}, u32[]{:S(2)}) async-start(f32[16,16,128]{2,1,0:T(8,128)} %pad_maximum_fusion), calls=%async_computation | async-start | bytes 262144 | tf_op jit(solution)/shard_map/all_to_all | solution.py:492
  13.4 0.0 copy-start.1
  13.5 0.0 copy-start.5
  13.5 3.8 %shard_map.122 = (f32[4,512,128]{2,1,0:T(8,128)}, f32[12,32,128]{2,1,0:T(8,128)S(1)}, f32[728,128]{1,0:T(8,128)}, f32[728,128]{1,0:T(8,128)}) custom-call(f32[112,512]{1,0:T(8,128)S(1)} %select_maximum_fusion.stack_ref, f32[16,32,512]{2,1,0:T(8,128)} %control_ref.1), custom_call_target="tpu_custom_call" | custom-call | flops 2617245696 | bytes 13631488 | tf_op jit(solution)/shard_map/pallas_call | solution.py:479
  17.3 0.5 collective-permute-start
  17.7 4.1 %collective-permute-start.1 = (f32[728,128]{1,0:T(8,128)}, f32[728,128]{1,0:T(8,128)S(1)}, u32[]{:S(2)}, u32[]{:S(2)}) collective-permute-start(f32[728,128]{1,0:T(8,128)} %get-tuple-element.23), channel_id=1, source_target_pairs={{1,0},{2,1},{3,2},{4,3},{5,4},{6,5},{7,6},{8,7},{9,8},{10,9},{11,1... | collective-permute-start | bytes 1118216 | tf_op jit(solution)/shard_map/ppermute | solution.py:490
  21.8 1.2 %copy-done = f32[4,512,128]{2,1,0:T(8,128)S(1)} copy-done((f32[4,512,128]{2,1,0:T(8,128)S(1)}, f32[4,512,128]{2,1,0:T(8,128)}, u32[]{:S(2)}) %copy-start) | copy-done | bytes 1048600
  23.0 3.0 %shard_map.123 = (f32[4,192,128]{2,1,0:T(8,128)S(1)}, f32[10,2,8,16,128]{4,3,2,1,0:T(8,128)S(1)}) custom-call(f32[4,512,128]{2,1,0:T(8,128)S(1)} %copy-done, f32[12,32,128]{2,1,0:T(8,128)S(1)} %get-tuple-element.19.faces_ref), custom_call_target="tpu_custom_call" | custom-call | flops 21299200 | bytes 17039360 | tf_op jit(solution)/shard_map/pallas_call | solution.py:512
  26.0 0.0 copy-start.3
  26.0 0.7 %copy-done.3 = f32[4,192,128]{2,1,0:T(8,128)} copy-done((f32[4,192,128]{2,1,0:T(8,128)}, f32[4,192,128]{2,1,0:T(8,128)S(1)}, u32[]{:S(2)}) %copy-start.3) | copy-done | bytes 393240
  26.7 0.0 all-to-all-done.recv_ref
  26.7 0.1 fusion
  26.8 0.1 convert_element_type.38
  26.9 0.0 copy-start.4
  27.0 1.4 %shard_map.124 = (f32[128,128]{1,0:T(8,128)S(1)}, f32[4,128,128]{2,1,0:T(8,128)S(1)}) custom-call(s32[2,128]{1,0:T(2,128)S(1)} %pad_add_fusion.place_ref, f32[16,16,128]{2,1,0:T(8,128)S(1)} %all-to-all-done.recv_ref, f32[16,32,512]{2,1,0:T(8,128)S(1)} %copy-done.1, s32[32,512]{1,0:T(8,128)S(1)} %copy-done.5), custom_call_target="tpu_custom_call" | custom-call | flops 50331648 | bytes 6815744 | tf_op jit(solution)/shard_map/pallas_call | solution.py:496
  28.4 0.0 collective-permute-done.1.from_right
  28.5 0.0 copy-start.2
  28.5 0.0 copy-start.6
  28.5 4.8 %shard_map.125 = (f32[136,128]{1,0:T(8,128)S(1)}, f32[16,128]{1,0:T(8,128)}) custom-call(s32[2,128]{1,0:T(2,128)S(1)} %pad_add_fusion.place_ref, f32[4,192,128]{2,1,0:T(8,128)S(1)} %copy-done.4, f32[10,2,8,16,128]{4,3,2,1,0:T(8,128)S(1)} %get-tuple-element.21.strips_ref, f32[728,128]{1,0:T(8,128)S(1)} %collective-permute-done.from_left, ...), custom_call_target="tpu_custom_call" | custom-call | flops 21299200 | bytes 17039360 | tf_op jit(solution)/shard_map/pallas_call | solution.py:522
  33.3 2.1 %collective-permute-start.2 = (f32[136,128]{1,0:T(8,128)S(1)}, f32[136,128]{1,0:T(8,128)S(1)}, u32[]{:S(2)}, u32[]{:S(2)}) collective-permute-start(f32[136,128]{1,0:T(8,128)S(1)} %get-tuple-element.26.own_ref), channel_id=1, source_target_pairs={{0,1},{1,2},{2,3},{3,4},{4,5},{5,6},{6,7},{7,8},{8,9},{9,10},{10,1... | collective-permute-start | bytes 208904 | tf_op jit(solution)/shard_map/ppermute | solution.py:533
  35.4 2.4 %collective-permute-start.3 = (f32[136,128]{1,0:T(8,128)S(1)}, f32[136,128]{1,0:T(8,128)S(1)}, u32[]{:S(2)}, u32[]{:S(2)}) collective-permute-start(f32[136,128]{1,0:T(8,128)S(1)} %get-tuple-element.26.own_ref), channel_id=1, source_target_pairs={{1,0},{2,1},{3,2},{4,3},{5,4},{6,5},{7,6},{8,7},{9,8},{10,9},{11,1... | collective-permute-start | bytes 208904 | tf_op jit(solution)/shard_map/ppermute | solution.py:534
  37.8 3.4 %all-to-all-start.1 = ((f32[16,1,128]{2,1,0:T(1,128)}), f32[16,1,128]{2,1,0:T(1,128)S(1)}, u32[]{:S(2)}, u32[]{:S(2)}) async-start(f32[16,1,128]{2,1,0:T(1,128)} %bitcast.6), calls=%async_computation.1 | async-start | bytes 16384 | tf_op jit(solution)/shard_map/all_to_all | solution.py:535
  41.2 8.3 %shard_map.126 = f32[16,32,512]{2,1,0:T(8,128)} custom-call(f32[16,16]{1,0:T(8,128)S(1)} %copy-done.6, f32[16,32,512]{2,1,0:T(8,128)S(1)} %copy-done.2, f32[136,128]{1,0:T(8,128)S(1)} %get-tuple-element.26.own_ref, f32[136,128]{1,0:T(8,128)S(1)} %collective-permute-done.2.left_ref, f32[136,128]{1,0:T(8,128)S(1)} %collective-permute-done.3.right_ref, ...), custom_call_target="tpu_custom_call" | custom-call | flops 42598400 | bytes 34078720 | tf_op jit(solution)/shard_map/pallas_call | solution.py:537
  49.6 0.1 copy.19
  49.7 0.6 %slice_bitcast_fusion = f32[1,16,8]{1,2,0:T(8,128)} fusion(f32[16,1,128]{0,2,1:T(8,128)S(1)} %copy.19), kind=kLoop, calls=%fused_computation.6 | loop fusion | bytes 1024 | tf_op jit(solution)/shard_map/broadcast_in_dim;squeeze | solution.py:542
  (14 shorter events, 0.0 us)
Async XLA Ops:
  6.0 20.7 %all-to-all-start = ((f32[16,16,128]{2,1,0:T(8,128)}), f32[16,16,128]{2,1,0:T(8,128)S(1)}, u32[]{:S(2)}, u32[]{:S(2)}) async-start(f32[16,16,128]{2,1,0:T(8,128)} %pad_maximum_fusion), calls=%async_computation | async-start | bytes 262144 | tf_op jit(solution)/shard_map/all_to_all | solution.py:492
  13.4 13.5 %copy-start.1 = (f32[16,32,512]{2,1,0:T(8,128)S(1)}, f32[16,32,512]{2,1,0:T(8,128)}, u32[]{:S(2)}) copy-start(f32[16,32,512]{2,1,0:T(8,128)} %std_ref.1) | copy-start | bytes 3145732
  13.5 13.5 %copy-start.5 = (s32[32,512]{1,0:T(8,128)S(1)}, s32[32,512]{1,0:T(8,128)}, u32[]{:S(2)}) copy-start(s32[32,512]{1,0:T(8,128)} %mask_ref.1) | copy-start | bytes 196612
  17.3 11.1 %collective-permute-start = (f32[728,128]{1,0:T(8,128)}, f32[728,128]{1,0:T(8,128)S(1)}, u32[]{:S(2)}, u32[]{:S(2)}) collective-permute-start(f32[728,128]{1,0:T(8,128)} %get-tuple-element.22), channel_id=1, source_target_pairs={{0,1},{1,2},{2,3},{3,4},{4,5},{5,6},{6,7},{7,8},{8,9},{9,10},{10,1... | collective-permute-start | bytes 1118216 | tf_op jit(solution)/shard_map/ppermute | solution.py:489
  17.7 10.7 %collective-permute-start.1 = (f32[728,128]{1,0:T(8,128)}, f32[728,128]{1,0:T(8,128)S(1)}, u32[]{:S(2)}, u32[]{:S(2)}) collective-permute-start(f32[728,128]{1,0:T(8,128)} %get-tuple-element.23), channel_id=1, source_target_pairs={{1,0},{2,1},{3,2},{4,3},{5,4},{6,5},{7,6},{8,7},{9,8},{10,9},{11,1... | collective-permute-start | bytes 1118216 | tf_op jit(solution)/shard_map/ppermute | solution.py:490
  21.8 1.2 %copy-start = (f32[4,512,128]{2,1,0:T(8,128)S(1)}, f32[4,512,128]{2,1,0:T(8,128)}, u32[]{:S(2)}) copy-start(f32[4,512,128]{2,1,0:T(8,128)} %get-tuple-element.18.mixed_ref) | copy-start | bytes 3145732
  26.0 0.7 %copy-start.3 = (f32[4,192,128]{2,1,0:T(8,128)}, f32[4,192,128]{2,1,0:T(8,128)S(1)}, u32[]{:S(2)}) copy-start(f32[4,192,128]{2,1,0:T(8,128)S(1)} %get-tuple-element.20.inner_ref) | copy-start | bytes 1179652
  26.9 1.5 %copy-start.4 = (f32[4,192,128]{2,1,0:T(8,128)S(1)}, f32[4,192,128]{2,1,0:T(8,128)}, u32[]{:S(2)}) copy-start(f32[4,192,128]{2,1,0:T(8,128)} %copy-done.3) | copy-start | bytes 1179652
  28.5 12.8 %copy-start.2 = (f32[16,32,512]{2,1,0:T(8,128)S(1)}, f32[16,32,512]{2,1,0:T(8,128)}, u32[]{:S(2)}) copy-start(f32[16,32,512]{2,1,0:T(8,128)} %control_ref.1) | copy-start | bytes 3145732
  28.5 12.8 %copy-start.6 = (f32[16,16]{1,0:T(8,128)S(1)}, f32[16,16]{1,0:T(8,128)}, u32[]{:S(2)}) copy-start(f32[16,16]{1,0:T(8,128)} %v_ref.1) | copy-start | bytes 3076
  33.3 7.9 %collective-permute-start.2 = (f32[136,128]{1,0:T(8,128)S(1)}, f32[136,128]{1,0:T(8,128)S(1)}, u32[]{:S(2)}, u32[]{:S(2)}) collective-permute-start(f32[136,128]{1,0:T(8,128)S(1)} %get-tuple-element.26.own_ref), channel_id=1, source_target_pairs={{0,1},{1,2},{2,3},{3,4},{4,5},{5,6},{6,7},{7,8},{8,9},{9,10},{10,1... | collective-permute-start | bytes 208904 | tf_op jit(solution)/shard_map/ppermute | solution.py:533
  35.4 5.8 %collective-permute-start.3 = (f32[136,128]{1,0:T(8,128)S(1)}, f32[136,128]{1,0:T(8,128)S(1)}, u32[]{:S(2)}, u32[]{:S(2)}) collective-permute-start(f32[136,128]{1,0:T(8,128)S(1)} %get-tuple-element.26.own_ref), channel_id=1, source_target_pairs={{1,0},{2,1},{3,2},{4,3},{5,4},{6,5},{7,6},{8,7},{9,8},{10,9},{11,1... | collective-permute-start | bytes 208904 | tf_op jit(solution)/shard_map/ppermute | solution.py:534
  37.8 11.8 %all-to-all-start.1 = ((f32[16,1,128]{2,1,0:T(1,128)}), f32[16,1,128]{2,1,0:T(1,128)S(1)}, u32[]{:S(2)}, u32[]{:S(2)}) async-start(f32[16,1,128]{2,1,0:T(1,128)} %bitcast.6), calls=%async_computation.1 | async-start | bytes 16384 | tf_op jit(solution)/shard_map/all_to_all | solution.py:535

commit v5 on v4

--- a/solution.py
+++ b/solution.py
@@ -10,7 +10,7 @@
 WIDE = 256
 F32 = jnp.float32
 BF16 = jnp.bfloat16
-HEAD_VMEM = 52 * 1024 * 1024
+WHOLE_VMEM = 60 * 1024 * 1024
 TIERS = ((0, 4), (4, PASSES))
 VMEM_LIMIT = 24 * 1024 * 1024
 
@@ -106,6 +106,15 @@
     return tuple(dot(part, matrix).astype(BF16) for part in x)
 
 
+def pack_meta(slots, values):
+    stacked = jnp.concatenate(values, axis=0)
+    eye = onehot(iota((stacked.shape[0], STEN), 0) == iota((stacked.shape[0], STEN), 1))
+    return sum(
+        lax.dot_general(part, eye, (((0,), (0,)), ((), ())), preferred_element_type=F32)
+        for part in split3(stacked)
+    )
+
+
 def unpack_meta(recv_ref, slots, field):
     owners = recv_ref.shape[0]
     total = owners * slots
@@ -115,27 +124,32 @@
 
 
 def head_kernel(
-    stack_ref, control_hbm, mixed_ref, faces_ref, left_ref, right_ref, control_ref, sem,
+    mask_hbm, klon_hbm, klat_hbm, v_hbm, control_hbm, mixed_ref, faces_ref, left_ref, right_ref,
+    mask_ref, klon_ref, klat_ref, v_ref, control_ref, sems,
 ):
-    copy = pltpu.make_async_copy(control_hbm, control_ref, sem)
-    copy.start()
+    pairs = (
+        (mask_hbm, mask_ref), (klon_hbm, klon_ref), (klat_hbm, klat_ref), (v_hbm, v_ref), (control_hbm, control_ref),
+    )
+    copies = [pltpu.make_async_copy(source, target, sems.at[k]) for k, (source, target) in enumerate(pairs)]
+    for copy in copies:
+        copy.start()
     levels, cols, lat = control_ref.shape
     parts = lat // STEN
     group = WIDE // levels
     halo = PASSES
     edge = halo * levels
     place = deinterleave(lat)
-    matrix = mixing_matrix(stack_ref[3 * cols : 3 * cols + levels, 0:levels])
-    wet = stack_ref[2 * cols : 3 * cols, :]
+    for copy in copies[:4]:
+        copy.wait()
+    matrix = mixing_matrix(v_ref[...])
+    wet = mask_ref[...].astype(F32)
     east = jnp.where(iota((cols, lat), 0) == cols - 1, F32(1.0), pltpu.roll(wet, cols - 1, 0))
     north = jnp.where(iota((cols, lat), 1) == lat - 1, F32(0.0), pltpu.roll(wet, lat - 1, 1))
-    for k, face in enumerate(
-        (stack_ref[0:cols, :] * wet * east, stack_ref[cols : 2 * cols, :] * wet * north, wet)
-    ):
+    for k, face in enumerate((klon_ref[...] * wet * east, klat_ref[...] * wet * north, wet)):
         held = sum(dot(piece, place) for piece in (split3(face) if k < 2 else (face.astype(BF16),)))
         for q in range(parts):
             faces_ref[k * parts + q] = held[:, q * STEN : (q + 1) * STEN]
-    copy.wait()
+    copies[4].wait()
     for g in range(cols // group):
         x = control_ref[:, g * group : (g + 1) * group, :].reshape(WIDE, lat)
         y = product(matrix, move(split(x), place))
@@ -151,6 +165,25 @@
         for q in range(parts):
             out[first + q : first + q + 1, :] = faces_ref[2 * parts + q, 0:1, :]
         out[first + parts :, :] = jnp.zeros((out.shape[0] - first - parts, STEN), F32)
+
+
+def pack_kernel(
+    index_hbm, value_hbm, rinv_hbm, count_hbm, weights_hbm, sent_ref,
+    index_ref, value_ref, rinv_ref, count_ref, sems,
+):
+    owners, slots, _ = weights_hbm.shape
+    pairs = (
+        (index_hbm, index_ref), (value_hbm, value_ref), (rinv_hbm, rinv_ref), (count_hbm, count_ref),
+        (weights_hbm, sent_ref.at[:, 0:slots, :]),
+    )
+    copies = [pltpu.make_async_copy(source, target, sems.at[k]) for k, (source, target) in enumerate(pairs)]
+    for copy in copies:
+        copy.start()
+    for copy in copies:
+        copy.wait()
+    valid = jnp.where(iota((slots, owners), 0) < count_ref[...], F32(1.0), F32(0.0))
+    meta = pack_meta(slots, [value_ref[...], rinv_ref[...], index_ref[...].astype(F32), valid])
+    sent_ref[:, slots:, :] = jnp.broadcast_to(meta[:, None, :], (owners, slots, STEN))
 
 
 def build_faces(faces_ref, from_left, from_right, lon_ref, lat_ref, levels):
@@ -467,25 +500,33 @@
 
     message = parts * halo * (levels + 2) + parts
     message = -(-message // 8) * 8
-    valid = jnp.arange(slots, dtype=jnp.int32)[None, :] < obs_count[0][:, None]
-    meta = jnp.concatenate([obs_value[0], obs_rinv[0], block_index[0].astype(F32), valid.astype(F32)], axis=1)
-    meta = jnp.pad(meta, ((0, 0), (0, STEN - 4 * slots)))
-    meta = jnp.broadcast_to(meta[:, None, :], (owners, slots, STEN))
-    sent = jnp.concatenate([weights[0], meta], axis=1)
-    stack = jnp.concatenate(
-        [kappa_lon, kappa_lat, sea_mask.astype(F32), jnp.pad(vertical, ((0, 0), (0, lat - levels)))]
-    )
-    sent, stack = lax.optimization_barrier((sent, stack))
+    hbm = pl.BlockSpec(memory_space=pltpu.HBM)
+    small = pltpu.VMEM((slots, owners), F32)
+    sent = call(
+        pack_kernel,
+        shape(owners, 2 * slots, STEN),
+        [hbm] * 5,
+        [
+            pltpu.VMEM((slots, owners), jnp.int32), small, small, pltpu.VMEM((1, owners), jnp.int32),
+            pltpu.SemaphoreType.DMA((5,)),
+        ],
+        6 * STEN * owners * STEN, 4 * 4 * total * STEN, WHOLE_VMEM,
+    )(block_index[0].T, obs_value[0].T, obs_rinv[0].T, obs_count, weights[0])
+    sent, matrix = lax.optimization_barrier((sent, vertical))
+    plane = pltpu.VMEM((cols, lat), F32)
     mixed, faces, edge_left, edge_right = call(
         head_kernel,
         (
             shape(parts, cols * levels, STEN), shape(3 * parts, cols, STEN),
             shape(message, STEN), shape(message, STEN),
         ),
-        [VMEM_SPEC, pl.BlockSpec(memory_space=pltpu.HBM)],
-        [pltpu.VMEM((levels, cols, lat), F32), pltpu.SemaphoreType.DMA(())],
-        12 * cells * lat, 8 * 4 * cells, HEAD_VMEM,
-    )(stack, control)
+        [hbm] * 5,
+        [
+            pltpu.VMEM((cols, lat), jnp.int32), plane, plane, pltpu.VMEM((levels, levels), F32),
+            pltpu.VMEM((levels, cols, lat), F32), pltpu.SemaphoreType.DMA((5,)),
+        ],
+        12 * cells * lat, 8 * 4 * cells, WHOLE_VMEM,
+    )(sea_mask, kappa_lon, kappa_lat, matrix, control)
     from_left = lax.ppermute(edge_right, "lon", to_right)
     from_right = lax.ppermute(edge_left, "lon", to_left)
 

time: 50.8 us -> 48.4 us (0.953)
  other arithmetic: 5.43 us -> 0.11 us
  Pallas kernels: 21.3 us -> 23.5 us
  local copies, waits for them, and re-layouts: 2.86 us -> 3.71 us
    concatenate x3 -> x0, other arithmetic: 3.12 us -> none  [the longest x1 1.5 us: local(): sent = jnp.concatenate([weights[0], meta], axis=1)]
    convert_element_type x3 -> x0, other arithmetic: 2.2 us -> none  [the longest x1 0.85 us: local(): sea_mask.astype(F32)]
    pallas_call x0 -> x1, Pallas kernels: none -> 1.78 us  [local(): call(pack_kernel, shape(owners, 2 * slots, STEN), [hbm] * 5, [pltpu.VMEM(...]
    ppermute x1, starting transfers between devices: 2.09 us -> 1.16 us  [local(): spread_left = lax.ppermute(spread, 'lon', to_right)]
    ppermute x1, starting transfers between devices: 2.35 us -> 3.28 us  [local(): spread_right = lax.ppermute(spread, 'lon', to_left)]
    unnamed x15 -> x18, local copies, waits for them, and re-layouts: 2.07 us -> 2.93 us
  transfers between devices with their start and end apart: 6 -> 6, of which waited for: 0 -> 0; matrix products, arithmetic and copies ran while one was open for 0% -> 0% of each run, Pallas kernels for 33% -> 35%
where the time goes in v5:
time: 48.4 us; the launch traced here: 48 us
  Pallas kernels  23.5 us (49%)
  starting transfers between devices  19.8 us (41%)
  local copies, waits for them, and re-layouts  3.71 us (8%)
  between operations  0.83 us (2%)
    pallas_call x1, Pallas kernels, local(): call(second_kernel, shape(levels, cols, lat), [VMEM_SPEC] * 8, [field, fi...  8.3 us
    all_to_all x1, starting transfers between devices, local(): recv = lax.all_to_all(sent, 'lon', split_axis=0, concat_axis=0, tiled=True)  7.4 us
    pallas_call x1, Pallas kernels, local(): call(edge_kernel, (shape(total + extra, STEN), shape(owners, STEN)), [SME...  4.9 us
    pallas_call x1, Pallas kernels, local(): call(head_kernel, (shape(parts, cols * levels, STEN), shape(3 * parts, co...  4.13 us
    ppermute x1, starting transfers between devices, local(): from_right = lax.ppermute(edge_left, 'lon', to_left)  4.04 us
    all_to_all x1, starting transfers between devices, local(): lax.all_to_all(departure[:, None, :], 'lon', split_axis=0, concat_axis=0,...  3.49 us
    ppermute x1, starting transfers between devices, local(): spread_right = lax.ppermute(spread, 'lon', to_left)  3.28 us
    pallas_call x1, Pallas kernels, local(): call(inner_kernel, (shape(parts, (cols - 2 * halo) * levels, STEN), shape...  2.97 us
  transfers between devices with their start and end apart: 6, of which 0 were waited for; matrix products, arithmetic and copies ran while one was open for 0% of the time, Pallas kernels for 35%

profile of v5, /device:TPU:0, one launch (start us, length us, event | category | flops | bytes accessed | tf_op | source)
XLA Modules:
  0.0 48.0 jit_solution(1632468131554964039)
XLA Ops:
  0.6 1.8 %shard_map.122 = f32[16,16,128]{2,1,0:T(8,128)} custom-call(s32[8,16]{1,0:T(8,128)} %bitcast.16, f32[8,16]{1,0:T(8,128)} %bitcast.17, f32[8,16]{1,0:T(8,128)} %bitcast.18, s32[1,16]{1,0:T(1,128)} %count_hbm.1, f32[16,8,128]{2,1,0:T(8,128)} %bitcast.15), custom_call_target="tpu_custom_call" | custom-call | flops 1572864 | bytes 262144 | tf_op jit(solution)/shard_map/pallas_call | solution.py:505
  2.4 7.4 %all-to-all-start = ((f32[16,16,128]{2,1,0:T(8,128)}), f32[16,16,128]{2,1,0:T(8,128)S(1)}, u32[]{:S(2)}, u32[]{:S(2)}) async-start(f32[16,16,128]{2,1,0:T(8,128)} %shard_map.122), calls=%async_computation | async-start | bytes 262144 | tf_op jit(solution)/shard_map/all_to_all | solution.py:533
  9.8 0.0 copy-start.3
  9.8 0.0 copy-start.7
  9.8 4.1 %shard_map.123 = (f32[4,512,128]{2,1,0:T(8,128)}, f32[12,32,128]{2,1,0:T(8,128)}, f32[728,128]{1,0:T(8,128)}, f32[728,128]{1,0:T(8,128)}) custom-call(s32[32,512]{1,0:T(8,128)} %mask_ref.1, f32[32,512]{1,0:T(8,128)} %klon_hbm.1, f32[32,512]{1,0:T(8,128)} %klat_hbm.1, f32[16,16]{1,0:T(8,128)} %v_ref.1, f32[16,32,512]{2,1,0:T(8,128)} %control_ref.1), custom_call_target="tpu_custom_call" | custom-call | flops 2617245696 | bytes 13631488 | tf_op jit(solution)/shard_map/pallas_call | solution.py:517
  14.0 0.5 collective-permute-start
  14.4 4.0 %collective-permute-start.1 = (f32[728,128]{1,0:T(8,128)}, f32[728,128]{1,0:T(8,128)S(1)}, u32[]{:S(2)}, u32[]{:S(2)}) collective-permute-start(f32[728,128]{1,0:T(8,128)} %get-tuple-element.23), channel_id=1, source_target_pairs={{1,0},{2,1},{3,2},{4,3},{5,4},{6,5},{7,6},{8,7},{9,8},{10,9},{11,1... | collective-permute-start | bytes 1118216 | tf_op jit(solution)/shard_map/ppermute | solution.py:531
  18.5 0.9 %copy-done = f32[12,32,128]{2,1,0:T(8,128)S(1)} copy-done((f32[12,32,128]{2,1,0:T(8,128)S(1)}, f32[12,32,128]{2,1,0:T(8,128)}, u32[]{:S(2)}) %copy-start) | copy-done | bytes 196632
  19.4 1.2 %copy-done.2 = f32[4,512,128]{2,1,0:T(8,128)S(1)} copy-done((f32[4,512,128]{2,1,0:T(8,128)S(1)}, f32[4,512,128]{2,1,0:T(8,128)}, u32[]{:S(2)}) %copy-start.2) | copy-done | bytes 1048600
  20.6 3.0 %shard_map.124 = (f32[4,192,128]{2,1,0:T(8,128)S(1)}, f32[10,2,8,16,128]{4,3,2,1,0:T(8,128)S(1)}) custom-call(f32[4,512,128]{2,1,0:T(8,128)S(1)} %copy-done.2, f32[12,32,128]{2,1,0:T(8,128)S(1)} %copy-done), custom_call_target="tpu_custom_call" | custom-call | flops 21299200 | bytes 17039360 | tf_op jit(solution)/shard_map/pallas_call | solution.py:553
  23.6 0.0 copy-start.5
  23.6 0.7 %copy-done.5 = f32[4,192,128]{2,1,0:T(8,128)} copy-done((f32[4,192,128]{2,1,0:T(8,128)}, f32[4,192,128]{2,1,0:T(8,128)S(1)}, u32[]{:S(2)}) %copy-start.5) | copy-done | bytes 393240
  24.4 0.0 all-to-all-done.recv_ref
  24.4 0.1 fusion
  24.5 0.1 convert_element_type.18
  24.6 0.0 copy-start.6
  24.6 0.0 copy-done.3
  24.6 1.4 %shard_map.125 = (f32[128,128]{1,0:T(8,128)S(1)}, f32[4,128,128]{2,1,0:T(8,128)S(1)}) custom-call(s32[2,128]{1,0:T(2,128)S(1)} %pad_add_fusion.place_ref, f32[16,16,128]{2,1,0:T(8,128)S(1)} %all-to-all-done.recv_ref, f32[16,32,512]{2,1,0:T(8,128)S(1)} %copy-done.3, s32[32,512]{1,0:T(8,128)S(1)} %copy-done.7), custom_call_target="tpu_custom_call" | custom-call | flops 50331648 | bytes 6815744 | tf_op jit(solution)/shard_map/pallas_call | solution.py:537
  26.1 0.0 collective-permute-done.from_left
  26.1 0.0 collective-permute-done.1.from_right
  26.1 0.0 copy-start.4
  26.1 0.0 copy-start.8
  26.1 4.9 %shard_map.126 = (f32[136,128]{1,0:T(8,128)S(1)}, f32[16,128]{1,0:T(8,128)}) custom-call(s32[2,128]{1,0:T(2,128)S(1)} %pad_add_fusion.place_ref, f32[4,192,128]{2,1,0:T(8,128)S(1)} %copy-done.6, f32[10,2,8,16,128]{4,3,2,1,0:T(8,128)S(1)} %get-tuple-element.21.strips_ref, f32[728,128]{1,0:T(8,128)S(1)} %collective-permute-done.from_left, ...), custom_call_target="tpu_custom_call" | custom-call | flops 21299200 | bytes 17039360 | tf_op jit(solution)/shard_map/pallas_call | solution.py:563
  31.0 1.2 %collective-permute-start.2 = (f32[136,128]{1,0:T(8,128)S(1)}, f32[136,128]{1,0:T(8,128)S(1)}, u32[]{:S(2)}, u32[]{:S(2)}) collective-permute-start(f32[136,128]{1,0:T(8,128)S(1)} %get-tuple-element.26.own_ref), channel_id=1, source_target_pairs={{0,1},{1,2},{2,3},{3,4},{4,5},{5,6},{6,7},{7,8},{8,9},{9,10},{10,1... | collective-permute-start | bytes 208904 | tf_op jit(solution)/shard_map/ppermute | solution.py:574
  32.2 3.3 %collective-permute-start.3 = (f32[136,128]{1,0:T(8,128)S(1)}, f32[136,128]{1,0:T(8,128)S(1)}, u32[]{:S(2)}, u32[]{:S(2)}) collective-permute-start(f32[136,128]{1,0:T(8,128)S(1)} %get-tuple-element.26.own_ref), channel_id=1, source_target_pairs={{1,0},{2,1},{3,2},{4,3},{5,4},{6,5},{7,6},{8,7},{9,8},{10,9},{11,1... | collective-permute-start | bytes 208904 | tf_op jit(solution)/shard_map/ppermute | solution.py:575
  35.5 3.5 %all-to-all-start.1 = ((f32[16,1,128]{2,1,0:T(1,128)}), f32[16,1,128]{2,1,0:T(1,128)S(1)}, u32[]{:S(2)}, u32[]{:S(2)}) async-start(f32[16,1,128]{2,1,0:T(1,128)} %bitcast.8), calls=%async_computation.1 | async-start | bytes 16384 | tf_op jit(solution)/shard_map/all_to_all | solution.py:576
  39.0 0.0 collective-permute-done.2.left_ref
  39.0 0.0 collective-permute-done.3.right_ref
  39.0 8.3 %shard_map.127 = f32[16,32,512]{2,1,0:T(8,128)} custom-call(f32[16,16]{1,0:T(8,128)S(1)} %copy-done.8, f32[16,32,512]{2,1,0:T(8,128)S(1)} %copy-done.4, f32[136,128]{1,0:T(8,128)S(1)} %get-tuple-element.26.own_ref, f32[136,128]{1,0:T(8,128)S(1)} %collective-permute-done.2.left_ref, f32[136,128]{1,0:T(8,128)S(1)} %collective-permute-done.3.right_ref, ...), custom_call_target="tpu_custom_call" | custom-call | flops 42598400 | bytes 34078720 | tf_op jit(solution)/shard_map/pallas_call | solution.py:578
  47.3 0.0 all-to-all-done.1
  47.3 0.1 copy.16
  47.4 0.6 %slice_bitcast_fusion = f32[1,16,8]{1,2,0:T(8,128)} fusion(f32[16,1,128]{0,2,1:T(8,128)S(1)} %copy.16), kind=kLoop, calls=%fused_computation.2 | loop fusion | bytes 1024 | tf_op jit(solution)/shard_map/broadcast_in_dim;squeeze | solution.py:583
  (10 shorter events, 0.0 us)
Async XLA Ops:
  2.4 21.9 %all-to-all-start = ((f32[16,16,128]{2,1,0:T(8,128)}), f32[16,16,128]{2,1,0:T(8,128)S(1)}, u32[]{:S(2)}, u32[]{:S(2)}) async-start(f32[16,16,128]{2,1,0:T(8,128)} %shard_map.122), calls=%async_computation | async-start | bytes 262144 | tf_op jit(solution)/shard_map/all_to_all | solution.py:533
  9.8 14.8 %copy-start.3 = (f32[16,32,512]{2,1,0:T(8,128)S(1)}, f32[16,32,512]{2,1,0:T(8,128)}, u32[]{:S(2)}) copy-start(f32[16,32,512]{2,1,0:T(8,128)} %std_ref.1) | copy-start | bytes 3145732
  9.8 14.8 %copy-start.7 = (s32[32,512]{1,0:T(8,128)S(1)}, s32[32,512]{1,0:T(8,128)}, u32[]{:S(2)}) copy-start(s32[32,512]{1,0:T(8,128)} %mask_ref.1) | copy-start | bytes 196612
  14.0 12.1 %collective-permute-start = (f32[728,128]{1,0:T(8,128)}, f32[728,128]{1,0:T(8,128)S(1)}, u32[]{:S(2)}, u32[]{:S(2)}) collective-permute-start(f32[728,128]{1,0:T(8,128)} %get-tuple-element.22), channel_id=1, source_target_pairs={{0,1},{1,2},{2,3},{3,4},{4,5},{5,6},{6,7},{7,8},{8,9},{9,10},{10,1... | collective-permute-start | bytes 1118216 | tf_op jit(solution)/shard_map/ppermute | solution.py:530
  14.4 11.6 %collective-permute-start.1 = (f32[728,128]{1,0:T(8,128)}, f32[728,128]{1,0:T(8,128)S(1)}, u32[]{:S(2)}, u32[]{:S(2)}) collective-permute-start(f32[728,128]{1,0:T(8,128)} %get-tuple-element.23), channel_id=1, source_target_pairs={{1,0},{2,1},{3,2},{4,3},{5,4},{6,5},{7,6},{8,7},{9,8},{10,9},{11,1... | collective-permute-start | bytes 1118216 | tf_op jit(solution)/shard_map/ppermute | solution.py:531
  18.5 0.9 %copy-start = (f32[12,32,128]{2,1,0:T(8,128)S(1)}, f32[12,32,128]{2,1,0:T(8,128)}, u32[]{:S(2)}) copy-start(f32[12,32,128]{2,1,0:T(8,128)} %get-tuple-element.19.faces_ref) | copy-start | bytes 589828
  19.4 1.2 %copy-start.2 = (f32[4,512,128]{2,1,0:T(8,128)S(1)}, f32[4,512,128]{2,1,0:T(8,128)}, u32[]{:S(2)}) copy-start(f32[4,512,128]{2,1,0:T(8,128)} %get-tuple-element.18.mixed_ref) | copy-start | bytes 3145732
  20.6 5.4 %copy-start.1 = (f32[12,32,128]{2,1,0:T(8,128)S(1)}, f32[12,32,128]{2,1,0:T(8,128)}, u32[]{:S(2)}) copy-start(f32[12,32,128]{2,1,0:T(8,128)} %get-tuple-element.19.faces_ref) | copy-start | bytes 589828
  23.6 0.7 %copy-start.5 = (f32[4,192,128]{2,1,0:T(8,128)}, f32[4,192,128]{2,1,0:T(8,128)S(1)}, u32[]{:S(2)}) copy-start(f32[4,192,128]{2,1,0:T(8,128)S(1)} %get-tuple-element.20.inner_ref) | copy-start | bytes 1179652
  24.6 1.5 %copy-start.6 = (f32[4,192,128]{2,1,0:T(8,128)S(1)}, f32[4,192,128]{2,1,0:T(8,128)}, u32[]{:S(2)}) copy-start(f32[4,192,128]{2,1,0:T(8,128)} %copy-done.5) | copy-start | bytes 1179652
  26.1 12.9 %copy-start.4 = (f32[16,32,512]{2,1,0:T(8,128)S(1)}, f32[16,32,512]{2,1,0:T(8,128)}, u32[]{:S(2)}) copy-start(f32[16,32,512]{2,1,0:T(8,128)} %control_ref.1) | copy-start | bytes 3145732
  26.1 12.9 %copy-start.8 = (f32[16,16]{1,0:T(8,128)S(1)}, f32[16,16]{1,0:T(8,128)}, u32[]{:S(2)}) copy-start(f32[16,16]{1,0:T(8,128)} %v_ref.1) | copy-start | bytes 3076
  31.0 7.9 %collective-permute-start.2 = (f32[136,128]{1,0:T(8,128)S(1)}, f32[136,128]{1,0:T(8,128)S(1)}, u32[]{:S(2)}, u32[]{:S(2)}) collective-permute-start(f32[136,128]{1,0:T(8,128)S(1)} %get-tuple-element.26.own_ref), channel_id=1, source_target_pairs={{0,1},{1,2},{2,3},{3,4},{4,5},{5,6},{6,7},{7,8},{8,9},{9,10},{10,1... | collective-permute-start | bytes 208904 | tf_op jit(solution)/shard_map/ppermute | solution.py:574
  32.2 6.8 %collective-permute-start.3 = (f32[136,128]{1,0:T(8,128)S(1)}, f32[136,128]{1,0:T(8,128)S(1)}, u32[]{:S(2)}, u32[]{:S(2)}) collective-permute-start(f32[136,128]{1,0:T(8,128)S(1)} %get-tuple-element.26.own_ref), channel_id=1, source_target_pairs={{1,0},{2,1},{3,2},{4,3},{5,4},{6,5},{7,6},{8,7},{9,8},{10,9},{11,1... | collective-permute-start | bytes 208904 | tf_op jit(solution)/shard_map/ppermute | solution.py:575
  35.5 11.8 %all-to-all-start.1 = ((f32[16,1,128]{2,1,0:T(1,128)}), f32[16,1,128]{2,1,0:T(1,128)S(1)}, u32[]{:S(2)}, u32[]{:S(2)}) async-start(f32[16,1,128]{2,1,0:T(1,128)} %bitcast.8), calls=%async_computation.1 | async-start | bytes 16384 | tf_op jit(solution)/shard_map/all_to_all | solution.py:576

commit v6 on v5

--- a/solution.py
+++ b/solution.py
@@ -11,7 +11,7 @@
 F32 = jnp.float32
 BF16 = jnp.bfloat16
 WHOLE_VMEM = 60 * 1024 * 1024
-TIERS = ((0, 4), (4, PASSES))
+TIERS = ((0, 2), (2, 6), (6, PASSES))
 VMEM_LIMIT = 24 * 1024 * 1024
 
 VMEM_SPEC = pl.BlockSpec(memory_space=pltpu.VMEM)
@@ -124,11 +124,16 @@
 
 
 def head_kernel(
-    mask_hbm, klon_hbm, klat_hbm, v_hbm, control_hbm, mixed_ref, faces_ref, left_ref, right_ref,
-    mask_ref, klon_ref, klat_ref, v_ref, control_ref, sems,
+    mask_hbm, klon_hbm, klat_hbm, v_hbm, control_hbm, index_hbm, value_hbm, rinv_hbm, count_hbm, weights_hbm,
+    mixed_ref, faces_ref, left_ref, right_ref, sent_ref,
+    mask_ref, klon_ref, klat_ref, v_ref, control_ref, index_ref, value_ref, rinv_ref, count_ref, sems,
 ):
+    owners, rows, _ = sent_ref.shape
+    slots = rows // 2
     pairs = (
-        (mask_hbm, mask_ref), (klon_hbm, klon_ref), (klat_hbm, klat_ref), (v_hbm, v_ref), (control_hbm, control_ref),
+        (mask_hbm, mask_ref), (klon_hbm, klon_ref), (klat_hbm, klat_ref), (v_hbm, v_ref),
+        (control_hbm, control_ref), (index_hbm, index_ref), (value_hbm, value_ref), (rinv_hbm, rinv_ref),
+        (count_hbm, count_ref), (weights_hbm, sent_ref.at[:, 0:slots, :]),
     )
     copies = [pltpu.make_async_copy(source, target, sems.at[k]) for k, (source, target) in enumerate(pairs)]
     for copy in copies:
@@ -165,21 +170,7 @@
         for q in range(parts):
             out[first + q : first + q + 1, :] = faces_ref[2 * parts + q, 0:1, :]
         out[first + parts :, :] = jnp.zeros((out.shape[0] - first - parts, STEN), F32)
-
-
-def pack_kernel(
-    index_hbm, value_hbm, rinv_hbm, count_hbm, weights_hbm, sent_ref,
-    index_ref, value_ref, rinv_ref, count_ref, sems,
-):
-    owners, slots, _ = weights_hbm.shape
-    pairs = (
-        (index_hbm, index_ref), (value_hbm, value_ref), (rinv_hbm, rinv_ref), (count_hbm, count_ref),
-        (weights_hbm, sent_ref.at[:, 0:slots, :]),
-    )
-    copies = [pltpu.make_async_copy(source, target, sems.at[k]) for k, (source, target) in enumerate(pairs)]
-    for copy in copies:
-        copy.start()
-    for copy in copies:
+    for copy in copies[5:]:
         copy.wait()
     valid = jnp.where(iota((slots, owners), 0) < count_ref[...], F32(1.0), F32(0.0))
     meta = pack_meta(slots, [value_ref[...], rinv_ref[...], index_ref[...].astype(F32), valid])
@@ -500,33 +491,25 @@
 
     message = parts * halo * (levels + 2) + parts
     message = -(-message // 8) * 8
-    hbm = pl.BlockSpec(memory_space=pltpu.HBM)
     small = pltpu.VMEM((slots, owners), F32)
-    sent = call(
-        pack_kernel,
-        shape(owners, 2 * slots, STEN),
-        [hbm] * 5,
-        [
-            pltpu.VMEM((slots, owners), jnp.int32), small, small, pltpu.VMEM((1, owners), jnp.int32),
-            pltpu.SemaphoreType.DMA((5,)),
-        ],
-        6 * STEN * owners * STEN, 4 * 4 * total * STEN, WHOLE_VMEM,
-    )(block_index[0].T, obs_value[0].T, obs_rinv[0].T, obs_count, weights[0])
-    sent, matrix = lax.optimization_barrier((sent, vertical))
     plane = pltpu.VMEM((cols, lat), F32)
-    mixed, faces, edge_left, edge_right = call(
+    mixed, faces, edge_left, edge_right, sent = call(
         head_kernel,
         (
             shape(parts, cols * levels, STEN), shape(3 * parts, cols, STEN),
-            shape(message, STEN), shape(message, STEN),
+            shape(message, STEN), shape(message, STEN), shape(owners, 2 * slots, STEN),
         ),
-        [hbm] * 5,
+        [pl.BlockSpec(memory_space=pltpu.HBM)] * 10,
         [
             pltpu.VMEM((cols, lat), jnp.int32), plane, plane, pltpu.VMEM((levels, levels), F32),
-            pltpu.VMEM((levels, cols, lat), F32), pltpu.SemaphoreType.DMA((5,)),
+            pltpu.VMEM((levels, cols, lat), F32), pltpu.VMEM((slots, owners), jnp.int32), small, small,
+            pltpu.VMEM((1, owners), jnp.int32), pltpu.SemaphoreType.DMA((10,)),
         ],
         12 * cells * lat, 8 * 4 * cells, WHOLE_VMEM,
-    )(sea_mask, kappa_lon, kappa_lat, matrix, control)
+    )(
+        sea_mask, kappa_lon, kappa_lat, vertical, control,
+        block_index[0].T, obs_value[0].T, obs_rinv[0].T, obs_count, weights[0],
+    )
     from_left = lax.ppermute(edge_right, "lon", to_right)
     from_right = lax.ppermute(edge_left, "lon", to_left)
 

time: 48.4 us -> 46.1 us (0.952)
  Pallas kernels: 23.5 us -> 20.9 us
    pallas_call x1 -> x0, Pallas kernels: 1.78 us -> none  [local(): call(pack_kernel, shape(owners, 2 * slots, STEN), [hbm] * 5, [pltpu.VMEM(...]
    pallas_call x1, Pallas kernels: 8.3 us -> 7.63 us  [local(): call(second_kernel, shape(levels, cols, lat), [VMEM_SPEC] * 8, [field, fi...]
    ppermute x1, starting transfers between devices: 1.16 us -> 1.75 us  [local(): spread_left = lax.ppermute(spread, 'lon', to_right)]
    ppermute x1, starting transfers between devices: 3.28 us -> 2.69 us  [local(): spread_right = lax.ppermute(spread, 'lon', to_left)]
  transfers between devices with their start and end apart: 6 -> 6, of which waited for: 0 -> 1; matrix products, arithmetic and copies ran while one was open for 0% -> 0% of each run, Pallas kernels for 35% -> 26%
where the time goes in v6:
time: 46.1 us; the launch traced here: 45.8 us
  Pallas kernels  20.9 us (45%)
  starting transfers between devices  20 us (43%)
  local copies, waits for them, and re-layouts  3.71 us (8%)
  between operations  0.8 us (2%)
    pallas_call x1, Pallas kernels, local(): call(second_kernel, shape(levels, cols, lat), [VMEM_SPEC] * 8, [field, fi...  7.63 us
    all_to_all x1, starting transfers between devices, local(): recv = lax.all_to_all(sent, 'lon', split_axis=0, concat_axis=0, tiled=True)  7.53 us
    pallas_call x1, Pallas kernels, local(): call(edge_kernel, (shape(total + extra, STEN), shape(owners, STEN)), [SME...  4.83 us
    pallas_call x1, Pallas kernels, local(): call(head_kernel, (shape(parts, cols * levels, STEN), shape(3 * parts, co...  4.4 us
    ppermute x1, starting transfers between devices, local(): from_right = lax.ppermute(edge_left, 'lon', to_left)  4.08 us
    all_to_all x1, starting transfers between devices, local(): lax.all_to_all(departure[:, None, :], 'lon', split_axis=0, concat_axis=0,...  3.49 us
    unnamed x18, local copies, waits for them, and re-layouts  2.92 us
    ppermute x1, starting transfers between devices, local(): spread_right = lax.ppermute(spread, 'lon', to_left)  2.69 us
  transfers between devices with their start and end apart: 6, of which 1 were waited for; matrix products, arithmetic and copies ran while one was open for 0% of the time, Pallas kernels for 26%

profile of v6, /device:TPU:0, one launch (start us, length us, event | category | flops | bytes accessed | tf_op | source)
XLA Modules:
  0.0 45.8 jit_solution(16332922754657644278)
XLA Ops:
  0.6 4.4 %shard_map.122 = (f32[4,512,128]{2,1,0:T(8,128)}, f32[12,32,128]{2,1,0:T(8,128)}, f32[728,128]{1,0:T(8,128)}, f32[728,128]{1,0:T(8,128)}, f32[16,16,128]{2,1,0:T(8,128)}) custom-call(s32[32,512]{1,0:T(8,128)} %mask_ref.1, f32[32,512]{1,0:T(8,128)} %klon_hbm.1, f32[32,512]{1,0:T(8,128)} %klat_hbm.1, f32[16,16]{1,0:T(8,128)} %v_ref.1, ...), custom_call_target="tpu_custom_call" | custom-call | flops 2617245696 | bytes 13631488 | tf_op jit(solution)/shard_map/pallas_call | solution.py:496
  5.0 0.0 copy-start.7
  5.1 0.0 copy-start.1
  5.1 7.5 %all-to-all-start = ((f32[16,16,128]{2,1,0:T(8,128)}), f32[16,16,128]{2,1,0:T(8,128)S(1)}, u32[]{:S(2)}, u32[]{:S(2)}) async-start(f32[16,16,128]{2,1,0:T(8,128)} %get-tuple-element.15), calls=%async_computation | async-start | bytes 262144 | tf_op jit(solution)/shard_map/all_to_all | solution.py:516
  12.6 0.4 collective-permute-start
  13.0 4.1 %collective-permute-start.1 = (f32[728,128]{1,0:T(8,128)}, f32[728,128]{1,0:T(8,128)S(1)}, u32[]{:S(2)}, u32[]{:S(2)}) collective-permute-start(f32[728,128]{1,0:T(8,128)} %get-tuple-element.21), channel_id=1, source_target_pairs={{1,0},{2,1},{3,2},{4,3},{5,4},{6,5},{7,6},{8,7},{9,8},{10,9},{11,1... | collective-permute-start | bytes 1118216 | tf_op jit(solution)/shard_map/ppermute | solution.py:514
  17.1 0.9 %copy-done = f32[12,32,128]{2,1,0:T(8,128)S(1)} copy-done((f32[12,32,128]{2,1,0:T(8,128)S(1)}, f32[12,32,128]{2,1,0:T(8,128)}, u32[]{:S(2)}) %copy-start) | copy-done | bytes 196632
  18.0 1.2 %copy-done.2 = f32[4,512,128]{2,1,0:T(8,128)S(1)} copy-done((f32[4,512,128]{2,1,0:T(8,128)S(1)}, f32[4,512,128]{2,1,0:T(8,128)}, u32[]{:S(2)}) %copy-start.2) | copy-done | bytes 1048600
  19.3 2.6 %shard_map.123 = (f32[4,192,128]{2,1,0:T(8,128)S(1)}, f32[10,2,8,16,128]{4,3,2,1,0:T(8,128)S(1)}) custom-call(f32[4,512,128]{2,1,0:T(8,128)S(1)} %copy-done.2, f32[12,32,128]{2,1,0:T(8,128)S(1)} %copy-done), custom_call_target="tpu_custom_call" | custom-call | flops 21299200 | bytes 17039360 | tf_op jit(solution)/shard_map/pallas_call | solution.py:536
  21.9 0.0 copy-start.5
  21.9 0.7 %copy-done.5 = f32[4,192,128]{2,1,0:T(8,128)} copy-done((f32[4,192,128]{2,1,0:T(8,128)}, f32[4,192,128]{2,1,0:T(8,128)S(1)}, u32[]{:S(2)}) %copy-start.5) | copy-done | bytes 393240
  22.7 0.0 all-to-all-done.recv_ref
  22.7 0.1 fusion
  22.8 0.1 convert_element_type.18
  22.9 0.0 copy-start.6
  22.9 0.0 copy-done.3
  22.9 0.0 copy-done.7
  22.9 1.4 %shard_map.124 = (f32[128,128]{1,0:T(8,128)S(1)}, f32[4,128,128]{2,1,0:T(8,128)S(1)}) custom-call(s32[2,128]{1,0:T(2,128)S(1)} %pad_add_fusion.place_ref, f32[16,16,128]{2,1,0:T(8,128)S(1)} %all-to-all-done.recv_ref, f32[16,32,512]{2,1,0:T(8,128)S(1)} %copy-done.3, s32[32,512]{1,0:T(8,128)S(1)} %copy-done.7), custom_call_target="tpu_custom_call" | custom-call | flops 50331648 | bytes 6815744 | tf_op jit(solution)/shard_map/pallas_call | solution.py:520
  24.4 0.2 collective-permute-done.from_left
  24.6 0.0 collective-permute-done.1.from_right
  24.6 0.0 copy-start.4
  24.6 0.0 copy-start.8
  24.6 4.8 %shard_map.125 = (f32[136,128]{1,0:T(8,128)S(1)}, f32[16,128]{1,0:T(8,128)}) custom-call(s32[2,128]{1,0:T(2,128)S(1)} %pad_add_fusion.place_ref, f32[4,192,128]{2,1,0:T(8,128)S(1)} %copy-done.6, f32[10,2,8,16,128]{4,3,2,1,0:T(8,128)S(1)} %get-tuple-element.19.strips_ref, f32[728,128]{1,0:T(8,128)S(1)} %collective-permute-done.from_left, ...), custom_call_target="tpu_custom_call" | custom-call | flops 21299200 | bytes 17039360 | tf_op jit(solution)/shard_map/pallas_call | solution.py:546
  29.5 1.7 %collective-permute-start.2 = (f32[136,128]{1,0:T(8,128)S(1)}, f32[136,128]{1,0:T(8,128)S(1)}, u32[]{:S(2)}, u32[]{:S(2)}) collective-permute-start(f32[136,128]{1,0:T(8,128)S(1)} %get-tuple-element.24.own_ref), channel_id=1, source_target_pairs={{0,1},{1,2},{2,3},{3,4},{4,5},{5,6},{6,7},{7,8},{8,9},{9,10},{10,1... | collective-permute-start | bytes 208904 | tf_op jit(solution)/shard_map/ppermute | solution.py:557
  31.2 2.7 %collective-permute-start.3 = (f32[136,128]{1,0:T(8,128)S(1)}, f32[136,128]{1,0:T(8,128)S(1)}, u32[]{:S(2)}, u32[]{:S(2)}) collective-permute-start(f32[136,128]{1,0:T(8,128)S(1)} %get-tuple-element.24.own_ref), channel_id=1, source_target_pairs={{1,0},{2,1},{3,2},{4,3},{5,4},{6,5},{7,6},{8,7},{9,8},{10,9},{11,1... | collective-permute-start | bytes 208904 | tf_op jit(solution)/shard_map/ppermute | solution.py:558
  33.9 3.5 %all-to-all-start.1 = ((f32[16,1,128]{2,1,0:T(1,128)}), f32[16,1,128]{2,1,0:T(1,128)S(1)}, u32[]{:S(2)}, u32[]{:S(2)}) async-start(f32[16,1,128]{2,1,0:T(1,128)} %bitcast.8), calls=%async_computation.1 | async-start | bytes 16384 | tf_op jit(solution)/shard_map/all_to_all | solution.py:559
  37.4 0.0 collective-permute-done.2.left_ref
  37.4 0.0 collective-permute-done.3.right_ref
  37.4 7.6 %shard_map.126 = f32[16,32,512]{2,1,0:T(8,128)} custom-call(f32[16,16]{1,0:T(8,128)S(1)} %copy-done.8, f32[16,32,512]{2,1,0:T(8,128)S(1)} %copy-done.4, f32[136,128]{1,0:T(8,128)S(1)} %get-tuple-element.24.own_ref, f32[136,128]{1,0:T(8,128)S(1)} %collective-permute-done.2.left_ref, f32[136,128]{1,0:T(8,128)S(1)} %collective-permute-done.3.right_ref, ...), custom_call_target="tpu_custom_call" | custom-call | flops 42598400 | bytes 34078720 | tf_op jit(solution)/shard_map/pallas_call | solution.py:561
  45.1 0.0 all-to-all-done.1
  45.1 0.1 copy.16
  45.2 0.6 %slice_bitcast_fusion = f32[1,16,8]{1,2,0:T(8,128)} fusion(f32[16,1,128]{0,2,1:T(8,128)S(1)} %copy.16), kind=kLoop, calls=%fused_computation.2 | loop fusion | bytes 1024 | tf_op jit(solution)/shard_map/broadcast_in_dim;squeeze | solution.py:566
  (9 shorter events, 0.0 us)
Async XLA Ops:
  0.6 22.3 %copy-start.3 = (f32[16,32,512]{2,1,0:T(8,128)S(1)}, f32[16,32,512]{2,1,0:T(8,128)}, u32[]{:S(2)}) copy-start(f32[16,32,512]{2,1,0:T(8,128)} %std_ref.1) | copy-start | bytes 3145732
  5.0 17.9 %copy-start.7 = (s32[32,512]{1,0:T(8,128)S(1)}, s32[32,512]{1,0:T(8,128)}, u32[]{:S(2)}) copy-start(s32[32,512]{1,0:T(8,128)} %mask_ref.1) | copy-start | bytes 196612
  5.1 19.5 %copy-start.1 = (f32[12,32,128]{2,1,0:T(8,128)S(1)}, f32[12,32,128]{2,1,0:T(8,128)}, u32[]{:S(2)}) copy-start(f32[12,32,128]{2,1,0:T(8,128)} %get-tuple-element.17.faces_ref) | copy-start | bytes 589828
  5.1 17.6 %all-to-all-start = ((f32[16,16,128]{2,1,0:T(8,128)}), f32[16,16,128]{2,1,0:T(8,128)S(1)}, u32[]{:S(2)}, u32[]{:S(2)}) async-start(f32[16,16,128]{2,1,0:T(8,128)} %get-tuple-element.15), calls=%async_computation | async-start | bytes 262144 | tf_op jit(solution)/shard_map/all_to_all | solution.py:516
  12.6 12.0 %collective-permute-start = (f32[728,128]{1,0:T(8,128)}, f32[728,128]{1,0:T(8,128)S(1)}, u32[]{:S(2)}, u32[]{:S(2)}) collective-permute-start(f32[728,128]{1,0:T(8,128)} %get-tuple-element.20), channel_id=1, source_target_pairs={{0,1},{1,2},{2,3},{3,4},{4,5},{5,6},{6,7},{7,8},{8,9},{9,10},{10,1... | collective-permute-start | bytes 1118216 | tf_op jit(solution)/shard_map/ppermute | solution.py:513
  13.0 11.6 %collective-permute-start.1 = (f32[728,128]{1,0:T(8,128)}, f32[728,128]{1,0:T(8,128)S(1)}, u32[]{:S(2)}, u32[]{:S(2)}) collective-permute-start(f32[728,128]{1,0:T(8,128)} %get-tuple-element.21), channel_id=1, source_target_pairs={{1,0},{2,1},{3,2},{4,3},{5,4},{6,5},{7,6},{8,7},{9,8},{10,9},{11,1... | collective-permute-start | bytes 1118216 | tf_op jit(solution)/shard_map/ppermute | solution.py:514
  17.1 0.9 %copy-start = (f32[12,32,128]{2,1,0:T(8,128)S(1)}, f32[12,32,128]{2,1,0:T(8,128)}, u32[]{:S(2)}) copy-start(f32[12,32,128]{2,1,0:T(8,128)} %get-tuple-element.17.faces_ref) | copy-start | bytes 589828
  18.0 1.2 %copy-start.2 = (f32[4,512,128]{2,1,0:T(8,128)S(1)}, f32[4,512,128]{2,1,0:T(8,128)}, u32[]{:S(2)}) copy-start(f32[4,512,128]{2,1,0:T(8,128)} %get-tuple-element.16.mixed_ref) | copy-start | bytes 3145732
  21.9 0.7 %copy-start.5 = (f32[4,192,128]{2,1,0:T(8,128)}, f32[4,192,128]{2,1,0:T(8,128)S(1)}, u32[]{:S(2)}) copy-start(f32[4,192,128]{2,1,0:T(8,128)S(1)} %get-tuple-element.18.inner_ref) | copy-start | bytes 1179652
  22.9 1.8 %copy-start.6 = (f32[4,192,128]{2,1,0:T(8,128)S(1)}, f32[4,192,128]{2,1,0:T(8,128)}, u32[]{:S(2)}) copy-start(f32[4,192,128]{2,1,0:T(8,128)} %copy-done.5) | copy-start | bytes 1179652
  24.6 12.8 %copy-start.4 = (f32[16,32,512]{2,1,0:T(8,128)S(1)}, f32[16,32,512]{2,1,0:T(8,128)}, u32[]{:S(2)}) copy-start(f32[16,32,512]{2,1,0:T(8,128)} %control_ref.1) | copy-start | bytes 3145732
  24.6 12.8 %copy-start.8 = (f32[16,16]{1,0:T(8,128)S(1)}, f32[16,16]{1,0:T(8,128)}, u32[]{:S(2)}) copy-start(f32[16,16]{1,0:T(8,128)} %v_ref.1) | copy-start | bytes 3076
  29.5 7.9 %collective-permute-start.2 = (f32[136,128]{1,0:T(8,128)S(1)}, f32[136,128]{1,0:T(8,128)S(1)}, u32[]{:S(2)}, u32[]{:S(2)}) collective-permute-start(f32[136,128]{1,0:T(8,128)S(1)} %get-tuple-element.24.own_ref), channel_id=1, source_target_pairs={{0,1},{1,2},{2,3},{3,4},{4,5},{5,6},{6,7},{7,8},{8,9},{9,10},{10,1... | collective-permute-start | bytes 208904 | tf_op jit(solution)/shard_map/ppermute | solution.py:557
  31.2 6.2 %collective-permute-start.3 = (f32[136,128]{1,0:T(8,128)S(1)}, f32[136,128]{1,0:T(8,128)S(1)}, u32[]{:S(2)}, u32[]{:S(2)}) collective-permute-start(f32[136,128]{1,0:T(8,128)S(1)} %get-tuple-element.24.own_ref), channel_id=1, source_target_pairs={{1,0},{2,1},{3,2},{4,3},{5,4},{6,5},{7,6},{8,7},{9,8},{10,9},{11,1... | collective-permute-start | bytes 208904 | tf_op jit(solution)/shard_map/ppermute | solution.py:558
  33.9 11.2 %all-to-all-start.1 = ((f32[16,1,128]{2,1,0:T(1,128)}), f32[16,1,128]{2,1,0:T(1,128)S(1)}, u32[]{:S(2)}, u32[]{:S(2)}) async-start(f32[16,1,128]{2,1,0:T(1,128)} %bitcast.8), calls=%async_computation.1 | async-start | bytes 16384 | tf_op jit(solution)/shard_map/all_to_all | solution.py:559

commit v7 on v6

--- a/solution.py
+++ b/solution.py
@@ -11,7 +11,7 @@
 F32 = jnp.float32
 BF16 = jnp.bfloat16
 WHOLE_VMEM = 60 * 1024 * 1024
-TIERS = ((0, 2), (2, 6), (6, PASSES))
+TIERS = tuple((k, k + 2) for k in range(0, PASSES, 2))
 VMEM_LIMIT = 24 * 1024 * 1024
 
 VMEM_SPEC = pl.BlockSpec(memory_space=pltpu.VMEM)

time: 46.1 us -> 45.1 us (0.978)
  Pallas kernels: 20.9 us -> 19.3 us
  waiting for transfers between devices: 0.25 us -> 0.9 us
    pallas_call x1, Pallas kernels: 7.63 us -> 6.65 us  [local(): call(second_kernel, shape(levels, cols, lat), [VMEM_SPEC] * 8, [field, fi...]
    pallas_call x1, Pallas kernels: 2.65 us -> 2 us  [local(): call(inner_kernel, (shape(parts, (cols - 2 * halo) * levels, STEN), shape...]
    ppermute x1, waiting for transfers between devices: 0.24 us -> 0.88 us  [local(): from_left = lax.ppermute(edge_right, 'lon', to_right)]
  transfers between devices with their start and end apart: 6 -> 6, of which waited for: 1 -> 1; matrix products, arithmetic and copies ran while one was open for 0% -> 0% of each run, Pallas kernels for 26% -> 23%
where the time goes in v7:
time: 45.1 us; the launch traced here: 44.8 us
  starting transfers between devices  20 us (44%)
  Pallas kernels  19.3 us (43%)
  local copies, waits for them, and re-layouts  3.71 us (8%)
  waiting for transfers between devices  0.9 us (2%)
  between operations  0.81 us (2%)
    all_to_all x1, starting transfers between devices, local(): recv = lax.all_to_all(sent, 'lon', split_axis=0, concat_axis=0, tiled=True)  7.53 us
    pallas_call x1, Pallas kernels, local(): call(second_kernel, shape(levels, cols, lat), [VMEM_SPEC] * 8, [field, fi...  6.65 us
    pallas_call x1, Pallas kernels, local(): call(edge_kernel, (shape(total + extra, STEN), shape(owners, STEN)), [SME...  4.83 us
    pallas_call x1, Pallas kernels, local(): call(head_kernel, (shape(parts, cols * levels, STEN), shape(3 * parts, co...  4.4 us
    ppermute x1, starting transfers between devices, local(): from_right = lax.ppermute(edge_left, 'lon', to_left)  4.08 us
    all_to_all x1, starting transfers between devices, local(): lax.all_to_all(departure[:, None, :], 'lon', split_axis=0, concat_axis=0,...  3.49 us
    unnamed x18, local copies, waits for them, and re-layouts  2.92 us
    ppermute x1, starting transfers between devices, local(): spread_right = lax.ppermute(spread, 'lon', to_left)  2.69 us
  transfers between devices with their start and end apart: 6, of which 1 were waited for; matrix products, arithmetic and copies ran while one was open for 0% of the time, Pallas kernels for 23%

profile of v7, /device:TPU:0, one launch (start us, length us, event | category | flops | bytes accessed | tf_op | source)
XLA Modules:
  0.0 44.8 jit_solution(8541632570648358382)
XLA Ops:
  0.6 0.0 copy-start.3
  0.6 4.4 %shard_map.122 = (f32[4,512,128]{2,1,0:T(8,128)}, f32[12,32,128]{2,1,0:T(8,128)}, f32[728,128]{1,0:T(8,128)}, f32[728,128]{1,0:T(8,128)}, f32[16,16,128]{2,1,0:T(8,128)}) custom-call(s32[32,512]{1,0:T(8,128)} %mask_ref.1, f32[32,512]{1,0:T(8,128)} %klon_hbm.1, f32[32,512]{1,0:T(8,128)} %klat_hbm.1, f32[16,16]{1,0:T(8,128)} %v_ref.1, ...), custom_call_target="tpu_custom_call" | custom-call | flops 2617245696 | bytes 13631488 | tf_op jit(solution)/shard_map/pallas_call | solution.py:496
  5.0 0.0 copy-start.7
  5.1 0.0 copy-start.1
  5.1 7.5 %all-to-all-start = ((f32[16,16,128]{2,1,0:T(8,128)}), f32[16,16,128]{2,1,0:T(8,128)S(1)}, u32[]{:S(2)}, u32[]{:S(2)}) async-start(f32[16,16,128]{2,1,0:T(8,128)} %get-tuple-element.15), calls=%async_computation | async-start | bytes 262144 | tf_op jit(solution)/shard_map/all_to_all | solution.py:516
  12.6 0.4 collective-permute-start
  13.0 4.1 %collective-permute-start.1 = (f32[728,128]{1,0:T(8,128)}, f32[728,128]{1,0:T(8,128)S(1)}, u32[]{:S(2)}, u32[]{:S(2)}) collective-permute-start(f32[728,128]{1,0:T(8,128)} %get-tuple-element.21), channel_id=1, source_target_pairs={{1,0},{2,1},{3,2},{4,3},{5,4},{6,5},{7,6},{8,7},{9,8},{10,9},{11,1... | collective-permute-start | bytes 1118216 | tf_op jit(solution)/shard_map/ppermute | solution.py:514
  17.1 0.9 %copy-done = f32[12,32,128]{2,1,0:T(8,128)S(1)} copy-done((f32[12,32,128]{2,1,0:T(8,128)S(1)}, f32[12,32,128]{2,1,0:T(8,128)}, u32[]{:S(2)}) %copy-start) | copy-done | bytes 196632
  18.0 1.2 %copy-done.2 = f32[4,512,128]{2,1,0:T(8,128)S(1)} copy-done((f32[4,512,128]{2,1,0:T(8,128)S(1)}, f32[4,512,128]{2,1,0:T(8,128)}, u32[]{:S(2)}) %copy-start.2) | copy-done | bytes 1048600
  19.3 2.0 %shard_map.123 = (f32[4,192,128]{2,1,0:T(8,128)S(1)}, f32[10,2,8,16,128]{4,3,2,1,0:T(8,128)S(1)}) custom-call(f32[4,512,128]{2,1,0:T(8,128)S(1)} %copy-done.2, f32[12,32,128]{2,1,0:T(8,128)S(1)} %copy-done), custom_call_target="tpu_custom_call" | custom-call | flops 21299200 | bytes 17039360 | tf_op jit(solution)/shard_map/pallas_call | solution.py:536
  21.3 0.0 copy-start.5
  21.3 0.7 %copy-done.5 = f32[4,192,128]{2,1,0:T(8,128)} copy-done((f32[4,192,128]{2,1,0:T(8,128)}, f32[4,192,128]{2,1,0:T(8,128)S(1)}, u32[]{:S(2)}) %copy-start.5) | copy-done | bytes 393240
  22.0 0.0 all-to-all-done.recv_ref
  22.0 0.1 fusion
  22.1 0.1 convert_element_type.18
  22.2 0.0 copy-start.6
  22.3 1.4 %shard_map.124 = (f32[128,128]{1,0:T(8,128)S(1)}, f32[4,128,128]{2,1,0:T(8,128)S(1)}) custom-call(s32[2,128]{1,0:T(2,128)S(1)} %pad_add_fusion.place_ref, f32[16,16,128]{2,1,0:T(8,128)S(1)} %all-to-all-done.recv_ref, f32[16,32,512]{2,1,0:T(8,128)S(1)} %copy-done.3, s32[32,512]{1,0:T(8,128)S(1)} %copy-done.7), custom_call_target="tpu_custom_call" | custom-call | flops 50331648 | bytes 6815744 | tf_op jit(solution)/shard_map/pallas_call | solution.py:520
  23.7 0.9 %collective-permute-done.from_left = f32[728,128]{1,0:T(8,128)S(1)} collective-permute-done((f32[728,128]{1,0:T(8,128)}, f32[728,128]{1,0:T(8,128)S(1)}, u32[]{:S(2)}, u32[]{:S(2)}) %collective-permute-start) | collective-permute-done | bytes 372768 | tf_op jit(solution)/shard_map/ppermute | solution.py:513
  24.6 0.0 collective-permute-done.1.from_right
  24.6 0.0 copy-done.6
  24.6 0.0 copy-start.4
  24.6 0.0 copy-start.8
  24.6 4.8 %shard_map.125 = (f32[136,128]{1,0:T(8,128)S(1)}, f32[16,128]{1,0:T(8,128)}) custom-call(s32[2,128]{1,0:T(2,128)S(1)} %pad_add_fusion.place_ref, f32[4,192,128]{2,1,0:T(8,128)S(1)} %copy-done.6, f32[10,2,8,16,128]{4,3,2,1,0:T(8,128)S(1)} %get-tuple-element.19.strips_ref, f32[728,128]{1,0:T(8,128)S(1)} %collective-permute-done.from_left, ...), custom_call_target="tpu_custom_call" | custom-call | flops 21299200 | bytes 17039360 | tf_op jit(solution)/shard_map/pallas_call | solution.py:546
  29.5 1.7 %collective-permute-start.2 = (f32[136,128]{1,0:T(8,128)S(1)}, f32[136,128]{1,0:T(8,128)S(1)}, u32[]{:S(2)}, u32[]{:S(2)}) collective-permute-start(f32[136,128]{1,0:T(8,128)S(1)} %get-tuple-element.24.own_ref), channel_id=1, source_target_pairs={{0,1},{1,2},{2,3},{3,4},{4,5},{5,6},{6,7},{7,8},{8,9},{9,10},{10,1... | collective-permute-start | bytes 208904 | tf_op jit(solution)/shard_map/ppermute | solution.py:557
  31.2 2.7 %collective-permute-start.3 = (f32[136,128]{1,0:T(8,128)S(1)}, f32[136,128]{1,0:T(8,128)S(1)}, u32[]{:S(2)}, u32[]{:S(2)}) collective-permute-start(f32[136,128]{1,0:T(8,128)S(1)} %get-tuple-element.24.own_ref), channel_id=1, source_target_pairs={{1,0},{2,1},{3,2},{4,3},{5,4},{6,5},{7,6},{8,7},{9,8},{10,9},{11,1... | collective-permute-start | bytes 208904 | tf_op jit(solution)/shard_map/ppermute | solution.py:558
  33.9 3.5 %all-to-all-start.1 = ((f32[16,1,128]{2,1,0:T(1,128)}), f32[16,1,128]{2,1,0:T(1,128)S(1)}, u32[]{:S(2)}, u32[]{:S(2)}) async-start(f32[16,1,128]{2,1,0:T(1,128)} %bitcast.8), calls=%async_computation.1 | async-start | bytes 16384 | tf_op jit(solution)/shard_map/all_to_all | solution.py:559
  37.4 0.0 collective-permute-done.2.left_ref
  37.4 0.0 collective-permute-done.3.right_ref
  37.4 6.6 %shard_map.126 = f32[16,32,512]{2,1,0:T(8,128)} custom-call(f32[16,16]{1,0:T(8,128)S(1)} %copy-done.8, f32[16,32,512]{2,1,0:T(8,128)S(1)} %copy-done.4, f32[136,128]{1,0:T(8,128)S(1)} %get-tuple-element.24.own_ref, f32[136,128]{1,0:T(8,128)S(1)} %collective-permute-done.2.left_ref, f32[136,128]{1,0:T(8,128)S(1)} %collective-permute-done.3.right_ref, ...), custom_call_target="tpu_custom_call" | custom-call | flops 42598400 | bytes 34078720 | tf_op jit(solution)/shard_map/pallas_call | solution.py:561
  44.1 0.0 all-to-all-done.1
  44.1 0.1 copy.16
  44.2 0.6 %slice_bitcast_fusion = f32[1,16,8]{1,2,0:T(8,128)} fusion(f32[16,1,128]{0,2,1:T(8,128)S(1)} %copy.16), kind=kLoop, calls=%fused_computation.2 | loop fusion | bytes 1024 | tf_op jit(solution)/shard_map/broadcast_in_dim;squeeze | solution.py:566
  (9 shorter events, 0.0 us)
Async XLA Ops:
  0.6 21.6 %copy-start.3 = (f32[16,32,512]{2,1,0:T(8,128)S(1)}, f32[16,32,512]{2,1,0:T(8,128)}, u32[]{:S(2)}) copy-start(f32[16,32,512]{2,1,0:T(8,128)} %std_ref.1) | copy-start | bytes 3145732
  5.0 17.2 %copy-start.7 = (s32[32,512]{1,0:T(8,128)S(1)}, s32[32,512]{1,0:T(8,128)}, u32[]{:S(2)}) copy-start(s32[32,512]{1,0:T(8,128)} %mask_ref.1) | copy-start | bytes 196612
  5.1 19.5 %copy-start.1 = (f32[12,32,128]{2,1,0:T(8,128)S(1)}, f32[12,32,128]{2,1,0:T(8,128)}, u32[]{:S(2)}) copy-start(f32[12,32,128]{2,1,0:T(8,128)} %get-tuple-element.17.faces_ref) | copy-start | bytes 589828
  5.1 16.9 %all-to-all-start = ((f32[16,16,128]{2,1,0:T(8,128)}), f32[16,16,128]{2,1,0:T(8,128)S(1)}, u32[]{:S(2)}, u32[]{:S(2)}) async-start(f32[16,16,128]{2,1,0:T(8,128)} %get-tuple-element.15), calls=%async_computation | async-start | bytes 262144 | tf_op jit(solution)/shard_map/all_to_all | solution.py:516
  12.6 12.0 %collective-permute-start = (f32[728,128]{1,0:T(8,128)}, f32[728,128]{1,0:T(8,128)S(1)}, u32[]{:S(2)}, u32[]{:S(2)}) collective-permute-start(f32[728,128]{1,0:T(8,128)} %get-tuple-element.20), channel_id=1, source_target_pairs={{0,1},{1,2},{2,3},{3,4},{4,5},{5,6},{6,7},{7,8},{8,9},{9,10},{10,1... | collective-permute-start | bytes 1118216 | tf_op jit(solution)/shard_map/ppermute | solution.py:513
  13.0 11.6 %collective-permute-start.1 = (f32[728,128]{1,0:T(8,128)}, f32[728,128]{1,0:T(8,128)S(1)}, u32[]{:S(2)}, u32[]{:S(2)}) collective-permute-start(f32[728,128]{1,0:T(8,128)} %get-tuple-element.21), channel_id=1, source_target_pairs={{1,0},{2,1},{3,2},{4,3},{5,4},{6,5},{7,6},{8,7},{9,8},{10,9},{11,1... | collective-permute-start | bytes 1118216 | tf_op jit(solution)/shard_map/ppermute | solution.py:514
  17.1 0.9 %copy-start = (f32[12,32,128]{2,1,0:T(8,128)S(1)}, f32[12,32,128]{2,1,0:T(8,128)}, u32[]{:S(2)}) copy-start(f32[12,32,128]{2,1,0:T(8,128)} %get-tuple-element.17.faces_ref) | copy-start | bytes 589828
  18.0 1.2 %copy-start.2 = (f32[4,512,128]{2,1,0:T(8,128)S(1)}, f32[4,512,128]{2,1,0:T(8,128)}, u32[]{:S(2)}) copy-start(f32[4,512,128]{2,1,0:T(8,128)} %get-tuple-element.16.mixed_ref) | copy-start | bytes 3145732
  21.3 0.7 %copy-start.5 = (f32[4,192,128]{2,1,0:T(8,128)}, f32[4,192,128]{2,1,0:T(8,128)S(1)}, u32[]{:S(2)}) copy-start(f32[4,192,128]{2,1,0:T(8,128)S(1)} %get-tuple-element.18.inner_ref) | copy-start | bytes 1179652
  22.2 2.4 %copy-start.6 = (f32[4,192,128]{2,1,0:T(8,128)S(1)}, f32[4,192,128]{2,1,0:T(8,128)}, u32[]{:S(2)}) copy-start(f32[4,192,128]{2,1,0:T(8,128)} %copy-done.5) | copy-start | bytes 1179652
  24.6 12.8 %copy-start.4 = (f32[16,32,512]{2,1,0:T(8,128)S(1)}, f32[16,32,512]{2,1,0:T(8,128)}, u32[]{:S(2)}) copy-start(f32[16,32,512]{2,1,0:T(8,128)} %control_ref.1) | copy-start | bytes 3145732
  24.6 12.8 %copy-start.8 = (f32[16,16]{1,0:T(8,128)S(1)}, f32[16,16]{1,0:T(8,128)}, u32[]{:S(2)}) copy-start(f32[16,16]{1,0:T(8,128)} %v_ref.1) | copy-start | bytes 3076
  29.5 7.9 %collective-permute-start.2 = (f32[136,128]{1,0:T(8,128)S(1)}, f32[136,128]{1,0:T(8,128)S(1)}, u32[]{:S(2)}, u32[]{:S(2)}) collective-permute-start(f32[136,128]{1,0:T(8,128)S(1)} %get-tuple-element.24.own_ref), channel_id=1, source_target_pairs={{0,1},{1,2},{2,3},{3,4},{4,5},{5,6},{6,7},{7,8},{8,9},{9,10},{10,1... | collective-permute-start | bytes 208904 | tf_op jit(solution)/shard_map/ppermute | solution.py:557
  31.2 6.2 %collective-permute-start.3 = (f32[136,128]{1,0:T(8,128)S(1)}, f32[136,128]{1,0:T(8,128)S(1)}, u32[]{:S(2)}, u32[]{:S(2)}) collective-permute-start(f32[136,128]{1,0:T(8,128)S(1)} %get-tuple-element.24.own_ref), channel_id=1, source_target_pairs={{1,0},{2,1},{3,2},{4,3},{5,4},{6,5},{7,6},{8,7},{9,8},{10,9},{11,1... | collective-permute-start | bytes 208904 | tf_op jit(solution)/shard_map/ppermute | solution.py:558
  33.9 10.2 %all-to-all-start.1 = ((f32[16,1,128]{2,1,0:T(1,128)}), f32[16,1,128]{2,1,0:T(1,128)S(1)}, u32[]{:S(2)}, u32[]{:S(2)}) async-start(f32[16,1,128]{2,1,0:T(1,128)} %bitcast.8), calls=%async_computation.1 | async-start | bytes 16384 | tf_op jit(solution)/shard_map/all_to_all | solution.py:559
